TPU v7x, 32 devices: a whole 2x2x4 slice. The times are simulated.
32 devices in a mesh: groups: 2 (over y), lev: 4 (over z), tm: 2 (over x), sub: 2 (over core).
Axes of the slice: x: 2, y: 2, z: 4, core: 2. Of those that a mesh axis runs over, the one named last changes fastest.
Arguments:
- level_field: float32 [32, 96, 16384], P(('groups', 'tm'), ('lev', 'sub')), parts along dimension 0, may hold values from -6 to 6
- tile_weight: float32 [64, 65536], P(None, ('lev', 'sub')), may hold values from -0.4 to 0.4
- tile_rows: int32 [1024], P(('lev', 'sub')), may hold values from 0 to 15
- tile_columns: int32 [1024], P(('lev', 'sub')), may hold values from 0 to 31
- live_count: int32 [8], P(('lev', 'sub')), may hold values from 16 to 128, as said below
- step_hour: int32 [16], P('tm'), may hold values from 0 to 1, as said below
Outputs:
- hourly: float32 [4, 96, 8192], P('groups', 'tm', ('lev', 'sub')), parts along dimension 0
There are 2 independent parts, one for each index of `groups`. A program takes and returns all parts, laid end to end along the dimension named above; an argument that names none is the same for every part. Nothing has to cross between parts.
Inputs may be any that keep to these rules, and one draw needn't show every extreme that they name: `live_count`: some shard has all 128 slots live in every draw, not always the same. `step_hour`: every hour has exactly 8 steps.
All inputs are finite; a program needn't handle non-finite values.
Results may differ from a plain program's by a relative error of at most 0.0003.
Values sent between devices are 32-bit elements; how exact they have to be, the bound alone decides.
No kernel may reach another device: no remote copies, remote signals or barrier semaphores. Data moves between devices by JAX's collectives and lax.ppermute only.
A program may use at most 128 MiB of HBM per device.

v0:
```python
import jax
import jax.numpy as jnp
from jax import lax
from jax.sharding import PartitionSpec as P

TILE = 64
HOURS = 2
CT_DEV = 32
PT_DEV = 16
SLOTS = 128


def assemble(weights, rows, columns, count):
    live_mask = (jnp.arange(SLOTS, dtype=jnp.int32) < count).astype(jnp.float32)
    column_hot = (columns[:, None] == jnp.arange(CT_DEV, dtype=jnp.int32)[None, :]).astype(
        jnp.float32
    ) * live_mask[:, None]
    row_hot = (rows[:, None] == jnp.arange(PT_DEV, dtype=jnp.int32)[None, :]).astype(jnp.float32)
    pair_hot = (column_hot[:, :, None] * row_hot[:, None, :]).reshape(SLOTS, CT_DEV * PT_DEV)
    slot_tiles = jnp.transpose(weights, (1, 2, 0)).reshape(SLOTS, TILE * TILE)
    placed = lax.dot_general(
        pair_hot,
        slot_tiles,
        (((0,), (0,)), ((), ())),
        precision=lax.Precision.HIGHEST,
        preferred_element_type=jnp.float32,
    )
    placed = placed.reshape(CT_DEV, PT_DEV, TILE, TILE)
    return jnp.transpose(placed, (0, 2, 1, 3)).reshape(CT_DEV * TILE, PT_DEV * TILE)


def regroup_blocks(blocks):
    return lax.all_to_all(blocks, ("lev", "sub"), split_axis=0, concat_axis=0, tiled=True)


def apply_map(regrouped, dense_map):
    lead_shape = regrouped.shape[:-1]
    flat = regrouped.reshape(-1, regrouped.shape[-1])
    pixel_values = jnp.dot(
        flat, dense_map, preferred_element_type=jnp.float32, precision=lax.Precision.HIGHEST
    )
    return pixel_values.reshape(lead_shape + (dense_map.shape[1],))


def body(level_field, tile_weight, tile_rows, tile_columns, live_count, step_hour):
    dense_map = assemble(
        tile_weight.reshape(TILE, SLOTS, TILE), tile_rows, tile_columns, live_count[0]
    )
    steps_here = level_field.shape[0]
    levels_here = level_field.shape[1]
    shard_count = lax.axis_size("lev") * lax.axis_size("sub")
    cells_dev = level_field.shape[2] // shard_count
    divisor = float(steps_here * lax.axis_size("tm") // HOURS)
    hour_table = (step_hour[None, :] == jnp.arange(HOURS, dtype=jnp.int32)[:, None]).astype(
        jnp.float32
    )
    split_field = level_field.reshape(steps_here, levels_here, shard_count, cells_dev)
    partial_value = jnp.einsum(
        "hs,slgc->ghlc", hour_table, split_field, precision=lax.Precision.HIGHEST
    )
    regrouped = regroup_blocks(partial_value)
    remapped = apply_map(regrouped, dense_map)
    hourly_part = jnp.transpose(remapped, (1, 0, 2, 3))
    hourly_part = (
        hourly_part.reshape(HOURS, shard_count * levels_here, dense_map.shape[1]) / divisor
    )
    return lax.psum_scatter(hourly_part, "tm", scatter_dimension=1, tiled=True)


def solution(mesh):
    placed = (
        P(("groups", "tm"), ("lev", "sub"), None),
        P(None, ("lev", "sub")),
        P(("lev", "sub")),
        P(("lev", "sub")),
        P(("lev", "sub")),
        P("tm"),
    )
    return jax.shard_map(
        body,
        mesh=mesh,
        in_specs=placed,
        out_specs=P("groups", "tm", ("lev", "sub")),
        check_vma=False,
    )
```

profile of v0, /device:TPU:0, one launch (start us, length us, event | category | flops | bytes accessed | tf_op | source)
XLA Modules:
  0.0 114.3 jit_solution(13328466790611541692)
XLA Ops:
  6.5 5.9 %convolution_bitcast_fusion.1 = f32[8,2,12,2048]{3,1,0,2:T(2,128)S(1)} fusion(f32[8,12,8,2048]{3,0,2,1:T(8,128)} %bitcast.48, s32[8]{0:T(128)} %param.11), kind=kOutput, calls=%fused_computation.3 | convolution fusion | flops 37748752 | bytes 7864352 | tf_op jit(solution)/shard_map/hs,slgc->ghlc/dot_general | solution.py:58
  12.4 1.3 %copy.10 = f32[8,2,12,2048]{3,1,2,0:T(2,128)} copy(f32[8,2,12,2048]{3,1,0,2:T(2,128)S(1)} %convolution_bitcast_fusion.1) | data formatting | bytes 3145728 | tf_op jit(solution)/shard_map/hs,slgc->ghlc/transpose | solution.py:58
  13.7 0.0 copy-start
  13.7 6.5 %all-to-all-start = ((f32[8,2,12,2048]{3,1,2,0:T(2,128)}), f32[8,2,12,2048]{3,1,2,0:T(2,128)}, u32[]{:S(2)}, u32[]{:S(2)}) async-start(f32[8,2,12,2048]{3,1,2,0:T(2,128)} %copy.10), calls=%async_computation | async-start | bytes 3145728 | tf_op jit(solution)/shard_map/all_to_all | solution.py:33
  20.1 0.2 all-reduce.3.cloned.1.call-start
  20.4 0.0 copy-done
  20.4 3.0 %reshape.87 = f32[64,128,64]{2,1,0:T(8,128)} reshape(f32[64,8192]{1,0:T(8,128)S(1)} %copy-done) | data formatting | bytes 4194304 | tf_op jit(solution)/shard_map/reshape | solution.py:47
  23.4 0.0 copy-start.1
  23.4 0.0 copy-start.2
  23.4 3.6 %copy.11 = f32[128,64,64]{0,2,1:T(8,128)S(1)} copy(f32[128,64,64]{1,0,2:T(8,128)} %bitcast.47) | data formatting | bytes 4194304 | tf_op jit(solution)/shard_map/transpose | solution.py:20
  27.6 0.0 copy-done.1
  27.6 0.0 copy-done.2
  27.7 15.8 %convolution_bitcast_fusion = f32[32,64,16,64]{3,2,1,0:T(8,128)} fusion(f32[128,64,64]{0,2,1:T(8,128)S(1)} %copy.11, f32[128,16]{0,1:T(8,128)S(1)} %fusion.19, f32[128,32]{0,1:T(8,128)S(1)} %fusion.18), kind=kOutput, calls=%fused_computation | convolution fusion | flops 3221291008 | bytes 10510336 | tf_op jit(solution)/shard_map/dot_general | solution.py:21
  43.4 14.5 %reshape.93 = f32[2048,1024,1,1]{1,0,2,3:T(8,128)} reshape(f32[32,64,16,64]{3,2,1,0:T(8,128)} %convolution_bitcast_fusion) | data formatting | bytes 16777216 | tf_op jit(solution)/shard_map/reshape | solution.py:29
  58.0 0.1 all-to-all-done
  58.1 10.3 %fusion.9 = f32[2,8,12,1024]{3,2,0,1:T(8,128)S(1)} fusion(f32[2048,1024,1,1]{1,0,2,3:T(8,128)} %reshape.93, f32[8,2,12,2048]{3,1,2,0:T(2,128)} %all-to-all-done), kind=kOutput, calls=%fused_computation.7 | convolution fusion | flops 4832034816 | bytes 10747904 | tf_op jit(solution)/shard_map/dot_general | solution.py:39
  68.4 0.0 copy-start.3
  68.4 1.5 %copy.13 = f32[2,8,12,1024]{3,0,2,1:T(2,128)} copy(f32[2,8,12,1024]{3,2,0,1:T(8,128)S(1)} %fusion.9) | data formatting | bytes 1572864 | tf_op jit(solution)/shard_map/div | solution.py:65
  69.9 0.0 all-reduce.3.cloned.1.call-update
  69.9 0.0 copy-done.3
  69.9 0.6 dynamic-slice
  71.2 34.3 %all-reduce.3.cloned.1.call-done = f32[2,96,1024]{2,0,1:T(2,128)} async-done(((f32[2,96,1024]{2,0,1:T(2,128)}), f32[2,96,1024]{2,0,1:T(2,128)}) %all-reduce.3.cloned.1.call-update) | async-done | bytes 786448
  105.5 1.0 constant_dynamic-slice_fusion
  106.5 0.9 copy.14
  (3 shorter events, 0.0 us)
Async XLA Ops:
  13.7 6.7 %copy-start = (f32[64,8192]{1,0:T(8,128)S(1)}, f32[64,8192]{1,0:T(8,128)}, u32[]{:S(2)}) copy-start(f32[64,8192]{1,0:T(8,128)} %param.7) | copy-start | bytes 6291460
  13.7 44.4 %all-to-all-start = ((f32[8,2,12,2048]{3,1,2,0:T(2,128)}), f32[8,2,12,2048]{3,1,2,0:T(2,128)}, u32[]{:S(2)}, u32[]{:S(2)}) async-start(f32[8,2,12,2048]{3,1,2,0:T(2,128)} %copy.10), calls=%async_computation | async-start | bytes 3145728 | tf_op jit(solution)/shard_map/all_to_all | solution.py:33
  20.1 85.4 %all-reduce.3.cloned.1.call-start = ((), (), s32[]{:S(2)}) async-start(), calls=%async_computation.1 | async-start | bytes 1572864
  23.4 4.2 %copy-start.1 = (s32[128]{0:T(128)S(1)}, s32[128]{0:T(128)}, u32[]{:S(2)}) copy-start(s32[128]{0:T(128)} %param.8) | copy-start | bytes 1540
  23.4 4.2 %copy-start.2 = (s32[128]{0:T(128)S(1)}, s32[128]{0:T(128)}, u32[]{:S(2)}) copy-start(s32[128]{0:T(128)} %param.9) | copy-start | bytes 1540
  68.4 1.5 %copy-start.3 = (u32[32]{0:T(128)S(1)}, u32[32]{0:T(128)}, u32[]{:S(2)}) copy-start(u32[32]{0:T(128)} %constant.9) | copy-start | bytes 388
Sparse Core Ops, SparseCore 0:
  70.0 35.4 all-reduce.2
where the time goes:
time: 115 us; the launch traced here: 114 us
  waiting for transfers between devices  34.5 us (30%)
  matrix products  31.9 us (28%)
  local copies, waits for them, and re-layouts  26.4 us (23%)
  between operations  14.8 us (13%)
  starting transfers between devices  6.67 us (6%)
    unnamed x2, waiting for transfers between devices  34.4 us
    dot_general x1, matrix products, assemble(): lax.dot_general(pair_hot, slot_tiles, (((0,), (0,)), ((), ())), precision...  15.8 us
    reshape x1, local copies, waits for them, and re-layouts, assemble(): jnp.transpose(placed, (0, 2, 1, 3)).reshape(CT_DEV * TILE, PT_DEV * TILE)  14.5 us
    dot_general x1, matrix products, apply_map(): jnp.dot(flat, dense_map, preferred_element_type=jnp.float32, precision=la...  10.3 us
    all_to_all x1, starting transfers between devices, regroup_blocks(): lax.all_to_all(blocks, ('lev', 'sub'), split_axis=0, concat_axis=0, tiled...  6.46 us
    dot_general x1, matrix products, body(): jnp.einsum('hs,slgc->ghlc', hour_table, split_field, precision=lax.Precis...  5.85 us
    transpose x1, local copies, waits for them, and re-layouts, assemble(): slot_tiles = jnp.transpose(weights, (1, 2, 0)).reshape(SLOTS, TILE * TILE)  3.55 us
    reshape x1, local copies, waits for them, and re-layouts, body(): tile_weight.reshape(TILE, SLOTS, TILE)  3.02 us
  transfers between devices with their start and end apart: 2, of which 2 were waited for; matrix products, arithmetic and copies ran while one was open for 33% of the time, Pallas kernels for 0%

commit v1 on v0

v1 whole, which is shorter than its diff:
```python
import functools

import jax
import jax.numpy as jnp
from jax import lax
from jax.experimental import pallas as pl
from jax.experimental.pallas import tpu as pltpu
from jax.sharding import PartitionSpec as P

TILE = 64
HOURS = 2
CT_DEV = 32
PT_DEV = 16
SLOTS = 128
CELLS_DEV = CT_DEV * TILE
PIXELS_DEV = PT_DEV * TILE
LANES = 2 * TILE
MIB = 1 << 20

LIGHT = pl.CostEstimate(flops=1, bytes_accessed=1, transcendentals=0)

NT = (((1,), (1,)), ((), ()))
NN = (((1,), (0,)), ((), ()))


def split(x):
    high = x.astype(jnp.bfloat16)
    return high, (x - high.astype(jnp.float32)).astype(jnp.bfloat16)


def dot(a, b, dims):
    return lax.dot_general(a, b, dims, preferred_element_type=jnp.float32)


def place_kernel(rows, columns, count, weights, *refs):
    high, low, total = refs[-3:]
    band = 128

    @pl.loop(0, PIXELS_DEV // band)
    def _(b):
        total[pl.ds(pl.multiple_of(b * band, band), band), :] = jnp.zeros((band, CELLS_DEV), jnp.float32)

    lane_half = lax.broadcasted_iota(jnp.int32, (TILE, LANES), 1) // TILE

    @pl.loop(0, count[0])
    def _(k):
        column = columns[k]
        side = column % 2
        tile = weights[:, pl.ds(pl.multiple_of((k // 2) * LANES, LANES), LANES)]
        moved = pltpu.roll(tile, ((k + column) % 2) * TILE, 1)
        at = (
            pl.ds(pl.multiple_of(rows[k] * TILE, TILE), TILE),
            pl.ds(pl.multiple_of((column // 2) * LANES, LANES), LANES),
        )
        total[at] = total[at] + jnp.where(lane_half == side, moved, 0.0)

    @pl.loop(0, PIXELS_DEV // band)
    def _(b):
        at = pl.ds(pl.multiple_of(b * band, band), band)
        high[at, :], low[at, :] = split(total[at, :])


def place_tiles(rows, columns, count, weights, *after):
    smem = pl.BlockSpec(memory_space=pltpu.SMEM)
    vmem = pl.BlockSpec(memory_space=pltpu.VMEM)
    half = jax.ShapeDtypeStruct((PIXELS_DEV, CELLS_DEV), jnp.bfloat16)
    return pl.pallas_call(
        place_kernel,
        out_shape=(half, half),
        in_specs=[smem, smem, smem, vmem] + [pl.BlockSpec(memory_space=pl.ANY)] * len(after),
        out_specs=(vmem, vmem),
        scratch_shapes=[pltpu.VMEM((PIXELS_DEV, CELLS_DEV), jnp.float32)],
        compiler_params=pltpu.CompilerParams(vmem_limit_bytes=28 * MIB),
        cost_estimate=LIGHT,
        name="place_tiles",
    )(rows, columns, count, weights, *after)


PIXEL_BLOCK = 256


def remap_body(x, high, low):
    m = x.shape[0]
    x_high, x_low = split(x)
    both = dot(jnp.concatenate([x_high, x_low], axis=0), high, NT)
    return both[:m] + both[m:] + dot(x_high, low, NT)


def remap_call(kernel, inputs, out_rows, high, low, name):
    whole = [pl.BlockSpec(a.shape, lambda i, nd=a.ndim: (0,) * nd) for a in inputs]
    map_block = pl.BlockSpec((PIXEL_BLOCK, CELLS_DEV), lambda i: (i, 0))
    return pl.pallas_call(
        kernel,
        out_shape=[jax.ShapeDtypeStruct((rows, PIXELS_DEV), jnp.float32) for rows in out_rows],
        grid=(PIXELS_DEV // PIXEL_BLOCK,),
        in_specs=whole + [map_block, map_block],
        out_specs=[pl.BlockSpec((rows, PIXEL_BLOCK), lambda i: (0, i)) for rows in out_rows],
        compiler_params=pltpu.CompilerParams(vmem_limit_bytes=24 * MIB),
        cost_estimate=LIGHT,
        name=name,
    )(*inputs, high, low)


def remap_rows_kernel(x, high, low, out):
    out[...] = remap_body(x[...], high[...], low[...])


def near_rows(own, other_sub, other_lev, other_both):
    even = lax.axis_index("sub") == 0
    lev_first = lax.axis_index("lev") % 2 == 0
    left, right = jnp.where(even, own, other_sub), jnp.where(even, other_sub, own)
    up, down = jnp.where(even, other_lev, other_both), jnp.where(even, other_both, other_lev)
    return [
        jnp.where(lev_first, left, up),
        jnp.where(lev_first, right, down),
        jnp.where(lev_first, up, left),
        jnp.where(lev_first, down, right),
    ]


def far_rows(same_sub, other_sub):
    even = lax.axis_index("sub") == 0
    levels = same_sub.shape[0] // 2
    blocks = [jnp.where(even, same_sub, other_sub), jnp.where(even, other_sub, same_sub)]
    return [jnp.concatenate([block[:levels], block[levels:]], axis=1) for block in blocks]


def remap_first_kernel(own, other_sub, other_lev, other_both, same, other, high, low, *outs):
    levels = own.shape[0] // HOURS
    blocks = near_rows(own[...], other_sub[...], other_lev[...], other_both[...])
    x = jnp.concatenate(blocks + far_rows(same[...], other[...]), axis=0)
    result = remap_body(x, high[...], low[...])
    for hour in range(HOURS):
        for lev in range(2):
            pieces = []
            for sub in range(2):
                start = ((lev * 2 + sub) * HOURS + hour) * levels
                pieces.append(result[start : start + levels])
            outs[hour * 2 + lev][...] = jnp.concatenate(pieces, axis=0)
    outs[-1][...] = result[4 * HOURS * levels :]


def remap_last_kernel(same, other, high, low, out):
    x = jnp.concatenate(far_rows(same[...], other[...]), axis=0)
    out[...] = remap_body(x, high[...], low[...])


def hour_matrix(step_hour, levels, steps, hours, cuts):
    rows, columns = cuts * levels, cuts * 2 * levels * steps
    row = lax.broadcasted_iota(jnp.int32, (rows, columns), 0)
    column = lax.broadcasted_iota(jnp.int32, (rows, columns), 1)
    span = levels * steps
    near = jnp.full((rows, columns), -1, jnp.int32)
    for cut in range(cuts):
        for half in range(2):
            step = column - (cut * 2 + half) * span - (row - cut * levels) * steps
            inside = (row >= cut * levels) & (row < (cut + 1) * levels)
            inside = inside & (step >= 0) & (step < steps)
            near = jnp.where(inside, step, near)
    blocks = []
    for hour in hours:
        block = jnp.zeros((rows, columns), jnp.float32)
        for step in range(steps):
            block = jnp.where(near == step, jnp.where(step_hour[step] == hour, 1.0, 0.0), block)
        blocks.append(block)
    return jnp.concatenate(blocks, axis=0).astype(jnp.bfloat16)


def peer_shard(k, j):
    subs = lax.axis_size("sub")
    return (lax.axis_index("lev") ^ k) * subs + (lax.axis_index("sub") ^ j)


def field_copies(field, buffer, arrived, peers):
    copies = []
    for place, (k, j) in enumerate(peers):
        start = pl.multiple_of(peer_shard(k, j) * CELLS_DEV, CELLS_DEV)
        copy = pltpu.make_async_copy(
            field.at[:, :, pl.ds(start, CELLS_DEV)], buffer.at[place], arrived.at[place]
        )
        copy.start()
        copies.append(copy)
    return copies


def near_sum_kernel(peers, step_hour, field, *refs):
    *outs, buffer, arrived = refs[-len(peers) - 2 :]
    _, levels, steps, cells = buffer.shape
    copies = field_copies(field, buffer, arrived, peers)
    matrix = hour_matrix(step_hour, levels, steps, range(HOURS), 1)
    for place, out in enumerate(outs):
        copies[place].wait()
        x = buffer[place].reshape(levels * steps, cells)
        out[...] = dot(matrix, jnp.concatenate(split(x), axis=0), NN)


def far_sum_kernel(peers, step_hour, field, *refs):
    theirs, mine, buffer, arrived = refs[-4:]
    _, levels, steps, cells = buffer.shape
    copies = field_copies(field, buffer, arrived, peers)
    me = lax.axis_index("tm")
    matrix = hour_matrix(step_hour, levels, steps, (1 - me, me), 2)
    rows, cut = 2 * levels, cells // 2
    for place, copy in enumerate(copies):
        copy.wait()
        high, low = split(buffer[place].reshape(levels * steps, cells))
        stacked = jnp.concatenate([high[:, :cut], low[:, :cut], high[:, cut:], low[:, cut:]], axis=0)
        result = dot(matrix, stacked, NN)
        theirs[place * rows : (place + 1) * rows] = result[:rows]
        mine[place * rows : (place + 1) * rows] = result[rows:]


def sum_call(kernel, peers, step_hour, field, after, out_shapes, name):
    levels, steps, _ = field.shape
    vmem = pl.BlockSpec(memory_space=pltpu.VMEM)
    return pl.pallas_call(
        functools.partial(kernel, peers),
        out_shape=out_shapes,
        in_specs=[pl.BlockSpec(memory_space=pltpu.SMEM)] + [pl.BlockSpec(memory_space=pl.ANY)] * (1 + len(after)),
        out_specs=[vmem] * len(out_shapes),
        scratch_shapes=[
            pltpu.VMEM((len(peers), levels, steps, CELLS_DEV), jnp.float32),
            pltpu.SemaphoreType.DMA((len(peers),)),
        ],
        compiler_params=pltpu.CompilerParams(vmem_limit_bytes=52 * MIB),
        cost_estimate=LIGHT,
        name=name,
    )(step_hour, field, *after)


def near_sums(peers, step_hour, field, *after):
    shape = jax.ShapeDtypeStruct((HOURS * field.shape[0], CELLS_DEV), jnp.float32)
    return sum_call(near_sum_kernel, peers, step_hour, field, after, [shape] * len(peers), "near_sums")


def far_sums(peers, step_hour, field, *after):
    shape = jax.ShapeDtypeStruct((len(peers) * 2 * field.shape[0], CELLS_DEV // 2), jnp.float32)
    return sum_call(far_sum_kernel, peers, step_hour, field, after, [shape] * 2, "far_sums")


def merge_kernel(mine, got, *outs):
    rows = outs[0].shape[0]
    for place, out in enumerate(outs):
        at = slice(place * rows, (place + 1) * rows)
        out[...] = mine[at] + got[at]


def merge(mine, got, parts):
    vmem = pl.BlockSpec(memory_space=pltpu.VMEM)
    shape = jax.ShapeDtypeStruct((mine.shape[0] // parts, mine.shape[1]), jnp.float32)
    return pl.pallas_call(
        merge_kernel,
        out_shape=[shape] * parts,
        in_specs=[vmem, vmem],
        out_specs=[vmem] * parts,
        compiler_params=pltpu.CompilerParams(vmem_limit_bytes=4 * MIB),
        cost_estimate=LIGHT,
        name="merge",
    )(mine, got)


def finish_kernel(divisor, *refs):
    *arrays, out = refs
    a_own, a_got, b_own, b_got = arrays[-4:]
    me, lev = lax.axis_index("tm"), lax.axis_index("lev")
    half = a_own.shape[0]
    keeps_near = me == lev // 2

    @pl.when(keeps_near)
    def _():
        for place in range(2 * HOURS):
            total = arrays[place][...] + arrays[2 * HOURS + place][...]
            out[place * half : (place + 1) * half, :] = total / divisor

    @pl.when(jnp.logical_not(keeps_near))
    def _():
        for hour in range(HOURS):
            a_at = pl.multiple_of((hour * 2 + lev % 2) * half, half)
            b_at = pl.multiple_of((hour * 2 + 1 - lev % 2) * half, half)
            out[pl.ds(a_at, half), :] = jnp.where(me == hour, a_own[...], a_got[...]) / divisor
            out[pl.ds(b_at, half), :] = jnp.where(me == hour, b_own[...], b_got[...]) / divisor


def finish(arrays, divisor):
    vmem = pl.BlockSpec(memory_space=pltpu.VMEM)
    rows, pixels = arrays[0].shape
    return pl.pallas_call(
        functools.partial(finish_kernel, divisor),
        out_shape=jax.ShapeDtypeStruct((2 * HOURS * rows, pixels), jnp.float32),
        in_specs=[vmem] * len(arrays),
        out_specs=vmem,
        compiler_params=pltpu.CompilerParams(vmem_limit_bytes=8 * MIB),
        name="finish",
    )(*arrays)


def hour_plan(level_field, tile_weight, tile_rows, tile_columns, live_count, step_hour):
    levs, subs, shards_tm = lax.axis_size("lev"), lax.axis_size("sub"), lax.axis_size("tm")
    half = levs // 2
    divisor = float(level_field.shape[0] * shards_tm // HOURS)
    field = jnp.transpose(level_field, (1, 0, 2))

    def to_peer(x, k, j):
        pairs = [(a * subs + b, (a ^ k) * subs + (b ^ j)) for a in range(levs) for b in range(subs)]
        return lax.ppermute(x, ("lev", "sub"), pairs)

    def swap(x):
        return lax.ppermute(x, "tm", [(0, 1), (1, 0)])

    def move(x, keeper):
        pairs = [(a * shards_tm + 1 - keeper(a), a * shards_tm + keeper(a)) for a in range(levs)]
        return lax.ppermute(x, ("lev", "tm"), pairs)

    far_peers = [[(k, j) for j in range(subs)] for k in range(half, levs)]
    near_peers = [(k, j) for k in range(half) for j in range(subs)]
    sums = []
    for peers in far_peers:
        sums.append(far_sums(peers, step_hour, field, *[theirs for theirs, _ in sums]))
    swapped = [swap(theirs) for theirs, _ in sums]
    near = near_sums(near_peers, step_hour, field, sums[-1][0])
    near = [near[0]] + [to_peer(x, k, j) for x, (k, j) in list(zip(near, near_peers))[1:]]
    far, merges = [], []
    for peers, (_, mine), got in zip(far_peers, sums, swapped):
        merged = merge(mine, got, subs)
        merges += merged
        far.append([to_peer(x, k, j) for x, (k, j) in zip(merged, peers)])

    high, low = place_tiles(tile_rows, tile_columns, live_count, tile_weight, *merges)
    rows = far[0][0].shape[0]
    *near_out, a_out = remap_call(
        remap_first_kernel, near + far[0], [rows] * (2 * HOURS + 1), high, low, "remap_first"
    )
    near_got = [move(x, lambda a: a // half) for x in near_out]
    a_got = move(a_out, lambda a: 1 - a // half)
    (b_out,) = remap_call(remap_last_kernel, far[1], [rows], high, low, "remap_last")
    b_got = move(b_out, lambda a: 1 - a // half)
    out = finish(near_out + near_got + [a_out, a_got, b_out, b_got], divisor)
    return out.reshape(HOURS, out.shape[0] // HOURS, PIXELS_DEV)


def general_plan(level_field, tile_weight, tile_rows, tile_columns, live_count, step_hour):
    steps, levels, cells = level_field.shape
    shards = lax.axis_size("lev") * lax.axis_size("sub")
    divisor = float(steps * lax.axis_size("tm") // HOURS)
    hours = jnp.arange(HOURS, dtype=jnp.int32)
    table = (step_hour[None, :] == hours[:, None]).astype(jnp.float32)
    fields = level_field.reshape(steps, levels, shards, cells // shards)
    partial = jnp.einsum("hs,slgc->ghlc", table, fields, precision=lax.Precision.HIGHEST)
    regrouped = lax.all_to_all(partial, ("lev", "sub"), split_axis=0, concat_axis=0, tiled=True)
    rows = jnp.transpose(regrouped, (1, 0, 2, 3)).reshape(-1, cells // shards)
    high, low = place_tiles(tile_rows, tile_columns, live_count, tile_weight)
    (out,) = remap_call(remap_rows_kernel, [rows], [rows.shape[0]], high, low, "remap_rows")
    out = out.reshape(HOURS, shards * levels, PIXELS_DEV) / divisor
    return lax.psum_scatter(out, "tm", scatter_dimension=1, tiled=True)


def solution(mesh):
    sizes = mesh.shape
    paired = sizes["tm"] == HOURS and sizes["lev"] == 4 and sizes["sub"] == 2
    placed = (
        P(("groups", "tm"), ("lev", "sub"), None),
        P(None, ("lev", "sub")),
        P(("lev", "sub")),
        P(("lev", "sub")),
        P(("lev", "sub")),
        P("tm"),
    )
    return jax.shard_map(
        hour_plan if paired else general_plan,
        mesh=mesh,
        in_specs=placed,
        out_specs=P("groups", "tm", ("lev", "sub")),
        check_vma=False,
    )
```

time: 115 us -> 53 us (0.46)
  waiting for transfers between devices: 34.5 us -> 2.19 us
  matrix products: 31.9 us -> 0 us
  local copies, waits for them, and re-layouts: 26.4 us -> 0.68 us
  Pallas kernels: 0 us -> 24 us
  starting transfers between devices: 6.67 us -> 25.5 us
  between operations: 14.8 us -> 0.92 us
    unnamed x2 -> x0, waiting for transfers between devices: 34.4 us -> none
    dot_general x3 -> x0, matrix products: 31.9 us -> none  [the longest x1 15.8 us: assemble(): lax.dot_general(pair_hot, slot_tiles, (((0,), (0,)), ((), ())), precision...]
    ppermute x0 -> x15, starting transfers between devices: none -> 25.5 us  [the longest x7 11.4 us: to_peer(): return lax.ppermute(x, ('lev', 'sub'), pairs)]
    pallas_call x0 -> x9, Pallas kernels: none -> 24 us  [the longest x1 9.57 us: place_tiles(): pl.pallas_call(place_kernel, out_shape=(half, half), in_specs=[smem, smem...]
    reshape x2 -> x0, local copies, waits for them, and re-layouts: 17.5 us -> none  [the longest x1 14.5 us: assemble(): jnp.transpose(placed, (0, 2, 1, 3)).reshape(CT_DEV * TILE, PT_DEV * TILE)]
    all_to_all x1 -> x0, starting transfers between devices: 6.46 us -> none  [regroup_blocks(): lax.all_to_all(blocks, ('lev', 'sub'), split_axis=0, concat_axis=0, tiled...]
    transpose x2 -> x0, local copies, waits for them, and re-layouts: 4.85 us -> none  [the longest x1 3.55 us: assemble(): slot_tiles = jnp.transpose(weights, (1, 2, 0)).reshape(SLOTS, TILE * TILE)]
    ppermute x0 -> x15, waiting for transfers between devices: none -> 2.19 us  [the longest x6 2.16 us: move(): return lax.ppermute(x, ('lev', 'tm'), pairs)]
  transfers between devices with their start and end apart: 2 -> 15, of which waited for: 2 -> 1; matrix products, arithmetic and copies ran while one was open for 33% -> 0% of each run, Pallas kernels for 0% -> 39%
where the time goes in v1:
time: 53 us; the launch traced here: 53.3 us
  starting transfers between devices  25.5 us (48%)
  Pallas kernels  24 us (45%)
  waiting for transfers between devices  2.19 us (4%)
  between operations  0.92 us (2%)
  local copies, waits for them, and re-layouts  0.68 us (1%)
    ppermute x7, starting transfers between devices, to_peer(): return lax.ppermute(x, ('lev', 'sub'), pairs)  11.4 us
    ppermute x6, starting transfers between devices, move(): return lax.ppermute(x, ('lev', 'tm'), pairs)  11 us
    pallas_call x1, Pallas kernels, place_tiles(): pl.pallas_call(place_kernel, out_shape=(half, half), in_specs=[smem, smem...  9.57 us
    pallas_call x3, Pallas kernels, sum_call(): pl.pallas_call(functools.partial(kernel, peers), out_shape=out_shapes, in...  7.19 us
    pallas_call x2, Pallas kernels, remap_call(): pl.pallas_call(kernel, out_shape=[jax.ShapeDtypeStruct((rows, PIXELS_DEV)...  6.37 us
    ppermute x2, starting transfers between devices, swap(): return lax.ppermute(x, 'tm', [(0, 1), (1, 0)])  3.08 us
    ppermute x6, waiting for transfers between devices, move(): return lax.ppermute(x, ('lev', 'tm'), pairs)  2.16 us
  transfers between devices with their start and end apart: 15, of which 1 were waited for; matrix products, arithmetic and copies ran while one was open for 0% of the time, Pallas kernels for 39%

profile of v1, /device:TPU:0, one launch (start us, length us, event | category | flops | bytes accessed | tf_op | source)
XLA Modules:
  0.0 53.3 jit_solution(9985901874166685345)
XLA Ops:
  0.0 0.7 %copy-done.1 = s32[8]{0:T(128)S(1)} copy-done((s32[8]{0:T(128)S(1)}, s32[8]{0:T(128)}, u32[]{:S(2)}) %copy-start.1) | copy-done | bytes 56
  0.7 2.2 %far_sums.2 = (f32[48,1024]{1,0:T(8,128)S(1)}, f32[48,1024]{1,0:T(8,128)S(1)}) custom-call(s32[8]{0:T(128)S(1)} %copy-done.1, f32[12,8,16384]{2,1,0:T(8,128)} %bitcast.2), custom_call_target="tpu_custom_call" | custom-call | flops 1 | bytes 1 | tf_op jit(solution)/shard_map/far_sums/pallas_call | solution.py:216
  2.9 0.0 copy-start.2
  2.9 3.0 %collective-permute-start.3 = (f32[48,1024]{1,0:T(8,128)S(1)}, f32[48,1024]{1,0:T(8,128)S(1)}, u32[]{:S(2)}, u32[]{:S(2)}) collective-permute-start(f32[48,1024]{1,0:T(8,128)S(1)} %get-tuple-element.24.refs_0_), channel_id=1, source_target_pairs={{0,2},{2,0},{1,3},{3,1},{4,6},{6,4},{5,7},{7,5},{8,10},{10,8},{9,1... | collective-permute-start | bytes 589832 | tf_op jit(solution)/shard_map/ppermute | solution.py:308
  5.9 2.2 %far_sums.3 = (f32[48,1024]{1,0:T(8,128)S(1)}, f32[48,1024]{1,0:T(8,128)S(1)}) custom-call(s32[8]{0:T(128)S(1)} %copy-done.1, f32[12,8,16384]{2,1,0:T(8,128)} %bitcast.3, f32[48,1024]{1,0:T(8,128)S(1)} %get-tuple-element.24.refs_0_), custom_call_target="tpu_custom_call" | custom-call | flops 1 | bytes 1 | tf_op jit(solution)/shard_map/far_sums/pallas_call | solution.py:216
  8.1 0.0 copy-start
  8.1 0.0 copy-start.3
  8.1 0.0 copy-start.4
  8.2 0.1 collective-permute-start.6
  8.2 2.8 %near_sums.1 = (f32[24,2048]{1,0:T(8,128)S(1)}, f32[24,2048]{1,0:T(8,128)S(1)}, f32[24,2048]{1,0:T(8,128)S(1)}, f32[24,2048]{1,0:T(8,128)S(1)}) custom-call(s32[8]{0:T(128)S(1)} %copy-done.2, f32[12,8,16384]{2,1,0:T(8,128)} %bitcast.4, f32[48,1024]{1,0:T(8,128)S(1)} %get-tuple-element.25.refs_0_), custom_call_target="tpu_custom_call" | custom-call | flops 1 | bytes 1 | tf_op jit(solution)/shard_map/near_sums/pallas_call | solution.py:216
  11.0 0.1 collective-permute-start
  11.1 2.1 %collective-permute-start.1 = (f32[24,2048]{1,0:T(8,128)S(1)}, f32[24,2048]{1,0:T(8,128)S(1)}, u32[]{:S(2)}, u32[]{:S(2)}) collective-permute-start(f32[24,2048]{1,0:T(8,128)S(1)} %get-tuple-element.28), channel_id=1, source_target_pairs={{0,4},{1,5},{4,0},{5,1},{8,12},{9,13},{12,8},{13,9},{2,6},{3,7},{6... | collective-permute-start | bytes 589832 | tf_op jit(solution)/shard_map/ppermute | solution.py:305
  13.2 0.1 collective-permute-start.2
  13.3 0.0 collective-permute-done.3.got
  13.3 2.8 %collective-permute-start.4 = (f32[24,1024]{1,0:T(8,128)S(1)}, f32[24,1024]{1,0:T(8,128)S(1)}, u32[]{:S(2)}, u32[]{:S(2)}) collective-permute-start(f32[24,1024]{1,0:T(8,128)S(1)} %get-tuple-element.31.refs_0_), channel_id=1, source_target_pairs={{0,8},{1,9},{4,12},{5,13},{8,0},{9,1},{12,4},{13,5},{2,10},{3,11},... | collective-permute-start | bytes 294920 | tf_op jit(solution)/shard_map/ppermute | solution.py:305
  16.1 0.0 collective-permute-done.6.got
  16.1 0.6 %collective-permute-start.5 = (f32[24,1024]{1,0:T(8,128)S(1)}, f32[24,1024]{1,0:T(8,128)S(1)}, u32[]{:S(2)}, u32[]{:S(2)}) collective-permute-start(f32[24,1024]{1,0:T(8,128)S(1)} %get-tuple-element.32.refs_1_), channel_id=1, source_target_pairs={{0,9},{1,8},{4,13},{5,12},{8,1},{9,0},{12,5},{13,4},{2,11},{3,10},... | collective-permute-start | bytes 294920 | tf_op jit(solution)/shard_map/ppermute | solution.py:305
  17.5 9.6 %place_tiles.1 = (bf16[1024,2048]{1,0:T(8,128)(2,1)S(1)}, bf16[1024,2048]{1,0:T(8,128)(2,1)S(1)}) custom-call(s32[128]{0:T(128)S(1)} %copy-done.3, s32[128]{0:T(128)S(1)} %copy-done.4, s32[1]{0:T(128)S(6)} %copy.7.count, f32[64,8192]{1,0:T(8,128)S(1)} %copy-done, f32[24,1024]{1,0:T(8,128)S(1)} %get-tuple-element.31.refs_0_, ...), custom_call_target="tpu_custom_call" | custom-call | flops 1 | bytes 1 | tf_op jit(solution)/shard_map/place_tiles/pallas_call | solution.py:67
  27.1 0.1 collective-permute-start.12
  27.2 0.0 collective-permute-done.1.other_lev
  27.2 5.6 %collective-permute-start.13 = (f32[24,1024]{1,0:T(8,128)S(1)}, f32[24,1024]{1,0:T(8,128)S(1)}, u32[]{:S(2)}, u32[]{:S(2)}) collective-permute-start(f32[24,1024]{1,0:T(8,128)S(1)} %get-tuple-element.35.refs_3_), channel_id=1, source_target_pairs={{0,13},{1,12},{4,9},{5,8},{8,5},{9,4},{12,1},{13,0},{2,15},{3,14},... | collective-permute-start | bytes 294920 | tf_op jit(solution)/shard_map/ppermute | solution.py:305
  32.8 0.0 collective-permute-done.2.other_both
  32.8 3.3 %remap_first.1 = (f32[24,1024]{1,0:T(8,128)S(1)}, f32[24,1024]{1,0:T(8,128)S(1)}, f32[24,1024]{1,0:T(8,128)S(1)}, f32[24,1024]{1,0:T(8,128)S(1)}, f32[24,1024]{1,0:T(8,128)S(1)}) custom-call(f32[24,2048]{1,0:T(8,128)S(1)} %get-tuple-element.26.own, f32[24,2048]{1,0:T(8,128)S(1)} %collective-permute-done.other_sub, ...), custom_call_target="tpu_custom_call" | custom-call | flops 1 | bytes 1 | tf_op jit(solution)/shard_map/remap_first/pallas_call | solution.py:92
  36.1 1.3 %collective-permute-start.7 = (f32[24,1024]{1,0:T(8,128)S(1)}, f32[24,1024]{1,0:T(8,128)S(1)}, u32[]{:S(2)}, u32[]{:S(2)}) collective-permute-start(f32[24,1024]{1,0:T(8,128)S(1)} %get-tuple-element.38.refs_0_), channel_id=1, source_target_pairs={{2,0},{6,4},{8,10},{12,14},{3,1},{7,5},{9,11},{13,15},{18,16},{22,... | collective-permute-start | bytes 294920 | tf_op jit(solution)/shard_map/ppermute | solution.py:312
  37.4 1.3 %collective-permute-start.8 = (f32[24,1024]{1,0:T(8,128)S(1)}, f32[24,1024]{1,0:T(8,128)S(1)}, u32[]{:S(2)}, u32[]{:S(2)}) collective-permute-start(f32[24,1024]{1,0:T(8,128)S(1)} %get-tuple-element.39.refs_1_), channel_id=1, source_target_pairs={{2,0},{6,4},{8,10},{12,14},{3,1},{7,5},{9,11},{13,15},{18,16},{22,... | collective-permute-start | bytes 294920 | tf_op jit(solution)/shard_map/ppermute | solution.py:312
  38.7 1.3 %collective-permute-start.9 = (f32[24,1024]{1,0:T(8,128)S(1)}, f32[24,1024]{1,0:T(8,128)S(1)}, u32[]{:S(2)}, u32[]{:S(2)}) collective-permute-start(f32[24,1024]{1,0:T(8,128)S(1)} %get-tuple-element.40.refs_2_), channel_id=1, source_target_pairs={{2,0},{6,4},{8,10},{12,14},{3,1},{7,5},{9,11},{13,15},{18,16},{22,... | collective-permute-start | bytes 294920 | tf_op jit(solution)/shard_map/ppermute | solution.py:312
  40.1 1.3 %collective-permute-start.10 = (f32[24,1024]{1,0:T(8,128)S(1)}, f32[24,1024]{1,0:T(8,128)S(1)}, u32[]{:S(2)}, u32[]{:S(2)}) collective-permute-start(f32[24,1024]{1,0:T(8,128)S(1)} %get-tuple-element.41.refs_3_), channel_id=1, source_target_pairs={{2,0},{6,4},{8,10},{12,14},{3,1},{7,5},{9,11},{13,15},{18,16},{22,... | collective-permute-start | bytes 294920 | tf_op jit(solution)/shard_map/ppermute | solution.py:312
  41.4 4.6 %collective-permute-start.11 = (f32[24,1024]{1,0:T(8,128)S(1)}, f32[24,1024]{1,0:T(8,128)S(1)}, u32[]{:S(2)}, u32[]{:S(2)}) collective-permute-start(f32[24,1024]{1,0:T(8,128)S(1)} %get-tuple-element.42.refs_8_), channel_id=1, source_target_pairs={{0,2},{4,6},{10,8},{14,12},{1,3},{5,7},{11,9},{15,13},{16,18},{20,... | collective-permute-start | bytes 294920 | tf_op jit(solution)/shard_map/ppermute | solution.py:312
  45.9 3.0 %remap_last.1.refs_10_ = f32[24,1024]{1,0:T(8,128)S(1)} custom-call(f32[24,1024]{1,0:T(8,128)S(1)} %collective-permute-done.12.same, f32[24,1024]{1,0:T(8,128)S(1)} %collective-permute-done.13.other, bf16[1024,2048]{1,0:T(8,128)(2,1)S(1)} %get-tuple-element.36.high, bf16[1024,2048]{1,0:T(8,128)(2,1)S(1)} %get-tuple-element.37.low), custom_call_target="tpu_custom_call" | custom-call | flops 1 | bytes 1 | tf_op jit(solution)/shard_map/remap_last/pallas_call | solution.py:92
  49.0 1.3 %collective-permute-start.14 = (f32[24,1024]{1,0:T(8,128)S(1)}, f32[24,1024]{1,0:T(8,128)S(1)}, u32[]{:S(2)}, u32[]{:S(2)}) collective-permute-start(f32[24,1024]{1,0:T(8,128)S(1)} %remap_last.1.refs_10_), channel_id=1, source_target_pairs={{0,2},{4,6},{10,8},{14,12},{1,3},{5,7},{11,9},{15,13},{16,18},{20,... | collective-permute-start | bytes 294920 | tf_op jit(solution)/shard_map/ppermute | solution.py:312
  50.3 2.1 %collective-permute-done.14.refs_11_ = f32[24,1024]{1,0:T(8,128)S(1)} collective-permute-done((f32[24,1024]{1,0:T(8,128)S(1)}, f32[24,1024]{1,0:T(8,128)S(1)}, u32[]{:S(2)}, u32[]{:S(2)}) %collective-permute-start.14) | collective-permute-done | bytes 98336 | tf_op jit(solution)/shard_map/ppermute | solution.py:312
  52.5 0.8 %finish.1 = f32[96,1024]{1,0:T(8,128)} custom-call(f32[24,1024]{1,0:T(8,128)S(1)} %get-tuple-element.38.refs_0_, f32[24,1024]{1,0:T(8,128)S(1)} %get-tuple-element.39.refs_1_, f32[24,1024]{1,0:T(8,128)S(1)} %get-tuple-element.40.refs_2_, f32[24,1024]{1,0:T(8,128)S(1)} %get-tuple-element.41.refs_3_, f32[24,1024]{1,0:T(8,128)S(1)} %collective-permute-done.7.refs_4_, ...), custom_call_target="tpu_custom_call" | custom-call | tf_op jit(solution)/shard_map/finish/pallas_call | solution.py:287
  (17 shorter events, 0.1 us)
Async XLA Ops:
  0.0 0.7 %copy-start.1 = (s32[8]{0:T(128)S(1)}, s32[8]{0:T(128)}, u32[]{:S(2)}) copy-start(s32[8]{0:T(128)} %step_hour.5) | copy-start | bytes 100
  2.9 5.4 %copy-start.2 = (s32[8]{0:T(128)S(1)}, s32[8]{0:T(128)}, u32[]{:S(2)}) copy-start(s32[8]{0:T(128)} %step_hour.5) | copy-start | bytes 100
  2.9 10.4 %collective-permute-start.3 = (f32[48,1024]{1,0:T(8,128)S(1)}, f32[48,1024]{1,0:T(8,128)S(1)}, u32[]{:S(2)}, u32[]{:S(2)}) collective-permute-start(f32[48,1024]{1,0:T(8,128)S(1)} %get-tuple-element.24.refs_0_), channel_id=1, source_target_pairs={{0,2},{2,0},{1,3},{3,1},{4,6},{6,4},{5,7},{7,5},{8,10},{10,8},{9,1... | collective-permute-start | bytes 589832 | tf_op jit(solution)/shard_map/ppermute | solution.py:308
  8.1 9.3 %copy-start = (f32[64,8192]{1,0:T(8,128)S(1)}, f32[64,8192]{1,0:T(8,128)}, u32[]{:S(2)}) copy-start(f32[64,8192]{1,0:T(8,128)} %weights.1) | copy-start | bytes 6291460
  8.1 9.3 %copy-start.3 = (s32[128]{0:T(128)S(1)}, s32[128]{0:T(128)}, u32[]{:S(2)}) copy-start(s32[128]{0:T(128)} %rows.1) | copy-start | bytes 1540
  8.1 9.3 %copy-start.4 = (s32[128]{0:T(128)S(1)}, s32[128]{0:T(128)}, u32[]{:S(2)}) copy-start(s32[128]{0:T(128)} %columns.1) | copy-start | bytes 1540
  8.2 8.0 %collective-permute-start.6 = (f32[48,1024]{1,0:T(8,128)S(1)}, f32[48,1024]{1,0:T(8,128)S(1)}, u32[]{:S(2)}, u32[]{:S(2)}) collective-permute-start(f32[48,1024]{1,0:T(8,128)S(1)} %get-tuple-element.25.refs_0_), channel_id=1, source_target_pairs={{0,2},{2,0},{1,3},{3,1},{4,6},{6,4},{5,7},{7,5},{8,10},{10,8},{9,1... | collective-permute-start | bytes 589832 | tf_op jit(solution)/shard_map/ppermute | solution.py:308
  11.0 16.1 %collective-permute-start = (f32[24,2048]{1,0:T(8,128)S(1)}, f32[24,2048]{1,0:T(8,128)S(1)}, u32[]{:S(2)}, u32[]{:S(2)}) collective-permute-start(f32[24,2048]{1,0:T(8,128)S(1)} %get-tuple-element.27), channel_id=1, source_target_pairs={{0,1},{1,0},{4,5},{5,4},{8,9},{9,8},{12,13},{13,12},{2,3},{3,2},{6... | collective-permute-start | bytes 589832 | tf_op jit(solution)/shard_map/ppermute | solution.py:305
  11.1 16.1 %collective-permute-start.1 = (f32[24,2048]{1,0:T(8,128)S(1)}, f32[24,2048]{1,0:T(8,128)S(1)}, u32[]{:S(2)}, u32[]{:S(2)}) collective-permute-start(f32[24,2048]{1,0:T(8,128)S(1)} %get-tuple-element.28), channel_id=1, source_target_pairs={{0,4},{1,5},{4,0},{5,1},{8,12},{9,13},{12,8},{13,9},{2,6},{3,7},{6... | collective-permute-start | bytes 589832 | tf_op jit(solution)/shard_map/ppermute | solution.py:305
  13.2 19.6 %collective-permute-start.2 = (f32[24,2048]{1,0:T(8,128)S(1)}, f32[24,2048]{1,0:T(8,128)S(1)}, u32[]{:S(2)}, u32[]{:S(2)}) collective-permute-start(f32[24,2048]{1,0:T(8,128)S(1)} %get-tuple-element.29), channel_id=1, source_target_pairs={{0,5},{1,4},{4,1},{5,0},{8,13},{9,12},{12,9},{13,8},{2,7},{3,6},{6... | collective-permute-start | bytes 589832 | tf_op jit(solution)/shard_map/ppermute | solution.py:305
  13.3 19.5 %collective-permute-start.4 = (f32[24,1024]{1,0:T(8,128)S(1)}, f32[24,1024]{1,0:T(8,128)S(1)}, u32[]{:S(2)}, u32[]{:S(2)}) collective-permute-start(f32[24,1024]{1,0:T(8,128)S(1)} %get-tuple-element.31.refs_0_), channel_id=1, source_target_pairs={{0,8},{1,9},{4,12},{5,13},{8,0},{9,1},{12,4},{13,5},{2,10},{3,11},... | collective-permute-start | bytes 294920 | tf_op jit(solution)/shard_map/ppermute | solution.py:305
  16.1 16.7 %collective-permute-start.5 = (f32[24,1024]{1,0:T(8,128)S(1)}, f32[24,1024]{1,0:T(8,128)S(1)}, u32[]{:S(2)}, u32[]{:S(2)}) collective-permute-start(f32[24,1024]{1,0:T(8,128)S(1)} %get-tuple-element.32.refs_1_), channel_id=1, source_target_pairs={{0,9},{1,8},{4,13},{5,12},{8,1},{9,0},{12,5},{13,4},{2,11},{3,10},... | collective-permute-start | bytes 294920 | tf_op jit(solution)/shard_map/ppermute | solution.py:305
  27.1 13.0 %collective-permute-start.12 = (f32[24,1024]{1,0:T(8,128)S(1)}, f32[24,1024]{1,0:T(8,128)S(1)}, u32[]{:S(2)}, u32[]{:S(2)}) collective-permute-start(f32[24,1024]{1,0:T(8,128)S(1)} %get-tuple-element.34.refs_2_), channel_id=1, source_target_pairs={{0,12},{1,13},{4,8},{5,9},{8,4},{9,5},{12,0},{13,1},{2,14},{3,15},... | collective-permute-start | bytes 294920 | tf_op jit(solution)/shard_map/ppermute | solution.py:305
  27.2 14.2 %collective-permute-start.13 = (f32[24,1024]{1,0:T(8,128)S(1)}, f32[24,1024]{1,0:T(8,128)S(1)}, u32[]{:S(2)}, u32[]{:S(2)}) collective-permute-start(f32[24,1024]{1,0:T(8,128)S(1)} %get-tuple-element.35.refs_3_), channel_id=1, source_target_pairs={{0,13},{1,12},{4,9},{5,8},{8,5},{9,4},{12,1},{13,0},{2,15},{3,14},... | collective-permute-start | bytes 294920 | tf_op jit(solution)/shard_map/ppermute | solution.py:305
  36.1 12.8 %collective-permute-start.7 = (f32[24,1024]{1,0:T(8,128)S(1)}, f32[24,1024]{1,0:T(8,128)S(1)}, u32[]{:S(2)}, u32[]{:S(2)}) collective-permute-start(f32[24,1024]{1,0:T(8,128)S(1)} %get-tuple-element.38.refs_0_), channel_id=1, source_target_pairs={{2,0},{6,4},{8,10},{12,14},{3,1},{7,5},{9,11},{13,15},{18,16},{22,... | collective-permute-start | bytes 294920 | tf_op jit(solution)/shard_map/ppermute | solution.py:312
  37.4 12.9 %collective-permute-start.8 = (f32[24,1024]{1,0:T(8,128)S(1)}, f32[24,1024]{1,0:T(8,128)S(1)}, u32[]{:S(2)}, u32[]{:S(2)}) collective-permute-start(f32[24,1024]{1,0:T(8,128)S(1)} %get-tuple-element.39.refs_1_), channel_id=1, source_target_pairs={{2,0},{6,4},{8,10},{12,14},{3,1},{7,5},{9,11},{13,15},{18,16},{22,... | collective-permute-start | bytes 294920 | tf_op jit(solution)/shard_map/ppermute | solution.py:312
  38.7 11.6 %collective-permute-start.9 = (f32[24,1024]{1,0:T(8,128)S(1)}, f32[24,1024]{1,0:T(8,128)S(1)}, u32[]{:S(2)}, u32[]{:S(2)}) collective-permute-start(f32[24,1024]{1,0:T(8,128)S(1)} %get-tuple-element.40.refs_2_), channel_id=1, source_target_pairs={{2,0},{6,4},{8,10},{12,14},{3,1},{7,5},{9,11},{13,15},{18,16},{22,... | collective-permute-start | bytes 294920 | tf_op jit(solution)/shard_map/ppermute | solution.py:312
  40.1 10.3 %collective-permute-start.10 = (f32[24,1024]{1,0:T(8,128)S(1)}, f32[24,1024]{1,0:T(8,128)S(1)}, u32[]{:S(2)}, u32[]{:S(2)}) collective-permute-start(f32[24,1024]{1,0:T(8,128)S(1)} %get-tuple-element.41.refs_3_), channel_id=1, source_target_pairs={{2,0},{6,4},{8,10},{12,14},{3,1},{7,5},{9,11},{13,15},{18,16},{22,... | collective-permute-start | bytes 294920 | tf_op jit(solution)/shard_map/ppermute | solution.py:312
  41.4 9.0 %collective-permute-start.11 = (f32[24,1024]{1,0:T(8,128)S(1)}, f32[24,1024]{1,0:T(8,128)S(1)}, u32[]{:S(2)}, u32[]{:S(2)}) collective-permute-start(f32[24,1024]{1,0:T(8,128)S(1)} %get-tuple-element.42.refs_8_), channel_id=1, source_target_pairs={{0,2},{4,6},{10,8},{14,12},{1,3},{5,7},{11,9},{15,13},{16,18},{20,... | collective-permute-start | bytes 294920 | tf_op jit(solution)/shard_map/ppermute | solution.py:312
  49.0 3.5 %collective-permute-start.14 = (f32[24,1024]{1,0:T(8,128)S(1)}, f32[24,1024]{1,0:T(8,128)S(1)}, u32[]{:S(2)}, u32[]{:S(2)}) collective-permute-start(f32[24,1024]{1,0:T(8,128)S(1)} %remap_last.1.refs_10_), channel_id=1, source_target_pairs={{0,2},{4,6},{10,8},{14,12},{1,3},{5,7},{11,9},{15,13},{16,18},{20,... | collective-permute-start | bytes 294920 | tf_op jit(solution)/shard_map/ppermute | solution.py:312

commit v2 on v1

--- a/solution.py
+++ b/solution.py
@@ -18,6 +18,7 @@
 MIB = 1 << 20
 
 LIGHT = pl.CostEstimate(flops=1, bytes_accessed=1, transcendentals=0)
+HEAVY = pl.CostEstimate(flops=10_000_000_000, bytes_accessed=1, transcendentals=0)
 
 NT = (((1,), (1,)), ((), ()))
 NN = (((1,), (0,)), ((), ()))
@@ -32,6 +33,9 @@
     return lax.dot_general(a, b, dims, preferred_element_type=jnp.float32)
 
 
+GROUP = 8
+
+
 def place_kernel(rows, columns, count, weights, *refs):
     high, low, total = refs[-3:]
     band = 128
@@ -41,18 +45,24 @@
         total[pl.ds(pl.multiple_of(b * band, band), band), :] = jnp.zeros((band, CELLS_DEV), jnp.float32)
 
     lane_half = lax.broadcasted_iota(jnp.int32, (TILE, LANES), 1) // TILE
-
-    @pl.loop(0, count[0])
-    def _(k):
-        column = columns[k]
-        side = column % 2
-        tile = weights[:, pl.ds(pl.multiple_of((k // 2) * LANES, LANES), LANES)]
-        moved = pltpu.roll(tile, ((k + column) % 2) * TILE, 1)
-        at = (
-            pl.ds(pl.multiple_of(rows[k] * TILE, TILE), TILE),
-            pl.ds(pl.multiple_of((column // 2) * LANES, LANES), LANES),
-        )
-        total[at] = total[at] + jnp.where(lane_half == side, moved, 0.0)
+    live = count[0]
+
+    @pl.loop(0, (live + GROUP - 1) // GROUP)
+    def _(g):
+        for pair in range(GROUP // 2):
+            lanes = pl.ds(pl.multiple_of((g * (GROUP // 2) + pair) * LANES, LANES), LANES)
+            tiles = weights[:, lanes]
+            turned = pltpu.roll(tiles, TILE, 1)
+            for i in range(2):
+                k = g * GROUP + pair * 2 + i
+                row, column = rows[k], columns[k]
+                side = jnp.where(k < live, column & 1, -1)
+                tile = jnp.where(lane_half == i, tiles, turned)
+                at = (
+                    pl.ds(pl.multiple_of(row * TILE, TILE), TILE),
+                    pl.ds(pl.multiple_of((column >> 1) * LANES, LANES), LANES),
+                )
+                total[at] = total[at] + jnp.where(lane_half == side, tile, 0.0)
 
     @pl.loop(0, PIXELS_DEV // band)
     def _(b):
@@ -71,7 +81,7 @@
         out_specs=(vmem, vmem),
         scratch_shapes=[pltpu.VMEM((PIXELS_DEV, CELLS_DEV), jnp.float32)],
         compiler_params=pltpu.CompilerParams(vmem_limit_bytes=28 * MIB),
-        cost_estimate=LIGHT,
+        cost_estimate=HEAVY,
         name="place_tiles",
     )(rows, columns, count, weights, *after)
 
@@ -79,30 +89,32 @@
 PIXEL_BLOCK = 256
 
 
-def remap_body(x, high, low):
+def remap_blocks(x, high, low):
     m = x.shape[0]
     x_high, x_low = split(x)
-    both = dot(jnp.concatenate([x_high, x_low], axis=0), high, NT)
-    return both[:m] + both[m:] + dot(x_high, low, NT)
-
-
-def remap_call(kernel, inputs, out_rows, high, low, name):
-    whole = [pl.BlockSpec(a.shape, lambda i, nd=a.ndim: (0,) * nd) for a in inputs]
-    map_block = pl.BlockSpec((PIXEL_BLOCK, CELLS_DEV), lambda i: (i, 0))
+    both = jnp.concatenate([x_high, x_low], axis=0)
+    for start in range(0, PIXELS_DEV, PIXEL_BLOCK):
+        at = slice(start, start + PIXEL_BLOCK)
+        first = dot(both, high[at, :], NT)
+        yield at, first[:m] + first[m:] + dot(x_high, low[at, :], NT)
+
+
+def remap_call(kernel, inputs, out_rows, high, low, cost, name):
+    vmem = pl.BlockSpec(memory_space=pltpu.VMEM)
     return pl.pallas_call(
         kernel,
         out_shape=[jax.ShapeDtypeStruct((rows, PIXELS_DEV), jnp.float32) for rows in out_rows],
-        grid=(PIXELS_DEV // PIXEL_BLOCK,),
-        in_specs=whole + [map_block, map_block],
-        out_specs=[pl.BlockSpec((rows, PIXEL_BLOCK), lambda i: (0, i)) for rows in out_rows],
+        in_specs=[vmem] * (len(inputs) + 2),
+        out_specs=[vmem] * len(out_rows),
         compiler_params=pltpu.CompilerParams(vmem_limit_bytes=24 * MIB),
-        cost_estimate=LIGHT,
+        cost_estimate=cost,
         name=name,
     )(*inputs, high, low)
 
 
 def remap_rows_kernel(x, high, low, out):
-    out[...] = remap_body(x[...], high[...], low[...])
+    for at, result in remap_blocks(x[...], high, low):
+        out[:, at] = result
 
 
 def near_rows(own, other_sub, other_lev, other_both):
@@ -125,24 +137,41 @@
     return [jnp.concatenate([block[:levels], block[levels:]], axis=1) for block in blocks]
 
 
-def remap_first_kernel(own, other_sub, other_lev, other_both, same, other, high, low, *outs):
-    levels = own.shape[0] // HOURS
-    blocks = near_rows(own[...], other_sub[...], other_lev[...], other_both[...])
+def keeps_near():
+    return lax.axis_index("tm") == lax.axis_index("lev") // 2
+
+
+def remap_first_kernel(own, sibling, other_lev, same, other, high, low, near_out, far_out, send):
+    rows = own.shape[0]
+    levels = rows // HOURS
+    blocks = near_rows(own[...], sibling[:rows], other_lev[:rows], other_lev[rows:])
     x = jnp.concatenate(blocks + far_rows(same[...], other[...]), axis=0)
-    result = remap_body(x, high[...], low[...])
-    for hour in range(HOURS):
-        for lev in range(2):
-            pieces = []
-            for sub in range(2):
-                start = ((lev * 2 + sub) * HOURS + hour) * levels
-                pieces.append(result[start : start + levels])
-            outs[hour * 2 + lev][...] = jnp.concatenate(pieces, axis=0)
-    outs[-1][...] = result[4 * HOURS * levels :]
+    for at, result in remap_blocks(x, high, low):
+        for hour in range(HOURS):
+            for lev in range(2):
+                pieces = []
+                for sub in range(2):
+                    start = ((lev * 2 + sub) * HOURS + hour) * levels
+                    pieces.append(result[start : start + levels])
+                place = (hour * 2 + lev) * rows
+                near_out[place : place + rows, at] = jnp.concatenate(pieces, axis=0)
+        far_out[:, at] = result[4 * rows :]
+    near = keeps_near()
+
+    @pl.when(near)
+    def _():
+        send[:rows] = far_out[...]
+        send[rows:] = jnp.zeros((send.shape[0] - rows, PIXELS_DEV), jnp.float32)
+
+    @pl.when(jnp.logical_not(near))
+    def _():
+        send[...] = near_out[...]
 
 
 def remap_last_kernel(same, other, high, low, out):
     x = jnp.concatenate(far_rows(same[...], other[...]), axis=0)
-    out[...] = remap_body(x, high[...], low[...])
+    for at, result in remap_blocks(x, high, low):
+        out[:, at] = result
 
 
 def hour_matrix(step_hour, levels, steps, hours, cuts):
@@ -184,14 +213,19 @@
 
 
 def near_sum_kernel(peers, step_hour, field, *refs):
-    *outs, buffer, arrived = refs[-len(peers) - 2 :]
+    own, other_lev, sibling, buffer, arrived = refs[-5:]
     _, levels, steps, cells = buffer.shape
+    rows = HOURS * levels
     copies = field_copies(field, buffer, arrived, peers)
     matrix = hour_matrix(step_hour, levels, steps, range(HOURS), 1)
-    for place, out in enumerate(outs):
+    for place, (k, j) in enumerate(peers):
         copies[place].wait()
         x = buffer[place].reshape(levels * steps, cells)
-        out[...] = dot(matrix, jnp.concatenate(split(x), axis=0), NN)
+        result = dot(matrix, jnp.concatenate(split(x), axis=0), NN)
+        if j == 0:
+            (own if k == 0 else other_lev)[...] = result
+        else:
+            sibling[k * rows : (k + 1) * rows] = result
 
 
 def far_sum_kernel(peers, step_hour, field, *refs):
@@ -229,8 +263,9 @@
 
 
 def near_sums(peers, step_hour, field, *after):
-    shape = jax.ShapeDtypeStruct((HOURS * field.shape[0], CELLS_DEV), jnp.float32)
-    return sum_call(near_sum_kernel, peers, step_hour, field, after, [shape] * len(peers), "near_sums")
+    rows = HOURS * field.shape[0]
+    shapes = [jax.ShapeDtypeStruct((n * rows, CELLS_DEV), jnp.float32) for n in (1, 1, 2)]
+    return sum_call(near_sum_kernel, peers, step_hour, field, after, shapes, "near_sums")
 
 
 def far_sums(peers, step_hour, field, *after):
@@ -238,60 +273,63 @@
     return sum_call(far_sum_kernel, peers, step_hour, field, after, [shape] * 2, "far_sums")
 
 
-def merge_kernel(mine, got, *outs):
+def merge_kernel(mine, got, *refs):
+    outs = refs[-2:]
     rows = outs[0].shape[0]
     for place, out in enumerate(outs):
         at = slice(place * rows, (place + 1) * rows)
         out[...] = mine[at] + got[at]
 
 
-def merge(mine, got, parts):
+def join_kernel(mine, got, *refs):
+    rows = mine.shape[0]
+    refs[-1][:rows] = mine[...]
+    refs[-1][rows:] = got[rows:]
+
+
+def small_call(kernel, inputs, after, shapes, cost, name):
     vmem = pl.BlockSpec(memory_space=pltpu.VMEM)
-    shape = jax.ShapeDtypeStruct((mine.shape[0] // parts, mine.shape[1]), jnp.float32)
     return pl.pallas_call(
-        merge_kernel,
-        out_shape=[shape] * parts,
-        in_specs=[vmem, vmem],
-        out_specs=[vmem] * parts,
-        compiler_params=pltpu.CompilerParams(vmem_limit_bytes=4 * MIB),
-        cost_estimate=LIGHT,
-        name="merge",
-    )(mine, got)
-
-
-def finish_kernel(divisor, *refs):
-    *arrays, out = refs
-    a_own, a_got, b_own, b_got = arrays[-4:]
+        kernel,
+        out_shape=[jax.ShapeDtypeStruct(shape, jnp.float32) for shape in shapes],
+        in_specs=[vmem] * len(inputs) + [pl.BlockSpec(memory_space=pl.ANY)] * len(after),
+        out_specs=[vmem] * len(shapes),
+        compiler_params=pltpu.CompilerParams(vmem_limit_bytes=8 * MIB),
+        cost_estimate=cost,
+        name=name,
+    )(*inputs, *after)
+
+
+def merge(mine, got, *after):
+    shape = (mine.shape[0] // 2, mine.shape[1])
+    return small_call(merge_kernel, [mine, got], after, [shape, shape], HEAVY, "merge")
+
+
+def join(mine, got, *after):
+    return small_call(join_kernel, [mine, got], after, [got.shape], HEAVY, "join")[0]
+
+
+def finish_kernel(divisor, near_own, far_own, got, last, got_last, out):
     me, lev = lax.axis_index("tm"), lax.axis_index("lev")
-    half = a_own.shape[0]
-    keeps_near = me == lev // 2
-
-    @pl.when(keeps_near)
+    rows = far_own.shape[0]
+    near = keeps_near()
+
+    @pl.when(near)
     def _():
-        for place in range(2 * HOURS):
-            total = arrays[place][...] + arrays[2 * HOURS + place][...]
-            out[place * half : (place + 1) * half, :] = total / divisor
-
-    @pl.when(jnp.logical_not(keeps_near))
+        out[...] = (near_own[...] + got[...]) / divisor
+
+    @pl.when(jnp.logical_not(near))
     def _():
         for hour in range(HOURS):
-            a_at = pl.multiple_of((hour * 2 + lev % 2) * half, half)
-            b_at = pl.multiple_of((hour * 2 + 1 - lev % 2) * half, half)
-            out[pl.ds(a_at, half), :] = jnp.where(me == hour, a_own[...], a_got[...]) / divisor
-            out[pl.ds(b_at, half), :] = jnp.where(me == hour, b_own[...], b_got[...]) / divisor
+            first_at = pl.multiple_of((hour * 2 + 1 - lev % 2) * rows, rows)
+            last_at = pl.multiple_of((hour * 2 + lev % 2) * rows, rows)
+            out[pl.ds(first_at, rows), :] = jnp.where(me == hour, far_own[...], got[:rows]) / divisor
+            out[pl.ds(last_at, rows), :] = jnp.where(me == hour, last[...], got_last[...]) / divisor
 
 
 def finish(arrays, divisor):
-    vmem = pl.BlockSpec(memory_space=pltpu.VMEM)
-    rows, pixels = arrays[0].shape
-    return pl.pallas_call(
-        functools.partial(finish_kernel, divisor),
-        out_shape=jax.ShapeDtypeStruct((2 * HOURS * rows, pixels), jnp.float32),
-        in_specs=[vmem] * len(arrays),
-        out_specs=vmem,
-        compiler_params=pltpu.CompilerParams(vmem_limit_bytes=8 * MIB),
-        name="finish",
-    )(*arrays)
+    call = functools.partial(finish_kernel, divisor)
+    return small_call(call, arrays, [], [arrays[0].shape], LIGHT, "finish")[0]
 
 
 def hour_plan(level_field, tile_weight, tile_rows, tile_columns, live_count, step_hour):
@@ -307,34 +345,34 @@
     def swap(x):
         return lax.ppermute(x, "tm", [(0, 1), (1, 0)])
 
-    def move(x, keeper):
-        pairs = [(a * shards_tm + 1 - keeper(a), a * shards_tm + keeper(a)) for a in range(levs)]
-        return lax.ppermute(x, ("lev", "tm"), pairs)
-
-    far_peers = [[(k, j) for j in range(subs)] for k in range(half, levs)]
-    near_peers = [(k, j) for k in range(half) for j in range(subs)]
-    sums = []
-    for peers in far_peers:
-        sums.append(far_sums(peers, step_hour, field, *[theirs for theirs, _ in sums]))
-    swapped = [swap(theirs) for theirs, _ in sums]
-    near = near_sums(near_peers, step_hour, field, sums[-1][0])
-    near = [near[0]] + [to_peer(x, k, j) for x, (k, j) in list(zip(near, near_peers))[1:]]
-    far, merges = [], []
-    for peers, (_, mine), got in zip(far_peers, sums, swapped):
-        merged = merge(mine, got, subs)
-        merges += merged
-        far.append([to_peer(x, k, j) for x, (k, j) in zip(merged, peers)])
-
-    high, low = place_tiles(tile_rows, tile_columns, live_count, tile_weight, *merges)
-    rows = far[0][0].shape[0]
-    *near_out, a_out = remap_call(
-        remap_first_kernel, near + far[0], [rows] * (2 * HOURS + 1), high, low, "remap_first"
+    def far_peers(k):
+        return [(k, j) for j in range(subs)]
+
+    near_peers = [(k, j) for j in reversed(range(subs)) for k in reversed(range(half))]
+    theirs_a, mine_a = far_sums(far_peers(half + 1), step_hour, field)
+    got_a = swap(theirs_a)
+    own, other_lev, sibling = near_sums(near_peers, step_hour, field, theirs_a)
+    got_sibling = to_peer(sibling, 0, 1)
+    theirs_b, mine_b = far_sums(far_peers(half), step_hour, field, sibling)
+    got_b = swap(theirs_b)
+
+    merged_a = merge(mine_a, got_a, theirs_b)
+    far_a = [to_peer(x, half + 1, j) for j, x in enumerate(merged_a)]
+    joined = join(other_lev, got_sibling, *merged_a)
+    got_lev = to_peer(joined, 1, 0)
+    merged_b = merge(mine_b, got_b, joined)
+    far_b = [to_peer(x, half, j) for j, x in enumerate(merged_b)]
+
+    high, low = place_tiles(tile_rows, tile_columns, live_count, tile_weight, *merged_b)
+    rows = mine_a.shape[0] // subs
+    near = [own, got_sibling, got_lev]
+    near_out, far_out, send = remap_call(
+        remap_first_kernel, near + far_a, [4 * rows, rows, 4 * rows], high, low, LIGHT, "remap_first"
     )
-    near_got = [move(x, lambda a: a // half) for x in near_out]
-    a_got = move(a_out, lambda a: 1 - a // half)
-    (b_out,) = remap_call(remap_last_kernel, far[1], [rows], high, low, "remap_last")
-    b_got = move(b_out, lambda a: 1 - a // half)
-    out = finish(near_out + near_got + [a_out, a_got, b_out, b_got], divisor)
+    got = swap(send)
+    (last,) = remap_call(remap_last_kernel, far_b, [rows], high, low, HEAVY, "remap_last")
+    got_last = swap(last)
+    out = finish([near_out, far_out, got, last, got_last], divisor)
     return out.reshape(HOURS, out.shape[0] // HOURS, PIXELS_DEV)
 
 
@@ -349,7 +387,7 @@
     regrouped = lax.all_to_all(partial, ("lev", "sub"), split_axis=0, concat_axis=0, tiled=True)
     rows = jnp.transpose(regrouped, (1, 0, 2, 3)).reshape(-1, cells // shards)
     high, low = place_tiles(tile_rows, tile_columns, live_count, tile_weight)
-    (out,) = remap_call(remap_rows_kernel, [rows], [rows.shape[0]], high, low, "remap_rows")
+    (out,) = remap_call(remap_rows_kernel, [rows], [rows.shape[0]], high, low, LIGHT, "remap_rows")
     out = out.reshape(HOURS, shards * levels, PIXELS_DEV) / divisor
     return lax.psum_scatter(out, "tm", scatter_dimension=1, tiled=True)
 

time: 53 us -> 50.5 us (0.953)
  waiting for transfers between devices: 2.19 us -> 20.1 us
  starting transfers between devices: 25.5 us -> 12.2 us
  Pallas kernels: 24 us -> 16.6 us
    ppermute x6 -> x0, starting transfers between devices: 11 us -> none  [move(): return lax.ppermute(x, ('lev', 'tm'), pairs)]
    ppermute x2 -> x4, waiting for transfers between devices: 0.01 us -> 10.5 us  [swap(): return lax.ppermute(x, 'tm', [(0, 1), (1, 0)])]
    ppermute x7 -> x6, waiting for transfers between devices: 0.02 us -> 9.59 us  [to_peer(): return lax.ppermute(x, ('lev', 'sub'), pairs)]
    pallas_call x1, Pallas kernels: 9.57 us -> 3.3 us  [place_tiles(): pl.pallas_call(place_kernel, out_shape=(half, half), in_specs=[smem, smem...]
    ppermute x7 -> x6, starting transfers between devices: 11.4 us -> 6.98 us  [to_peer(): return lax.ppermute(x, ('lev', 'sub'), pairs)]
    ppermute x6 -> x0, waiting for transfers between devices: 2.16 us -> none  [move(): return lax.ppermute(x, ('lev', 'tm'), pairs)]
    ppermute x2 -> x4, starting transfers between devices: 3.08 us -> 5.24 us  [swap(): return lax.ppermute(x, 'tm', [(0, 1), (1, 0)])]
    pallas_call x2, Pallas kernels: 6.37 us -> 5.2 us  [remap_call(): pl.pallas_call(kernel, out_shape=[jax.ShapeDtypeStruct((rows, PIXELS_DEV)...]
  transfers between devices with their start and end apart: 15 -> 10, of which waited for: 1 -> 3; matrix products, arithmetic and copies ran while one was open for 0% -> 0% of each run, Pallas kernels for 39% -> 27%
where the time goes in v2:
time: 50.5 us; the launch traced here: 50.3 us
  waiting for transfers between devices  20.1 us (40%)
  Pallas kernels  16.6 us (33%)
  starting transfers between devices  12.2 us (24%)
  between operations  0.77 us (2%)
  local copies, waits for them, and re-layouts  0.67 us (1%)
    ppermute x4, waiting for transfers between devices, swap(): return lax.ppermute(x, 'tm', [(0, 1), (1, 0)])  10.5 us
    ppermute x6, waiting for transfers between devices, to_peer(): return lax.ppermute(x, ('lev', 'sub'), pairs)  9.59 us
    pallas_call x3, Pallas kernels, sum_call(): pl.pallas_call(functools.partial(kernel, peers), out_shape=out_shapes, in...  7.18 us
    ppermute x6, starting transfers between devices, to_peer(): return lax.ppermute(x, ('lev', 'sub'), pairs)  6.98 us
    ppermute x4, starting transfers between devices, swap(): return lax.ppermute(x, 'tm', [(0, 1), (1, 0)])  5.24 us
    pallas_call x2, Pallas kernels, remap_call(): pl.pallas_call(kernel, out_shape=[jax.ShapeDtypeStruct((rows, PIXELS_DEV)...  5.2 us
    pallas_call x1, Pallas kernels, place_tiles(): pl.pallas_call(place_kernel, out_shape=(half, half), in_specs=[smem, smem...  3.3 us
  transfers between devices with their start and end apart: 10, of which 3 were waited for; matrix products, arithmetic and copies ran while one was open for 0% of the time, Pallas kernels for 27%

profile of v2, /device:TPU:0, one launch (start us, length us, event | category | flops | bytes accessed | tf_op | source)
XLA Modules:
  0.0 50.3 jit_solution(4728560343397354467)
XLA Ops:
  0.0 0.0 copy-start
  0.0 0.7 %copy-done = s32[8]{0:T(128)S(1)} copy-done((s32[8]{0:T(128)S(1)}, s32[8]{0:T(128)}, u32[]{:S(2)}) %copy-start) | copy-done | bytes 56
  0.7 2.2 %far_sums.2 = (f32[48,1024]{1,0:T(8,128)S(1)}, f32[48,1024]{1,0:T(8,128)S(1)}) custom-call(s32[8]{0:T(128)S(1)} %copy-done, f32[12,8,16384]{2,1,0:T(8,128)} %bitcast.2), custom_call_target="tpu_custom_call" | custom-call | flops 1 | bytes 1 | tf_op jit(solution)/shard_map/far_sums/pallas_call | solution.py:250
  2.9 3.0 %collective-permute-start.1 = (f32[48,1024]{1,0:T(8,128)S(1)}, f32[48,1024]{1,0:T(8,128)S(1)}, u32[]{:S(2)}, u32[]{:S(2)}) collective-permute-start(f32[48,1024]{1,0:T(8,128)S(1)} %get-tuple-element.21.refs_0_), channel_id=1, source_target_pairs={{0,2},{2,0},{1,3},{3,1},{4,6},{6,4},{5,7},{7,5},{8,10},{10,8},{9,1... | collective-permute-start | bytes 589832 | tf_op jit(solution)/shard_map/ppermute | solution.py:346
  5.9 2.7 %near_sums.1 = (f32[24,2048]{1,0:T(8,128)S(1)}, f32[24,2048]{1,0:T(8,128)S(1)}, f32[48,2048]{1,0:T(8,128)S(1)}) custom-call(s32[8]{0:T(128)S(1)} %copy-done, f32[12,8,16384]{2,1,0:T(8,128)} %bitcast.3, f32[48,1024]{1,0:T(8,128)S(1)} %get-tuple-element.21.refs_0_), custom_call_target="tpu_custom_call" | custom-call | flops 1 | bytes 1 | tf_op jit(solution)/shard_map/near_sums/pallas_call | solution.py:250
  8.6 0.1 collective-permute-start
  8.7 2.2 %far_sums.3 = (f32[48,1024]{1,0:T(8,128)S(1)}, f32[48,1024]{1,0:T(8,128)S(1)}) custom-call(s32[8]{0:T(128)S(1)} %copy-done, f32[12,8,16384]{2,1,0:T(8,128)} %bitcast.4, f32[48,2048]{1,0:T(8,128)S(1)} %get-tuple-element.23.refs_0_), custom_call_target="tpu_custom_call" | custom-call | flops 1 | bytes 1 | tf_op jit(solution)/shard_map/far_sums/pallas_call | solution.py:250
  10.9 0.1 collective-permute-start.5
  11.7 0.0 collective-permute-done.1.got
  11.7 4.2 %collective-permute-start.3 = (f32[24,1024]{1,0:T(8,128)S(1)}, f32[24,1024]{1,0:T(8,128)S(1)}, u32[]{:S(2)}, u32[]{:S(2)}) collective-permute-start(f32[24,1024]{1,0:T(8,128)S(1)} %get-tuple-element.27.refs_0_), channel_id=1, source_target_pairs={{0,12},{1,13},{4,8},{5,9},{8,4},{9,5},{12,0},{13,1},{2,14},{3,15},... | collective-permute-start | bytes 294920 | tf_op jit(solution)/shard_map/ppermute | solution.py:343
  15.9 0.0 collective-permute-start.4
  15.9 0.0 collective-permute-done.got.sibling
  15.9 0.1 collective-permute-start.2
  16.0 2.3 %collective-permute-done.5.got = f32[48,1024]{1,0:T(8,128)S(1)} collective-permute-done((f32[48,1024]{1,0:T(8,128)S(1)}, f32[48,1024]{1,0:T(8,128)S(1)}, u32[]{:S(2)}, u32[]{:S(2)}) %collective-permute-start.5) | collective-permute-done | bytes 196640 | tf_op jit(solution)/shard_map/ppermute | solution.py:346
  18.4 2.7 %collective-permute-start.7 = (f32[24,1024]{1,0:T(8,128)S(1)}, f32[24,1024]{1,0:T(8,128)S(1)}, u32[]{:S(2)}, u32[]{:S(2)}) collective-permute-start(f32[24,1024]{1,0:T(8,128)S(1)} %get-tuple-element.30.refs_0_), channel_id=1, source_target_pairs={{0,8},{1,9},{4,12},{5,13},{8,0},{9,1},{12,4},{13,5},{2,10},{3,11},... | collective-permute-start | bytes 294920 | tf_op jit(solution)/shard_map/ppermute | solution.py:343
  21.0 0.0 collective-permute-start.8
  21.0 0.0 copy-done.1
  21.0 0.0 copy-done.2
  21.0 0.0 copy-done.3
  21.0 3.3 %place_tiles.1 = (bf16[1024,2048]{1,0:T(8,128)(2,1)S(1)}, bf16[1024,2048]{1,0:T(8,128)(2,1)S(1)}) custom-call(s32[128]{0:T(128)S(1)} %copy-done.2, s32[128]{0:T(128)S(1)} %copy-done.3, s32[1]{0:T(128)S(6)} %copy.7.count, f32[64,8192]{1,0:T(8,128)S(1)} %copy-done.1, f32[24,1024]{1,0:T(8,128)S(1)} %get-tuple-element.30.refs_0_, ...), custom_call_target="tpu_custom_call" | custom-call | flops 10000000000 | bytes 1 | tf_op jit(solution)/shard_map/place_tiles/pallas_call | solution.py:77
  24.3 0.0 collective-permute-done.3.same
  24.3 0.0 collective-permute-done.4.other
  24.4 9.6 %collective-permute-done.2.other_lev = f32[48,2048]{1,0:T(8,128)S(1)} collective-permute-done((f32[48,2048]{1,0:T(8,128)S(1)}, f32[48,2048]{1,0:T(8,128)S(1)}, u32[]{:S(2)}, u32[]{:S(2)}) %collective-permute-start.2) | collective-permute-done | bytes 393248 | tf_op jit(solution)/shard_map/ppermute | solution.py:343
  33.9 2.6 %remap_first.1 = (f32[96,1024]{1,0:T(8,128)S(1)}, f32[24,1024]{1,0:T(8,128)S(1)}, f32[96,1024]{1,0:T(8,128)S(1)}) custom-call(f32[24,2048]{1,0:T(8,128)S(1)} %get-tuple-element.22.own, f32[48,2048]{1,0:T(8,128)S(1)} %collective-permute-done.got.sibling, f32[48,2048]{1,0:T(8,128)S(1)} %collective-permute-done.2.other_lev, ...), custom_call_target="tpu_custom_call" | custom-call | flops 1 | bytes 1 | tf_op jit(solution)/shard_map/remap_first/pallas_call | solution.py:104
  36.5 1.6 %collective-permute-start.6 = (f32[96,1024]{1,0:T(8,128)S(1)}, f32[96,1024]{1,0:T(8,128)S(1)}, u32[]{:S(2)}, u32[]{:S(2)}) collective-permute-start(f32[96,1024]{1,0:T(8,128)S(1)} %get-tuple-element.36), channel_id=1, source_target_pairs={{0,2},{2,0},{1,3},{3,1},{4,6},{6,4},{5,7},{7,5},{8,10},{10,8},{9,1... | collective-permute-start | bytes 1179656 | tf_op jit(solution)/shard_map/ppermute | solution.py:346
  38.1 0.0 collective-permute-done.7.same
  38.1 0.0 collective-permute-done.8.other
  38.1 2.6 %remap_last.1.last = f32[24,1024]{1,0:T(8,128)S(1)} custom-call(f32[24,1024]{1,0:T(8,128)S(1)} %collective-permute-done.7.same, f32[24,1024]{1,0:T(8,128)S(1)} %collective-permute-done.8.other, bf16[1024,2048]{1,0:T(8,128)(2,1)S(1)} %get-tuple-element.32.high, bf16[1024,2048]{1,0:T(8,128)(2,1)S(1)} %get-tuple-element.33.low), custom_call_target="tpu_custom_call" | custom-call | flops 10000000000 | bytes 1 | tf_op jit(solution)/shard_map/remap_last/pallas_call | solution.py:104
  40.7 0.6 %collective-permute-start.9 = (f32[24,1024]{1,0:T(8,128)S(1)}, f32[24,1024]{1,0:T(8,128)S(1)}, u32[]{:S(2)}, u32[]{:S(2)}) collective-permute-start(f32[24,1024]{1,0:T(8,128)S(1)} %remap_last.1.last), channel_id=1, source_target_pairs={{0,2},{2,0},{1,3},{3,1},{4,6},{6,4},{5,7},{7,5},{8,10},{10,8},{9,1... | collective-permute-start | bytes 294920 | tf_op jit(solution)/shard_map/ppermute | solution.py:346
  41.3 8.2 %collective-permute-done.9.got_last = f32[24,1024]{1,0:T(8,128)S(1)} collective-permute-done((f32[24,1024]{1,0:T(8,128)S(1)}, f32[24,1024]{1,0:T(8,128)S(1)}, u32[]{:S(2)}, u32[]{:S(2)}) %collective-permute-start.9) | collective-permute-done | bytes 98336 | tf_op jit(solution)/shard_map/ppermute | solution.py:346
  49.5 0.0 collective-permute-done.6.got
  49.5 0.8 %finish.1 = f32[96,1024]{1,0:T(8,128)} custom-call(f32[96,1024]{1,0:T(8,128)S(1)} %get-tuple-element.34.near_own, f32[24,1024]{1,0:T(8,128)S(1)} %get-tuple-element.35.far_own, f32[96,1024]{1,0:T(8,128)S(1)} %collective-permute-done.6.got, f32[24,1024]{1,0:T(8,128)S(1)} %remap_last.1.last, f32[24,1024]{1,0:T(8,128)S(1)} %collective-permute-done.9.got_last), custom_call_target="tpu_custom_call" | custom-call | flops 1 | bytes 1 | tf_op jit(solution)/shard_map/finish/pallas_call | solution.py:292
  (6 shorter events, 0.1 us)
Async XLA Ops:
  0.0 0.7 %copy-start = (s32[8]{0:T(128)S(1)}, s32[8]{0:T(128)}, u32[]{:S(2)}) copy-start(s32[8]{0:T(128)} %step_hour.5) | copy-start | bytes 100
  2.9 8.8 %collective-permute-start.1 = (f32[48,1024]{1,0:T(8,128)S(1)}, f32[48,1024]{1,0:T(8,128)S(1)}, u32[]{:S(2)}, u32[]{:S(2)}) collective-permute-start(f32[48,1024]{1,0:T(8,128)S(1)} %get-tuple-element.21.refs_0_), channel_id=1, source_target_pairs={{0,2},{2,0},{1,3},{3,1},{4,6},{6,4},{5,7},{7,5},{8,10},{10,8},{9,1... | collective-permute-start | bytes 589832 | tf_op jit(solution)/shard_map/ppermute | solution.py:346
  8.6 7.3 %collective-permute-start = (f32[48,2048]{1,0:T(8,128)S(1)}, f32[48,2048]{1,0:T(8,128)S(1)}, u32[]{:S(2)}, u32[]{:S(2)}) collective-permute-start(f32[48,2048]{1,0:T(8,128)S(1)} %get-tuple-element.23.refs_0_), channel_id=1, source_target_pairs={{0,1},{1,0},{4,5},{5,4},{8,9},{9,8},{12,13},{13,12},{2,3},{3,2},{6... | collective-permute-start | bytes 1179656 | tf_op jit(solution)/shard_map/ppermute | solution.py:343
  10.9 7.4 %collective-permute-start.5 = (f32[48,1024]{1,0:T(8,128)S(1)}, f32[48,1024]{1,0:T(8,128)S(1)}, u32[]{:S(2)}, u32[]{:S(2)}) collective-permute-start(f32[48,1024]{1,0:T(8,128)S(1)} %get-tuple-element.26.refs_0_), channel_id=1, source_target_pairs={{0,2},{2,0},{1,3},{3,1},{4,6},{6,4},{5,7},{7,5},{8,10},{10,8},{9,1... | collective-permute-start | bytes 589832 | tf_op jit(solution)/shard_map/ppermute | solution.py:346
  11.7 12.6 %collective-permute-start.3 = (f32[24,1024]{1,0:T(8,128)S(1)}, f32[24,1024]{1,0:T(8,128)S(1)}, u32[]{:S(2)}, u32[]{:S(2)}) collective-permute-start(f32[24,1024]{1,0:T(8,128)S(1)} %get-tuple-element.27.refs_0_), channel_id=1, source_target_pairs={{0,12},{1,13},{4,8},{5,9},{8,4},{9,5},{12,0},{13,1},{2,14},{3,15},... | collective-permute-start | bytes 294920 | tf_op jit(solution)/shard_map/ppermute | solution.py:343
  15.9 8.4 %collective-permute-start.4 = (f32[24,1024]{1,0:T(8,128)S(1)}, f32[24,1024]{1,0:T(8,128)S(1)}, u32[]{:S(2)}, u32[]{:S(2)}) collective-permute-start(f32[24,1024]{1,0:T(8,128)S(1)} %get-tuple-element.28.refs_1_), channel_id=1, source_target_pairs={{0,13},{1,12},{4,9},{5,8},{8,5},{9,4},{12,1},{13,0},{2,15},{3,14},... | collective-permute-start | bytes 294920 | tf_op jit(solution)/shard_map/ppermute | solution.py:343
  15.9 18.0 %collective-permute-start.2 = (f32[48,2048]{1,0:T(8,128)S(1)}, f32[48,2048]{1,0:T(8,128)S(1)}, u32[]{:S(2)}, u32[]{:S(2)}) collective-permute-start(f32[48,2048]{1,0:T(8,128)S(1)} %join.1.refs_0_), channel_id=1, source_target_pairs={{0,4},{1,5},{4,0},{5,1},{8,12},{9,13},{12,8},{13,9},{2,6},{3,7},{6... | collective-permute-start | bytes 1179656 | tf_op jit(solution)/shard_map/ppermute | solution.py:343
  18.3 2.7 %copy-start.1 = (f32[64,8192]{1,0:T(8,128)S(1)}, f32[64,8192]{1,0:T(8,128)}, u32[]{:S(2)}) copy-start(f32[64,8192]{1,0:T(8,128)} %weights.1) | copy-start | bytes 6291460
  18.3 2.7 %copy-start.2 = (s32[128]{0:T(128)S(1)}, s32[128]{0:T(128)}, u32[]{:S(2)}) copy-start(s32[128]{0:T(128)} %rows.1) | copy-start | bytes 1540
  18.3 2.7 %copy-start.3 = (s32[128]{0:T(128)S(1)}, s32[128]{0:T(128)}, u32[]{:S(2)}) copy-start(s32[128]{0:T(128)} %columns.1) | copy-start | bytes 1540
  18.4 19.8 %collective-permute-start.7 = (f32[24,1024]{1,0:T(8,128)S(1)}, f32[24,1024]{1,0:T(8,128)S(1)}, u32[]{:S(2)}, u32[]{:S(2)}) collective-permute-start(f32[24,1024]{1,0:T(8,128)S(1)} %get-tuple-element.30.refs_0_), channel_id=1, source_target_pairs={{0,8},{1,9},{4,12},{5,13},{8,0},{9,1},{12,4},{13,5},{2,10},{3,11},... | collective-permute-start | bytes 294920 | tf_op jit(solution)/shard_map/ppermute | solution.py:343
  21.0 17.1 %collective-permute-start.8 = (f32[24,1024]{1,0:T(8,128)S(1)}, f32[24,1024]{1,0:T(8,128)S(1)}, u32[]{:S(2)}, u32[]{:S(2)}) collective-permute-start(f32[24,1024]{1,0:T(8,128)S(1)} %get-tuple-element.31.refs_1_), channel_id=1, source_target_pairs={{0,9},{1,8},{4,13},{5,12},{8,1},{9,0},{12,5},{13,4},{2,11},{3,10},... | collective-permute-start | bytes 294920 | tf_op jit(solution)/shard_map/ppermute | solution.py:343
  36.5 12.9 %collective-permute-start.6 = (f32[96,1024]{1,0:T(8,128)S(1)}, f32[96,1024]{1,0:T(8,128)S(1)}, u32[]{:S(2)}, u32[]{:S(2)}) collective-permute-start(f32[96,1024]{1,0:T(8,128)S(1)} %get-tuple-element.36), channel_id=1, source_target_pairs={{0,2},{2,0},{1,3},{3,1},{4,6},{6,4},{5,7},{7,5},{8,10},{10,8},{9,1... | collective-permute-start | bytes 1179656 | tf_op jit(solution)/shard_map/ppermute | solution.py:346
  40.7 8.8 %collective-permute-start.9 = (f32[24,1024]{1,0:T(8,128)S(1)}, f32[24,1024]{1,0:T(8,128)S(1)}, u32[]{:S(2)}, u32[]{:S(2)}) collective-permute-start(f32[24,1024]{1,0:T(8,128)S(1)} %remap_last.1.last), channel_id=1, source_target_pairs={{0,2},{2,0},{1,3},{3,1},{4,6},{6,4},{5,7},{7,5},{8,10},{10,8},{9,1... | collective-permute-start | bytes 294920 | tf_op jit(solution)/shard_map/ppermute | solution.py:346

commit v3 on v2

v3 whole, which is shorter than its diff:
```python
import functools

import jax
import jax.numpy as jnp
from jax import lax
from jax.experimental import pallas as pl
from jax.experimental.pallas import tpu as pltpu
from jax.sharding import PartitionSpec as P

TILE = 64
HOURS = 2
CT_DEV = 32
PT_DEV = 16
SLOTS = 128
CELLS_DEV = CT_DEV * TILE
PIXELS_DEV = PT_DEV * TILE
LANES = 2 * TILE
MIB = 1 << 20

LIGHT = pl.CostEstimate(flops=1, bytes_accessed=1, transcendentals=0)
HEAVY = pl.CostEstimate(flops=10_000_000_000, bytes_accessed=1, transcendentals=0)

NT = (((1,), (1,)), ((), ()))
NN = (((1,), (0,)), ((), ()))


def split(x):
    high = x.astype(jnp.bfloat16)
    return high, (x - high.astype(jnp.float32)).astype(jnp.bfloat16)


def dot(a, b, dims):
    return lax.dot_general(a, b, dims, preferred_element_type=jnp.float32)


GROUP = 8


def place_kernel(rows, columns, count, weights, *refs):
    held, high, low, passed, total = refs
    band = 128
    passed[...] = held[...]

    @pl.loop(0, PIXELS_DEV // band)
    def _(b):
        total[pl.ds(pl.multiple_of(b * band, band), band), :] = jnp.zeros((band, CELLS_DEV), jnp.float32)

    lane_half = lax.broadcasted_iota(jnp.int32, (TILE, LANES), 1) // TILE
    live = count[0]

    @pl.loop(0, (live + GROUP - 1) // GROUP)
    def _(g):
        for pair in range(GROUP // 2):
            lanes = pl.ds(pl.multiple_of((g * (GROUP // 2) + pair) * LANES, LANES), LANES)
            tiles = weights[:, lanes]
            turned = pltpu.roll(tiles, TILE, 1)
            for i in range(2):
                k = g * GROUP + pair * 2 + i
                row, column = rows[k], columns[k]
                side = jnp.where(k < live, column & 1, -1)
                tile = jnp.where(lane_half == i, tiles, turned)
                at = (
                    pl.ds(pl.multiple_of(row * TILE, TILE), TILE),
                    pl.ds(pl.multiple_of((column >> 1) * LANES, LANES), LANES),
                )
                total[at] = total[at] + jnp.where(lane_half == side, tile, 0.0)

    @pl.loop(0, PIXELS_DEV // band)
    def _(b):
        at = pl.ds(pl.multiple_of(b * band, band), band)
        high[at, :], low[at, :] = split(total[at, :])


def place_tiles(rows, columns, count, weights, held):
    smem = pl.BlockSpec(memory_space=pltpu.SMEM)
    vmem = pl.BlockSpec(memory_space=pltpu.VMEM)
    half = jax.ShapeDtypeStruct((PIXELS_DEV, CELLS_DEV), jnp.bfloat16)
    return pl.pallas_call(
        place_kernel,
        out_shape=(half, half, jax.ShapeDtypeStruct(held.shape, held.dtype)),
        in_specs=[smem, smem, smem, vmem, vmem],
        out_specs=(vmem, vmem, vmem),
        scratch_shapes=[pltpu.VMEM((PIXELS_DEV, CELLS_DEV), jnp.float32)],
        compiler_params=pltpu.CompilerParams(vmem_limit_bytes=28 * MIB),
        cost_estimate=HEAVY,
        name="place_tiles",
    )(rows, columns, count, weights, held)


PIXEL_BLOCK = 256


def remap_blocks(x, high, low):
    m = x.shape[0]
    x_high, x_low = split(x)
    both = jnp.concatenate([x_high, x_low], axis=0)
    for start in range(0, PIXELS_DEV, PIXEL_BLOCK):
        at = slice(start, start + PIXEL_BLOCK)
        first = dot(both, high[at, :], NT)
        yield at, first[:m] + first[m:] + dot(x_high, low[at, :], NT)


def remap_call(kernel, inputs, after, out_rows, high, low, cost, name):
    vmem = pl.BlockSpec(memory_space=pltpu.VMEM)
    return pl.pallas_call(
        kernel,
        out_shape=[jax.ShapeDtypeStruct((rows, PIXELS_DEV), jnp.float32) for rows in out_rows],
        in_specs=[vmem] * (len(inputs) + 2) + [pl.BlockSpec(memory_space=pl.ANY)] * len(after),
        out_specs=[vmem] * len(out_rows),
        compiler_params=pltpu.CompilerParams(vmem_limit_bytes=24 * MIB),
        cost_estimate=cost,
        name=name,
    )(*inputs, high, low, *after)


def remap_rows_kernel(x, high, low, out):
    for at, result in remap_blocks(x[...], high, low):
        out[:, at] = result


def far_rows(same_sub, other_sub):
    even = lax.axis_index("sub") == 0
    levels = same_sub.shape[0] // 2
    blocks = [jnp.where(even, same_sub, other_sub), jnp.where(even, other_sub, same_sub)]
    return [jnp.concatenate([block[:levels], block[levels:]], axis=1) for block in blocks]


def keeps_near():
    return lax.axis_index("tm") == lax.axis_index("lev") // 2


def near_rows(same_sub, other_sub):
    even = lax.axis_index("sub") == 0
    return [jnp.where(even, same_sub, other_sub), jnp.where(even, other_sub, same_sub)]


def by_hour(result, levels):
    pieces = [result[start : start + levels] for start in range(0, 2 * HOURS * levels, levels)]
    return jnp.concatenate([pieces[sub * HOURS + hour] for hour in range(HOURS) for sub in range(2)], axis=0)


def remap_chip_kernel(own, sibling, high, low, *refs):
    out = refs[-1]
    x = jnp.concatenate(near_rows(own[...], sibling[...]), axis=0)
    for at, result in remap_blocks(x, high, low):
        out[:, at] = by_hour(result, own.shape[0] // HOURS)


def remap_first_kernel(near_same, near_other, same, other, high, low, *refs):
    near_out, far_out, send = refs[-3:]
    levels = near_same.shape[0] // HOURS
    rows = 2 * HOURS * levels
    blocks = near_rows(near_same[...], near_other[...]) + far_rows(same[...], other[...])
    for at, result in remap_blocks(jnp.concatenate(blocks, axis=0), high, low):
        near_out[:, at] = by_hour(result, levels)
        far_out[:, at] = result[rows:]
    near = keeps_near()
    half = far_out.shape[0]

    @pl.when(near)
    def _():
        send[:half] = far_out[...]
        send[half:] = jnp.zeros((send.shape[0] - half, PIXELS_DEV), jnp.float32)

    @pl.when(jnp.logical_not(near))
    def _():
        send[...] = near_out[...]


def remap_last_kernel(same, other, high, low, *refs):
    out = refs[-1]
    x = jnp.concatenate(far_rows(same[...], other[...]), axis=0)
    for at, result in remap_blocks(x, high, low):
        out[:, at] = result


def hour_matrix(step_hour, levels, steps, hours, cuts):
    rows, columns = cuts * levels, cuts * 2 * levels * steps
    row = lax.broadcasted_iota(jnp.int32, (rows, columns), 0)
    column = lax.broadcasted_iota(jnp.int32, (rows, columns), 1)
    span = levels * steps
    near = jnp.full((rows, columns), -1, jnp.int32)
    for cut in range(cuts):
        for half in range(2):
            step = column - (cut * 2 + half) * span - (row - cut * levels) * steps
            inside = (row >= cut * levels) & (row < (cut + 1) * levels)
            inside = inside & (step >= 0) & (step < steps)
            near = jnp.where(inside, step, near)
    blocks = []
    for hour in hours:
        block = jnp.zeros((rows, columns), jnp.float32)
        for step in range(steps):
            block = jnp.where(near == step, jnp.where(step_hour[step] == hour, 1.0, 0.0), block)
        blocks.append(block)
    return jnp.concatenate(blocks, axis=0).astype(jnp.bfloat16)


def peer_shard(k, j):
    subs = lax.axis_size("sub")
    return (lax.axis_index("lev") ^ k) * subs + (lax.axis_index("sub") ^ j)


def field_copies(field, buffer, arrived, peers):
    copies = []
    for place, (k, j) in enumerate(peers):
        start = pl.multiple_of(peer_shard(k, j) * CELLS_DEV, CELLS_DEV)
        copy = pltpu.make_async_copy(
            field.at[:, :, pl.ds(start, CELLS_DEV)], buffer.at[place], arrived.at[place]
        )
        copy.start()
        copies.append(copy)
    return copies


def sums_kernel(near_peers, far_peers, step_hour, field, *refs):
    buffer, arrived = refs[-2:]
    near = refs[: len(near_peers)]
    theirs, mine = refs[len(near_peers) : -2 : 2], refs[len(near_peers) + 1 : -2 : 2]
    _, levels, steps, cells = buffer.shape
    peers = [*sum(far_peers, []), *near_peers]
    copies = field_copies(field, buffer, arrived, peers)
    me = lax.axis_index("tm")
    matrix = hour_matrix(step_hour, levels, steps, (1 - me, me), 2)
    rows, cut = 2 * levels, cells // 2
    place = 0
    for chunk, members in enumerate(far_peers):
        for j in range(len(members)):
            copies[place].wait()
            high, low = split(buffer[place].reshape(levels * steps, cells))
            halves = [high[:, :cut], low[:, :cut], high[:, cut:], low[:, cut:]]
            result = dot(matrix, jnp.concatenate(halves, axis=0), NN)
            theirs[chunk][j * rows : (j + 1) * rows] = result[:rows]
            mine[chunk][j * rows : (j + 1) * rows] = result[rows:]
            place += 1
    matrix = hour_matrix(step_hour, levels, steps, range(HOURS), 1)
    for out in near:
        copies[place].wait()
        x = buffer[place].reshape(levels * steps, cells)
        out[...] = dot(matrix, jnp.concatenate(split(x), axis=0), NN)
        place += 1


def hour_sums(near_peers, far_peers, step_hour, field):
    levels, steps, _ = field.shape
    vmem = pl.BlockSpec(memory_space=pltpu.VMEM)
    shapes = [(HOURS * levels, CELLS_DEV)] * len(near_peers)
    for members in far_peers:
        shapes += [(len(members) * 2 * levels, CELLS_DEV // 2)] * 2
    count = len(near_peers) + sum(map(len, far_peers))
    outs = pl.pallas_call(
        functools.partial(sums_kernel, near_peers, far_peers),
        out_shape=[jax.ShapeDtypeStruct(shape, jnp.float32) for shape in shapes],
        in_specs=[pl.BlockSpec(memory_space=pltpu.SMEM), pl.BlockSpec(memory_space=pl.ANY)],
        out_specs=[vmem] * len(shapes),
        scratch_shapes=[
            pltpu.VMEM((count, levels, steps, CELLS_DEV), jnp.float32),
            pltpu.SemaphoreType.DMA((count,)),
        ],
        compiler_params=pltpu.CompilerParams(vmem_limit_bytes=52 * MIB),
        cost_estimate=LIGHT,
        name="hour_sums",
    )(step_hour, field)
    far = outs[len(near_peers) :]
    return outs[: len(near_peers)], list(zip(far[::2], far[1::2]))


def merge_kernel(mine, got, *refs):
    outs = refs[-2:]
    rows = outs[0].shape[0]
    for place, out in enumerate(outs):
        at = slice(place * rows, (place + 1) * rows)
        out[...] = mine[at] + got[at]


def small_call(kernel, inputs, after, shapes, cost, name):
    vmem = pl.BlockSpec(memory_space=pltpu.VMEM)
    return pl.pallas_call(
        kernel,
        out_shape=[jax.ShapeDtypeStruct(shape, jnp.float32) for shape in shapes],
        in_specs=[vmem] * len(inputs) + [pl.BlockSpec(memory_space=pl.ANY)] * len(after),
        out_specs=[vmem] * len(shapes),
        compiler_params=pltpu.CompilerParams(vmem_limit_bytes=8 * MIB),
        cost_estimate=cost,
        name=name,
    )(*inputs, *after)


def merge(mine, got, *after):
    shape = (mine.shape[0] // 2, mine.shape[1])
    return small_call(merge_kernel, [mine, got], after, [shape, shape], HEAVY, "merge")


def finish_kernel(divisor, chip, got_chip, near_own, far_own, got, last, got_last, out):
    me, lev = lax.axis_index("tm"), lax.axis_index("lev") % 2
    rows = far_own.shape[0]
    near = keeps_near()
    for hour in range(HOURS):
        first_at = pl.ds(pl.multiple_of((hour * 2 + 1 - lev) * rows, rows), rows)
        last_at = pl.ds(pl.multiple_of((hour * 2 + lev) * rows, rows), rows)
        here = slice(hour * rows, (hour + 1) * rows)

        @pl.when(near)
        def _():
            out[first_at, :] = (near_own[here] + got[here]) / divisor
            out[last_at, :] = (chip[here] + got_chip[here]) / divisor

        @pl.when(jnp.logical_not(near))
        def _():
            out[first_at, :] = jnp.where(me == hour, far_own[...], got[:rows]) / divisor
            out[last_at, :] = jnp.where(me == hour, last[...], got_last[...]) / divisor


def finish(arrays, divisor):
    call = functools.partial(finish_kernel, divisor)
    shape = (2 * arrays[0].shape[0], PIXELS_DEV)
    return small_call(call, arrays, [], [shape], LIGHT, "finish")[0]


def hour_plan(level_field, tile_weight, tile_rows, tile_columns, live_count, step_hour):
    levs, subs, shards_tm = lax.axis_size("lev"), lax.axis_size("sub"), lax.axis_size("tm")
    half = levs // 2
    divisor = float(level_field.shape[0] * shards_tm // HOURS)
    field = jnp.transpose(level_field, (1, 0, 2))

    def to_peer(x, k, j):
        pairs = [(a * subs + b, (a ^ k) * subs + (b ^ j)) for a in range(levs) for b in range(subs)]
        return lax.ppermute(x, ("lev", "sub"), pairs)

    def swap(x):
        return lax.ppermute(x, "tm", [(0, 1), (1, 0)])

    near_peers = [(1, 0), (1, 1), (0, 1), (0, 0)]
    far_peers = [[(k, j) for j in range(subs)] for k in (half + 1, half)]
    near, ((theirs_a, mine_a), (theirs_b, mine_b)) = hour_sums(near_peers, far_peers, step_hour, field)
    got_a = swap(theirs_a)
    near = [to_peer(x, k, j) for x, (k, j) in list(zip(near, near_peers))[:-1]] + [near[-1]]
    near_same, near_other, sibling, own = near
    high, low, theirs_b = place_tiles(tile_rows, tile_columns, live_count, tile_weight, theirs_b)
    got_b = swap(theirs_b)
    merged_a = merge(mine_a, got_a, sibling, high)
    far_a = [to_peer(x, *peer) for x, peer in zip(merged_a, far_peers[0])]

    rows = mine_a.shape[0] // subs
    (chip,) = remap_call(
        remap_chip_kernel, [own, sibling], merged_a, [2 * rows], high, low, HEAVY, "remap_chip"
    )
    got_chip = swap(chip)
    merged_b = merge(mine_b, got_b, near_same, near_other, chip)
    far_b = [to_peer(x, *peer) for x, peer in zip(merged_b, far_peers[1])]
    near_out, far_out, send = remap_call(
        remap_first_kernel,
        [near_same, near_other, *far_a],
        merged_b,
        [2 * rows, rows, 2 * rows],
        high,
        low,
        HEAVY,
        "remap_first",
    )
    got = swap(send)
    (last,) = remap_call(remap_last_kernel, far_b, [send], [rows], high, low, HEAVY, "remap_last")
    got_last = swap(last)
    out = finish([chip, got_chip, near_out, far_out, got, last, got_last], divisor)
    return out.reshape(HOURS, out.shape[0] // HOURS, PIXELS_DEV)


def general_plan(level_field, tile_weight, tile_rows, tile_columns, live_count, step_hour):
    steps, levels, cells = level_field.shape
    shards = lax.axis_size("lev") * lax.axis_size("sub")
    divisor = float(steps * lax.axis_size("tm") // HOURS)
    hours = jnp.arange(HOURS, dtype=jnp.int32)
    table = (step_hour[None, :] == hours[:, None]).astype(jnp.float32)
    fields = level_field.reshape(steps, levels, shards, cells // shards)
    partial = jnp.einsum("hs,slgc->ghlc", table, fields, precision=lax.Precision.HIGHEST)
    regrouped = lax.all_to_all(partial, ("lev", "sub"), split_axis=0, concat_axis=0, tiled=True)
    rows = jnp.transpose(regrouped, (1, 0, 2, 3)).reshape(-1, cells // shards)
    high, low, rows = place_tiles(tile_rows, tile_columns, live_count, tile_weight, rows)
    (out,) = remap_call(remap_rows_kernel, [rows], [], [rows.shape[0]], high, low, LIGHT, "remap_rows")
    out = out.reshape(HOURS, shards * levels, PIXELS_DEV) / divisor
    return lax.psum_scatter(out, "tm", scatter_dimension=1, tiled=True)


def solution(mesh):
    sizes = mesh.shape
    paired = sizes["tm"] == HOURS and sizes["lev"] == 4 and sizes["sub"] == 2
    placed = (
        P(("groups", "tm"), ("lev", "sub"), None),
        P(None, ("lev", "sub")),
        P(("lev", "sub")),
        P(("lev", "sub")),
        P(("lev", "sub")),
        P("tm"),
    )
    return jax.shard_map(
        hour_plan if paired else general_plan,
        mesh=mesh,
        in_specs=placed,
        out_specs=P("groups", "tm", ("lev", "sub")),
        check_vma=False,
    )
```

time: 50.5 us -> 43.6 us (0.86)
  waiting for transfers between devices: 20.1 us -> 9.71 us
  starting transfers between devices: 12.2 us -> 16.8 us
  Pallas kernels: 16.6 us -> 15.5 us
    ppermute x4 -> x5, waiting for transfers between devices: 10.5 us -> 3.74 us  [swap(): return lax.ppermute(x, 'tm', [(0, 1), (1, 0)])]
    pallas_call x4 -> x2, Pallas kernels: 10.5 us -> 6.71 us  [the longest x1 3.91 us: hour_sums(): pl.pallas_call(functools.partial(sums_kernel, near_peers, far_peers), out...]
    ppermute x6 -> x7, waiting for transfers between devices: 9.59 us -> 5.97 us  [to_peer(): return lax.ppermute(x, ('lev', 'sub'), pairs)]
    pallas_call x2 -> x3, Pallas kernels: 5.2 us -> 7.95 us  [remap_call(): pl.pallas_call(kernel, out_shape=[jax.ShapeDtypeStruct((rows, PIXELS_DEV)...]
    ppermute x4 -> x5, starting transfers between devices: 5.24 us -> 7.86 us  [swap(): return lax.ppermute(x, 'tm', [(0, 1), (1, 0)])]
    ppermute x6 -> x7, starting transfers between devices: 6.98 us -> 8.96 us  [to_peer(): return lax.ppermute(x, ('lev', 'sub'), pairs)]
  transfers between devices with their start and end apart: 10 -> 12, of which waited for: 3 -> 4; matrix products, arithmetic and copies ran while one was open for 0% -> 0% of each run, Pallas kernels for 27% -> 25%
where the time goes in v3:
time: 43.6 us; the launch traced here: 43.5 us
  starting transfers between devices  16.8 us (39%)
  Pallas kernels  15.5 us (36%)
  waiting for transfers between devices  9.71 us (22%)
  between operations  0.75 us (2%)
  local copies, waits for them, and re-layouts  0.69 us (2%)
    ppermute x7, starting transfers between devices, to_peer(): return lax.ppermute(x, ('lev', 'sub'), pairs)  8.96 us
    pallas_call x3, Pallas kernels, remap_call(): pl.pallas_call(kernel, out_shape=[jax.ShapeDtypeStruct((rows, PIXELS_DEV)...  7.95 us
    ppermute x5, starting transfers between devices, swap(): return lax.ppermute(x, 'tm', [(0, 1), (1, 0)])  7.86 us
    ppermute x7, waiting for transfers between devices, to_peer(): return lax.ppermute(x, ('lev', 'sub'), pairs)  5.97 us
    pallas_call x1, Pallas kernels, hour_sums(): pl.pallas_call(functools.partial(sums_kernel, near_peers, far_peers), out...  3.91 us
    ppermute x5, waiting for transfers between devices, swap(): return lax.ppermute(x, 'tm', [(0, 1), (1, 0)])  3.74 us
    pallas_call x1, Pallas kernels, place_tiles(): pl.pallas_call(place_kernel, out_shape=(half, half, jax.ShapeDtypeStruct(...  2.8 us
  transfers between devices with their start and end apart: 12, of which 4 were waited for; matrix products, arithmetic and copies ran while one was open for 0% of the time, Pallas kernels for 25%

profile of v3, /device:TPU:0, one launch (start us, length us, event | category | flops | bytes accessed | tf_op | source)
XLA Modules:
  0.0 43.5 jit_solution(13551252655471104507)
XLA Ops:
  0.0 0.7 %copy-done = s32[8]{0:T(128)S(1)} copy-done((s32[8]{0:T(128)S(1)}, s32[8]{0:T(128)}, u32[]{:S(2)}) %copy-start) | copy-done | bytes 56
  0.7 3.9 %hour_sums.1 = (f32[24,2048]{1,0:T(8,128)S(1)}, f32[24,2048]{1,0:T(8,128)S(1)}, f32[24,2048]{1,0:T(8,128)S(1)}, f32[24,2048]{1,0:T(8,128)S(1)}, f32[48,1024]{1,0...) custom-call(s32[8]{0:T(128)S(1)} %copy-done, f32[12,8,16384]{2,1,0:T(8,128)} %bitcast.2), custom_call_target="tpu_custom_call" | custom-call | flops 1 | bytes 1 | tf_op jit(solution)/shard_map/hour_sums/pallas_call | solution.py:250
  4.6 0.5 %collective-permute-start = (f32[24,2048]{1,0:T(8,128)S(1)}, f32[24,2048]{1,0:T(8,128)S(1)}, u32[]{:S(2)}, u32[]{:S(2)}) collective-permute-start(f32[24,2048]{1,0:T(8,128)S(1)} %get-tuple-element.24), channel_id=1, source_target_pairs={{0,1},{1,0},{4,5},{5,4},{8,9},{9,8},{12,13},{13,12},{2,3},{3,2},{6... | collective-permute-start | bytes 589832 | tf_op jit(solution)/shard_map/ppermute | solution.py:327
  5.1 2.6 %collective-permute-start.1 = (f32[48,1024]{1,0:T(8,128)S(1)}, f32[48,1024]{1,0:T(8,128)S(1)}, u32[]{:S(2)}, u32[]{:S(2)}) collective-permute-start(f32[48,1024]{1,0:T(8,128)S(1)} %get-tuple-element.29), channel_id=1, source_target_pairs={{0,2},{2,0},{1,3},{3,1},{4,6},{6,4},{5,7},{7,5},{8,10},{10,8},{9,1... | collective-permute-start | bytes 589832 | tf_op jit(solution)/shard_map/ppermute | solution.py:330
  7.7 1.6 %collective-permute-start.3 = (f32[24,2048]{1,0:T(8,128)S(1)}, f32[24,2048]{1,0:T(8,128)S(1)}, u32[]{:S(2)}, u32[]{:S(2)}) collective-permute-start(f32[24,2048]{1,0:T(8,128)S(1)} %get-tuple-element.32), channel_id=1, source_target_pairs={{0,4},{1,5},{4,0},{5,1},{8,12},{9,13},{12,8},{13,9},{2,6},{3,7},{6... | collective-permute-start | bytes 589832 | tf_op jit(solution)/shard_map/ppermute | solution.py:327
  9.3 0.0 collective-permute-start.4
  9.9 0.0 copy-done.3
  10.0 2.8 %place_tiles.1 = (bf16[1024,2048]{1,0:T(8,128)(2,1)S(1)}, bf16[1024,2048]{1,0:T(8,128)(2,1)S(1)}, f32[48,1024]{1,0:T(8,128)S(1)}) custom-call(s32[128]{0:T(128)S(1)} %copy-done.2, s32[128]{0:T(128)S(1)} %copy-done.3, s32[1]{0:T(128)S(6)} %copy.7.count, f32[64,8192]{1,0:T(8,128)S(1)} %copy-done.1, f32[48,1024]{1,0:T(8,128)S(1)} %get-tuple-element.25.refs_0_), custom_call_target="tpu_custom_call" | custom-call | flops 10000000000 | bytes 1 | tf_op jit(solution)/shard_map/place_tiles/pallas_call | solution.py:78
  12.8 0.6 %collective-permute-start.7 = (f32[48,1024]{1,0:T(8,128)S(1)}, f32[48,1024]{1,0:T(8,128)S(1)}, u32[]{:S(2)}, u32[]{:S(2)}) collective-permute-start(f32[48,1024]{1,0:T(8,128)S(1)} %get-tuple-element.35), channel_id=1, source_target_pairs={{0,2},{2,0},{1,3},{3,1},{4,6},{6,4},{5,7},{7,5},{8,10},{10,8},{9,1... | collective-permute-start | bytes 589832 | tf_op jit(solution)/shard_map/ppermute | solution.py:330
  13.4 0.0 collective-permute-done.refs_0_.sibling
  13.4 0.0 collective-permute-done.1.got
  13.4 4.6 %collective-permute-start.5 = (f32[24,1024]{1,0:T(8,128)S(1)}, f32[24,1024]{1,0:T(8,128)S(1)}, u32[]{:S(2)}, u32[]{:S(2)}) collective-permute-start(f32[24,1024]{1,0:T(8,128)S(1)} %get-tuple-element.30.refs_0_), channel_id=1, source_target_pairs={{0,12},{1,13},{4,8},{5,9},{8,4},{9,5},{12,0},{13,1},{2,14},{3,15},... | collective-permute-start | bytes 294920 | tf_op jit(solution)/shard_map/ppermute | solution.py:327
  18.0 0.0 collective-permute-start.6
  18.0 2.6 %remap_chip.1.refs_2_.chip = f32[48,1024]{1,0:T(8,128)S(1)} custom-call(f32[24,2048]{1,0:T(8,128)S(1)} %get-tuple-element.23.own, f32[24,2048]{1,0:T(8,128)S(1)} %collective-permute-done.refs_0_.sibling, bf16[1024,2048]{1,0:T(8,128)(2,1)S(1)} %get-tuple-element.26.refs_1_.high, bf16[1024,2048]{1,0:T(8,128)(2,1)S(1)} %get-tuple-element.27.low, ...), custom_call_target="tpu_custom_call" | custom-call | flops 10000000000 | bytes 1 | tf_op jit(solution)/shard_map/remap_chip/pallas_call | solution.py:105
  20.7 0.0 collective-permute-done.3.refs_0_.near_same
  20.7 1.6 %collective-permute-start.2 = (f32[48,1024]{1,0:T(8,128)S(1)}, f32[48,1024]{1,0:T(8,128)S(1)}, u32[]{:S(2)}, u32[]{:S(2)}) collective-permute-start(f32[48,1024]{1,0:T(8,128)S(1)} %remap_chip.1.refs_2_.chip), channel_id=1, source_target_pairs={{0,2},{2,0},{1,3},{3,1},{4,6},{6,4},{5,7},{7,5},{8,10},{10,8},{9,1... | collective-permute-start | bytes 589832 | tf_op jit(solution)/shard_map/ppermute | solution.py:330
  22.2 0.0 collective-permute-done.4.refs_1_.near_other
  22.2 0.0 collective-permute-done.7.got
  22.3 1.4 %collective-permute-start.9 = (f32[24,1024]{1,0:T(8,128)S(1)}, f32[24,1024]{1,0:T(8,128)S(1)}, u32[]{:S(2)}, u32[]{:S(2)}) collective-permute-start(f32[24,1024]{1,0:T(8,128)S(1)} %get-tuple-element.36.refs_0_), channel_id=1, source_target_pairs={{0,8},{1,9},{4,12},{5,13},{8,0},{9,1},{12,4},{13,5},{2,10},{3,11},... | collective-permute-start | bytes 294920 | tf_op jit(solution)/shard_map/ppermute | solution.py:327
  23.7 0.8 %collective-permute-start.10 = (f32[24,1024]{1,0:T(8,128)S(1)}, f32[24,1024]{1,0:T(8,128)S(1)}, u32[]{:S(2)}, u32[]{:S(2)}) collective-permute-start(f32[24,1024]{1,0:T(8,128)S(1)} %get-tuple-element.37.refs_1_), channel_id=1, source_target_pairs={{0,9},{1,8},{4,13},{5,12},{8,1},{9,0},{12,5},{13,4},{2,11},{3,10},... | collective-permute-start | bytes 294920 | tf_op jit(solution)/shard_map/ppermute | solution.py:327
  24.5 0.0 collective-permute-done.5.same
  24.5 0.5 %collective-permute-done.6.other = f32[24,1024]{1,0:T(8,128)S(1)} collective-permute-done((f32[24,1024]{1,0:T(8,128)S(1)}, f32[24,1024]{1,0:T(8,128)S(1)}, u32[]{:S(2)}, u32[]{:S(2)}) %collective-permute-start.6) | collective-permute-done | bytes 98336 | tf_op jit(solution)/shard_map/ppermute | solution.py:327
  25.0 2.7 %remap_first.1 = (f32[48,1024]{1,0:T(8,128)S(1)}, f32[24,1024]{1,0:T(8,128)S(1)}, f32[48,1024]{1,0:T(8,128)S(1)}) custom-call(f32[24,2048]{1,0:T(8,128)S(1)} %collective-permute-done.3.refs_0_.near_same, f32[24,2048]{1,0:T(8,128)S(1)} %collective-permute-done.4.refs_1_.near_other, f32[24,1024]{1,0:T(8,128)S(1)} %collective-permute-done.5.same, ...), custom_call_target="tpu_custom_call" | custom-call | flops 10000000000 | bytes 1 | tf_op jit(solution)/shard_map/remap_first/pallas_call | solution.py:105
  27.8 1.4 %collective-permute-start.8 = (f32[48,1024]{1,0:T(8,128)S(1)}, f32[48,1024]{1,0:T(8,128)S(1)}, u32[]{:S(2)}, u32[]{:S(2)}) collective-permute-start(f32[48,1024]{1,0:T(8,128)S(1)} %get-tuple-element.40.refs_0_), channel_id=1, source_target_pairs={{0,2},{2,0},{1,3},{3,1},{4,6},{6,4},{5,7},{7,5},{8,10},{10,8},{9,1... | collective-permute-start | bytes 589832 | tf_op jit(solution)/shard_map/ppermute | solution.py:330
  29.2 5.1 %collective-permute-done.9.same = f32[24,1024]{1,0:T(8,128)S(1)} collective-permute-done((f32[24,1024]{1,0:T(8,128)S(1)}, f32[24,1024]{1,0:T(8,128)S(1)}, u32[]{:S(2)}, u32[]{:S(2)}) %collective-permute-start.9) | collective-permute-done | bytes 98336 | tf_op jit(solution)/shard_map/ppermute | solution.py:327
  34.3 0.3 collective-permute-done.10.other
  34.6 2.6 %remap_last.1.last = f32[24,1024]{1,0:T(8,128)S(1)} custom-call(f32[24,1024]{1,0:T(8,128)S(1)} %collective-permute-done.9.same, f32[24,1024]{1,0:T(8,128)S(1)} %collective-permute-done.10.other, bf16[1024,2048]{1,0:T(8,128)(2,1)S(1)} %get-tuple-element.26.refs_1_.high, bf16[1024,2048]{1,0:T(8,128)(2,1)S(1)} %get-tuple-element.27.low, ...), custom_call_target="tpu_custom_call" | custom-call | flops 10000000000 | bytes 1 | tf_op jit(solution)/shard_map/remap_last/pallas_call | solution.py:105
  37.2 1.7 %collective-permute-start.11 = (f32[24,1024]{1,0:T(8,128)S(1)}, f32[24,1024]{1,0:T(8,128)S(1)}, u32[]{:S(2)}, u32[]{:S(2)}) collective-permute-start(f32[24,1024]{1,0:T(8,128)S(1)} %remap_last.1.last), channel_id=1, source_target_pairs={{0,2},{2,0},{1,3},{3,1},{4,6},{6,4},{5,7},{7,5},{8,10},{10,8},{9,1... | collective-permute-start | bytes 294920 | tf_op jit(solution)/shard_map/ppermute | solution.py:330
  38.9 0.0 collective-permute-done.2.got_chip
  38.9 3.7 %collective-permute-done.11.got_last = f32[24,1024]{1,0:T(8,128)S(1)} collective-permute-done((f32[24,1024]{1,0:T(8,128)S(1)}, f32[24,1024]{1,0:T(8,128)S(1)}, u32[]{:S(2)}, u32[]{:S(2)}) %collective-permute-start.11) | collective-permute-done | bytes 98336 | tf_op jit(solution)/shard_map/ppermute | solution.py:330
  42.7 0.0 collective-permute-done.8.got
  42.7 0.8 %finish.1 = f32[96,1024]{1,0:T(8,128)} custom-call(f32[48,1024]{1,0:T(8,128)S(1)} %remap_chip.1.refs_2_.chip, f32[48,1024]{1,0:T(8,128)S(1)} %collective-permute-done.2.got_chip, f32[48,1024]{1,0:T(8,128)S(1)} %get-tuple-element.38.near_own, f32[24,1024]{1,0:T(8,128)S(1)} %get-tuple-element.39.far_own, f32[48,1024]{1,0:T(8,128)S(1)} %collective-permute-done.8.got, ...), custom_call_target="tpu_custom_call" | custom-call | flops 1 | bytes 1 | tf_op jit(solution)/shard_map/finish/pallas_call | solution.py:277
  (8 shorter events, 0.1 us)
Async XLA Ops:
  0.0 9.9 %copy-start.3 = (s32[128]{0:T(128)S(1)}, s32[128]{0:T(128)}, u32[]{:S(2)}) copy-start(s32[128]{0:T(128)} %columns.1) | copy-start | bytes 1540
  0.0 9.9 %copy-start.2 = (s32[128]{0:T(128)S(1)}, s32[128]{0:T(128)}, u32[]{:S(2)}) copy-start(s32[128]{0:T(128)} %rows.1) | copy-start | bytes 1540
  0.0 0.7 %copy-start = (s32[8]{0:T(128)S(1)}, s32[8]{0:T(128)}, u32[]{:S(2)}) copy-start(s32[8]{0:T(128)} %step_hour.1) | copy-start | bytes 100
  0.7 9.3 %copy-start.1 = (f32[64,8192]{1,0:T(8,128)S(1)}, f32[64,8192]{1,0:T(8,128)}, u32[]{:S(2)}) copy-start(f32[64,8192]{1,0:T(8,128)} %weights.1) | copy-start | bytes 6291460
  4.6 8.8 %collective-permute-start = (f32[24,2048]{1,0:T(8,128)S(1)}, f32[24,2048]{1,0:T(8,128)S(1)}, u32[]{:S(2)}, u32[]{:S(2)}) collective-permute-start(f32[24,2048]{1,0:T(8,128)S(1)} %get-tuple-element.24), channel_id=1, source_target_pairs={{0,1},{1,0},{4,5},{5,4},{8,9},{9,8},{12,13},{13,12},{2,3},{3,2},{6... | collective-permute-start | bytes 589832 | tf_op jit(solution)/shard_map/ppermute | solution.py:327
  5.1 8.2 %collective-permute-start.1 = (f32[48,1024]{1,0:T(8,128)S(1)}, f32[48,1024]{1,0:T(8,128)S(1)}, u32[]{:S(2)}, u32[]{:S(2)}) collective-permute-start(f32[48,1024]{1,0:T(8,128)S(1)} %get-tuple-element.29), channel_id=1, source_target_pairs={{0,2},{2,0},{1,3},{3,1},{4,6},{6,4},{5,7},{7,5},{8,10},{10,8},{9,1... | collective-permute-start | bytes 589832 | tf_op jit(solution)/shard_map/ppermute | solution.py:330
  7.7 13.0 %collective-permute-start.3 = (f32[24,2048]{1,0:T(8,128)S(1)}, f32[24,2048]{1,0:T(8,128)S(1)}, u32[]{:S(2)}, u32[]{:S(2)}) collective-permute-start(f32[24,2048]{1,0:T(8,128)S(1)} %get-tuple-element.32), channel_id=1, source_target_pairs={{0,4},{1,5},{4,0},{5,1},{8,12},{9,13},{12,8},{13,9},{2,6},{3,7},{6... | collective-permute-start | bytes 589832 | tf_op jit(solution)/shard_map/ppermute | solution.py:327
  9.3 13.0 %collective-permute-start.4 = (f32[24,2048]{1,0:T(8,128)S(1)}, f32[24,2048]{1,0:T(8,128)S(1)}, u32[]{:S(2)}, u32[]{:S(2)}) collective-permute-start(f32[24,2048]{1,0:T(8,128)S(1)} %get-tuple-element.33), channel_id=1, source_target_pairs={{0,5},{1,4},{4,1},{5,0},{8,13},{9,12},{12,9},{13,8},{2,7},{3,6},{6... | collective-permute-start | bytes 589832 | tf_op jit(solution)/shard_map/ppermute | solution.py:327
  12.8 9.5 %collective-permute-start.7 = (f32[48,1024]{1,0:T(8,128)S(1)}, f32[48,1024]{1,0:T(8,128)S(1)}, u32[]{:S(2)}, u32[]{:S(2)}) collective-permute-start(f32[48,1024]{1,0:T(8,128)S(1)} %get-tuple-element.35), channel_id=1, source_target_pairs={{0,2},{2,0},{1,3},{3,1},{4,6},{6,4},{5,7},{7,5},{8,10},{10,8},{9,1... | collective-permute-start | bytes 589832 | tf_op jit(solution)/shard_map/ppermute | solution.py:330
  13.4 11.1 %collective-permute-start.5 = (f32[24,1024]{1,0:T(8,128)S(1)}, f32[24,1024]{1,0:T(8,128)S(1)}, u32[]{:S(2)}, u32[]{:S(2)}) collective-permute-start(f32[24,1024]{1,0:T(8,128)S(1)} %get-tuple-element.30.refs_0_), channel_id=1, source_target_pairs={{0,12},{1,13},{4,8},{5,9},{8,4},{9,5},{12,0},{13,1},{2,14},{3,15},... | collective-permute-start | bytes 294920 | tf_op jit(solution)/shard_map/ppermute | solution.py:327
  18.0 7.0 %collective-permute-start.6 = (f32[24,1024]{1,0:T(8,128)S(1)}, f32[24,1024]{1,0:T(8,128)S(1)}, u32[]{:S(2)}, u32[]{:S(2)}) collective-permute-start(f32[24,1024]{1,0:T(8,128)S(1)} %get-tuple-element.31.refs_1_), channel_id=1, source_target_pairs={{0,13},{1,12},{4,9},{5,8},{8,5},{9,4},{12,1},{13,0},{2,15},{3,14},... | collective-permute-start | bytes 294920 | tf_op jit(solution)/shard_map/ppermute | solution.py:327
  20.7 18.2 %collective-permute-start.2 = (f32[48,1024]{1,0:T(8,128)S(1)}, f32[48,1024]{1,0:T(8,128)S(1)}, u32[]{:S(2)}, u32[]{:S(2)}) collective-permute-start(f32[48,1024]{1,0:T(8,128)S(1)} %remap_chip.1.refs_2_.chip), channel_id=1, source_target_pairs={{0,2},{2,0},{1,3},{3,1},{4,6},{6,4},{5,7},{7,5},{8,10},{10,8},{9,1... | collective-permute-start | bytes 589832 | tf_op jit(solution)/shard_map/ppermute | solution.py:330
  22.3 12.0 %collective-permute-start.9 = (f32[24,1024]{1,0:T(8,128)S(1)}, f32[24,1024]{1,0:T(8,128)S(1)}, u32[]{:S(2)}, u32[]{:S(2)}) collective-permute-start(f32[24,1024]{1,0:T(8,128)S(1)} %get-tuple-element.36.refs_0_), channel_id=1, source_target_pairs={{0,8},{1,9},{4,12},{5,13},{8,0},{9,1},{12,4},{13,5},{2,10},{3,11},... | collective-permute-start | bytes 294920 | tf_op jit(solution)/shard_map/ppermute | solution.py:327
  23.7 10.9 %collective-permute-start.10 = (f32[24,1024]{1,0:T(8,128)S(1)}, f32[24,1024]{1,0:T(8,128)S(1)}, u32[]{:S(2)}, u32[]{:S(2)}) collective-permute-start(f32[24,1024]{1,0:T(8,128)S(1)} %get-tuple-element.37.refs_1_), channel_id=1, source_target_pairs={{0,9},{1,8},{4,13},{5,12},{8,1},{9,0},{12,5},{13,4},{2,11},{3,10},... | collective-permute-start | bytes 294920 | tf_op jit(solution)/shard_map/ppermute | solution.py:327
  27.8 14.9 %collective-permute-start.8 = (f32[48,1024]{1,0:T(8,128)S(1)}, f32[48,1024]{1,0:T(8,128)S(1)}, u32[]{:S(2)}, u32[]{:S(2)}) collective-permute-start(f32[48,1024]{1,0:T(8,128)S(1)} %get-tuple-element.40.refs_0_), channel_id=1, source_target_pairs={{0,2},{2,0},{1,3},{3,1},{4,6},{6,4},{5,7},{7,5},{8,10},{10,8},{9,1... | collective-permute-start | bytes 589832 | tf_op jit(solution)/shard_map/ppermute | solution.py:330
  37.2 5.5 %collective-permute-start.11 = (f32[24,1024]{1,0:T(8,128)S(1)}, f32[24,1024]{1,0:T(8,128)S(1)}, u32[]{:S(2)}, u32[]{:S(2)}) collective-permute-start(f32[24,1024]{1,0:T(8,128)S(1)} %remap_last.1.last), channel_id=1, source_target_pairs={{0,2},{2,0},{1,3},{3,1},{4,6},{6,4},{5,7},{7,5},{8,10},{10,8},{9,1... | collective-permute-start | bytes 294920 | tf_op jit(solution)/shard_map/ppermute | solution.py:330

commit v4 on v3

--- a/solution.py
+++ b/solution.py
@@ -37,9 +37,8 @@
 
 
 def place_kernel(rows, columns, count, weights, *refs):
-    held, high, low, passed, total = refs
+    high, low, total = refs[-3:]
     band = 128
-    passed[...] = held[...]
 
     @pl.loop(0, PIXELS_DEV // band)
     def _(b):
@@ -71,20 +70,20 @@
         high[at, :], low[at, :] = split(total[at, :])
 
 
-def place_tiles(rows, columns, count, weights, held):
+def place_tiles(rows, columns, count, weights, *after):
     smem = pl.BlockSpec(memory_space=pltpu.SMEM)
     vmem = pl.BlockSpec(memory_space=pltpu.VMEM)
     half = jax.ShapeDtypeStruct((PIXELS_DEV, CELLS_DEV), jnp.bfloat16)
     return pl.pallas_call(
         place_kernel,
-        out_shape=(half, half, jax.ShapeDtypeStruct(held.shape, held.dtype)),
-        in_specs=[smem, smem, smem, vmem, vmem],
-        out_specs=(vmem, vmem, vmem),
+        out_shape=(half, half),
+        in_specs=[smem, smem, smem, vmem] + [pl.BlockSpec(memory_space=pl.ANY)] * len(after),
+        out_specs=(vmem, vmem),
         scratch_shapes=[pltpu.VMEM((PIXELS_DEV, CELLS_DEV), jnp.float32)],
         compiler_params=pltpu.CompilerParams(vmem_limit_bytes=28 * MIB),
         cost_estimate=HEAVY,
         name="place_tiles",
-    )(rows, columns, count, weights, held)
+    )(rows, columns, count, weights, *after)
 
 
 PIXEL_BLOCK = 256
@@ -214,8 +213,8 @@
 
 def sums_kernel(near_peers, far_peers, step_hour, field, *refs):
     buffer, arrived = refs[-2:]
-    near = refs[: len(near_peers)]
-    theirs, mine = refs[len(near_peers) : -2 : 2], refs[len(near_peers) + 1 : -2 : 2]
+    outs = refs[-2 - len(near_peers) - 2 * len(far_peers) : -2]
+    near, theirs, mine = outs[: len(near_peers)], outs[len(near_peers) :: 2], outs[len(near_peers) + 1 :: 2]
     _, levels, steps, cells = buffer.shape
     peers = [*sum(far_peers, []), *near_peers]
     copies = field_copies(field, buffer, arrived, peers)
@@ -232,7 +231,8 @@
             theirs[chunk][j * rows : (j + 1) * rows] = result[:rows]
             mine[chunk][j * rows : (j + 1) * rows] = result[rows:]
             place += 1
-    matrix = hour_matrix(step_hour, levels, steps, range(HOURS), 1)
+    if near:
+        matrix = hour_matrix(step_hour, levels, steps, range(HOURS), 1)
     for out in near:
         copies[place].wait()
         x = buffer[place].reshape(levels * steps, cells)
@@ -240,7 +240,7 @@
         place += 1
 
 
-def hour_sums(near_peers, far_peers, step_hour, field):
+def hour_sums(near_peers, far_peers, step_hour, field, *after):
     levels, steps, _ = field.shape
     vmem = pl.BlockSpec(memory_space=pltpu.VMEM)
     shapes = [(HOURS * levels, CELLS_DEV)] * len(near_peers)
@@ -250,7 +250,7 @@
     outs = pl.pallas_call(
         functools.partial(sums_kernel, near_peers, far_peers),
         out_shape=[jax.ShapeDtypeStruct(shape, jnp.float32) for shape in shapes],
-        in_specs=[pl.BlockSpec(memory_space=pltpu.SMEM), pl.BlockSpec(memory_space=pl.ANY)],
+        in_specs=[pl.BlockSpec(memory_space=pltpu.SMEM)] + [pl.BlockSpec(memory_space=pl.ANY)] * (1 + len(after)),
         out_specs=[vmem] * len(shapes),
         scratch_shapes=[
             pltpu.VMEM((count, levels, steps, CELLS_DEV), jnp.float32),
@@ -259,14 +259,14 @@
         compiler_params=pltpu.CompilerParams(vmem_limit_bytes=52 * MIB),
         cost_estimate=LIGHT,
         name="hour_sums",
-    )(step_hour, field)
+    )(step_hour, field, *after)
     far = outs[len(near_peers) :]
     return outs[: len(near_peers)], list(zip(far[::2], far[1::2]))
 
 
-def merge_kernel(mine, got, *refs):
-    outs = refs[-2:]
-    rows = outs[0].shape[0]
+def merge_kernel(parts, mine, got, *refs):
+    outs = refs[-parts:]
+    rows = mine.shape[0] // parts
     for place, out in enumerate(outs):
         at = slice(place * rows, (place + 1) * rows)
         out[...] = mine[at] + got[at]
@@ -285,9 +285,9 @@
     )(*inputs, *after)
 
 
-def merge(mine, got, *after):
-    shape = (mine.shape[0] // 2, mine.shape[1])
-    return small_call(merge_kernel, [mine, got], after, [shape, shape], HEAVY, "merge")
+def merge(parts, mine, got, *after):
+    shapes = [(mine.shape[0] // parts, mine.shape[1])] * parts
+    return small_call(functools.partial(merge_kernel, parts), [mine, got], after, shapes, HEAVY, "merge")
 
 
 def finish_kernel(divisor, chip, got_chip, near_own, far_own, got, last, got_last, out):
@@ -330,27 +330,33 @@
         return lax.ppermute(x, "tm", [(0, 1), (1, 0)])
 
     near_peers = [(1, 0), (1, 1), (0, 1), (0, 0)]
-    far_peers = [[(k, j) for j in range(subs)] for k in (half + 1, half)]
-    near, ((theirs_a, mine_a), (theirs_b, mine_b)) = hour_sums(near_peers, far_peers, step_hour, field)
-    got_a = swap(theirs_a)
-    near = [to_peer(x, k, j) for x, (k, j) in list(zip(near, near_peers))[:-1]] + [near[-1]]
-    near_same, near_other, sibling, own = near
-    high, low, theirs_b = place_tiles(tile_rows, tile_columns, live_count, tile_weight, theirs_b)
-    got_b = swap(theirs_b)
-    merged_a = merge(mine_a, got_a, sibling, high)
-    far_a = [to_peer(x, *peer) for x, peer in zip(merged_a, far_peers[0])]
-
-    rows = mine_a.shape[0] // subs
+    chunks = [[(half + 1, 0)], [(half + 1, 1)], [(half, j) for j in range(subs)]]
+
+    def send_merged(chunk, mine, got, *after):
+        merged = merge(len(chunk), mine, got, *after)
+        return merged, [to_peer(x, *peer) for x, peer in zip(merged, chunk)]
+
+    _, [(theirs_0, mine_0)] = hour_sums([], chunks[:1], step_hour, field)
+    got_0 = swap(theirs_0)
+    near, [(theirs_1, mine_1)] = hour_sums(near_peers, chunks[1:2], step_hour, field, theirs_0)
+    got_1 = swap(theirs_1)
+    near_same, near_other, sibling = [to_peer(x, *peer) for x, peer in zip(near[:3], near_peers)]
+    merged_0, far_0 = send_merged(chunks[0], mine_0, got_0, theirs_1)
+    merged_1, far_1 = send_merged(chunks[1], mine_1, got_1, sibling, *merged_0)
+    _, [(theirs_2, mine_2)] = hour_sums([], chunks[2:], step_hour, field, *merged_1)
+    got_2 = swap(theirs_2)
+    high, low = place_tiles(tile_rows, tile_columns, live_count, tile_weight, theirs_2)
+    merged_2, far_2 = send_merged(chunks[2], mine_2, got_2, high, near_same, near_other)
+
+    rows = mine_0.shape[0]
     (chip,) = remap_call(
-        remap_chip_kernel, [own, sibling], merged_a, [2 * rows], high, low, HEAVY, "remap_chip"
+        remap_chip_kernel, [near[3], sibling], merged_2, [2 * rows], high, low, HEAVY, "remap_chip"
     )
     got_chip = swap(chip)
-    merged_b = merge(mine_b, got_b, near_same, near_other, chip)
-    far_b = [to_peer(x, *peer) for x, peer in zip(merged_b, far_peers[1])]
     near_out, far_out, send = remap_call(
         remap_first_kernel,
-        [near_same, near_other, *far_a],
-        merged_b,
+        [near_same, near_other, *far_0, *far_1],
+        [chip],
         [2 * rows, rows, 2 * rows],
         high,
         low,
@@ -358,7 +364,7 @@
         "remap_first",
     )
     got = swap(send)
-    (last,) = remap_call(remap_last_kernel, far_b, [send], [rows], high, low, HEAVY, "remap_last")
+    (last,) = remap_call(remap_last_kernel, far_2, [send], [rows], high, low, HEAVY, "remap_last")
     got_last = swap(last)
     out = finish([chip, got_chip, near_out, far_out, got, last, got_last], divisor)
     return out.reshape(HOURS, out.shape[0] // HOURS, PIXELS_DEV)
@@ -374,7 +380,7 @@
     partial = jnp.einsum("hs,slgc->ghlc", table, fields, precision=lax.Precision.HIGHEST)
     regrouped = lax.all_to_all(partial, ("lev", "sub"), split_axis=0, concat_axis=0, tiled=True)
     rows = jnp.transpose(regrouped, (1, 0, 2, 3)).reshape(-1, cells // shards)
-    high, low, rows = place_tiles(tile_rows, tile_columns, live_count, tile_weight, rows)
+    high, low = place_tiles(tile_rows, tile_columns, live_count, tile_weight)
     (out,) = remap_call(remap_rows_kernel, [rows], [], [rows.shape[0]], high, low, LIGHT, "remap_rows")
     out = out.reshape(HOURS, shards * levels, PIXELS_DEV) / divisor
     return lax.psum_scatter(out, "tm", scatter_dimension=1, tiled=True)

time: 43.6 us -> 46 us (1.055)
  Pallas kernels: 15.5 us -> 19.3 us
  waiting for transfers between devices: 9.71 us -> 8.95 us
  starting transfers between devices: 16.8 us -> 16.1 us
    ppermute x7, waiting for transfers between devices: 5.97 us -> 1.84 us  [to_peer(): return lax.ppermute(x, ('lev', 'sub'), pairs)]
    ppermute x5 -> x6, waiting for transfers between devices: 3.74 us -> 7.11 us  [swap(): return lax.ppermute(x, 'tm', [(0, 1), (1, 0)])]
    pallas_call x1 -> x3, Pallas kernels: 3.91 us -> 7.2 us  [hour_sums(): pl.pallas_call(functools.partial(sums_kernel, near_peers, far_peers), out...]
    ppermute x5 -> x6, starting transfers between devices: 7.86 us -> 6.99 us  [swap(): return lax.ppermute(x, 'tm', [(0, 1), (1, 0)])]
    pallas_call x1, Pallas kernels: 2.8 us -> 3.3 us  [place_tiles(): pl.pallas_call(place_kernel, out_shape=(half, half), in_specs=[smem, smem...]
  transfers between devices with their start and end apart: 12 -> 13, of which waited for: 4 -> 4; matrix products, arithmetic and copies ran while one was open for 0% -> 0% of each run, Pallas kernels for 25% -> 36%
where the time goes in v4:
time: 46 us; the launch traced here: 45.8 us
  Pallas kernels  19.3 us (42%)
  starting transfers between devices  16.1 us (35%)
  waiting for transfers between devices  8.95 us (19%)
  between operations  0.8 us (2%)
  local copies, waits for them, and re-layouts  0.67 us (1%)
    ppermute x7, starting transfers between devices, to_peer(): return lax.ppermute(x, ('lev', 'sub'), pairs)  9.08 us
    pallas_call x3, Pallas kernels, remap_call(): pl.pallas_call(kernel, out_shape=[jax.ShapeDtypeStruct((rows, PIXELS_DEV)...  7.95 us
    pallas_call x3, Pallas kernels, hour_sums(): pl.pallas_call(functools.partial(sums_kernel, near_peers, far_peers), out...  7.2 us
    ppermute x6, waiting for transfers between devices, swap(): return lax.ppermute(x, 'tm', [(0, 1), (1, 0)])  7.11 us
    ppermute x6, starting transfers between devices, swap(): return lax.ppermute(x, 'tm', [(0, 1), (1, 0)])  6.99 us
    pallas_call x1, Pallas kernels, place_tiles(): pl.pallas_call(place_kernel, out_shape=(half, half), in_specs=[smem, smem...  3.3 us
    ppermute x7, waiting for transfers between devices, to_peer(): return lax.ppermute(x, ('lev', 'sub'), pairs)  1.84 us
  transfers between devices with their start and end apart: 13, of which 4 were waited for; matrix products, arithmetic and copies ran while one was open for 0% of the time, Pallas kernels for 36%

profile of v4, /device:TPU:0, one launch (start us, length us, event | category | flops | bytes accessed | tf_op | source)
XLA Modules:
  0.0 45.8 jit_solution(12685050547991771631)
XLA Ops:
  0.0 0.7 %copy-done = s32[8]{0:T(128)S(1)} copy-done((s32[8]{0:T(128)S(1)}, s32[8]{0:T(128)}, u32[]{:S(2)}) %copy-start) | copy-done | bytes 56
  0.7 2.0 %hour_sums.3 = (f32[24,1024]{1,0:T(8,128)S(1)}, f32[24,1024]{1,0:T(8,128)S(1)}) custom-call(s32[8]{0:T(128)S(1)} %copy-done, f32[12,8,16384]{2,1,0:T(8,128)} %bitcast.2), custom_call_target="tpu_custom_call" | custom-call | flops 1 | bytes 1 | tf_op jit(solution)/shard_map/hour_sums/pallas_call | solution.py:250
  2.6 3.0 %collective-permute-start.2 = (f32[24,1024]{1,0:T(8,128)S(1)}, f32[24,1024]{1,0:T(8,128)S(1)}, u32[]{:S(2)}, u32[]{:S(2)}) collective-permute-start(f32[24,1024]{1,0:T(8,128)S(1)} %get-tuple-element.22.refs_0_), channel_id=1, source_target_pairs={{0,2},{2,0},{1,3},{3,1},{4,6},{6,4},{5,7},{7,5},{8,10},{10,8},{9,1... | collective-permute-start | bytes 294920 | tf_op jit(solution)/shard_map/ppermute | solution.py:330
  5.6 3.0 %hour_sums.4 = (f32[24,2048]{1,0:T(8,128)S(1)}, f32[24,2048]{1,0:T(8,128)S(1)}, f32[24,2048]{1,0:T(8,128)S(1)}, f32[24,2048]{1,0:T(8,128)S(1)}, f32[24,1024]{1,0:T(8,128)S(1)}, /*index=5*/f32[24,1024]{1,0:T(8,128)S(1)}) custom-call(s32[8]{0:T(128)S(1)} %copy-done, f32[12,8,16384]{2,1,0:T(8,128)} %bitcast.3, f32[24,1024]{1,0:T(8,128)S(1)} %get-tuple-element.22.refs_0_), custom_call_target="tpu_custom_call" | custom-call | flops 1 | bytes 1 | tf_op jit(solution)/shard_map/hour_sums/pallas_call | solution.py:250
  8.7 0.1 collective-permute-start.1
  8.7 0.1 collective-permute-start
  8.8 2.0 %collective-permute-start.4 = (f32[24,2048]{1,0:T(8,128)S(1)}, f32[24,2048]{1,0:T(8,128)S(1)}, u32[]{:S(2)}, u32[]{:S(2)}) collective-permute-start(f32[24,2048]{1,0:T(8,128)S(1)} %get-tuple-element.32), channel_id=1, source_target_pairs={{0,4},{1,5},{4,0},{5,1},{8,12},{9,13},{12,8},{13,9},{2,6},{3,7},{6... | collective-permute-start | bytes 589832 | tf_op jit(solution)/shard_map/ppermute | solution.py:327
  10.8 0.1 collective-permute-start.5
  11.7 3.8 %collective-permute-start.7 = (f32[24,1024]{1,0:T(8,128)S(1)}, f32[24,1024]{1,0:T(8,128)S(1)}, u32[]{:S(2)}, u32[]{:S(2)}) collective-permute-start(f32[24,1024]{1,0:T(8,128)S(1)} %merge.3.refs_1_), channel_id=1, source_target_pairs={{0,12},{1,13},{4,8},{5,9},{8,4},{9,5},{12,0},{13,1},{2,14},{3,15},... | collective-permute-start | bytes 294920 | tf_op jit(solution)/shard_map/ppermute | solution.py:327
  15.5 0.0 collective-permute-done.1.got
  15.5 0.0 collective-permute-done.refs_0_.sibling
  15.5 0.0 copy-start.1
  15.5 0.0 copy-start.2
  15.5 0.0 copy-start.3
  15.5 0.1 collective-permute-start.8
  15.6 2.2 %hour_sums.5 = (f32[48,1024]{1,0:T(8,128)S(1)}, f32[48,1024]{1,0:T(8,128)S(1)}) custom-call(s32[8]{0:T(128)S(1)} %copy-done, f32[12,8,16384]{2,1,0:T(8,128)} %bitcast.4, f32[24,1024]{1,0:T(8,128)S(1)} %merge.4.refs_0_), custom_call_target="tpu_custom_call" | custom-call | flops 1 | bytes 1 | tf_op jit(solution)/shard_map/hour_sums/pallas_call | solution.py:250
  17.8 1.6 %collective-permute-start.3 = (f32[48,1024]{1,0:T(8,128)S(1)}, f32[48,1024]{1,0:T(8,128)S(1)}, u32[]{:S(2)}, u32[]{:S(2)}) collective-permute-start(f32[48,1024]{1,0:T(8,128)S(1)} %get-tuple-element.28.refs_0_), channel_id=1, source_target_pairs={{0,2},{2,0},{1,3},{3,1},{4,6},{6,4},{5,7},{7,5},{8,10},{10,8},{9,1... | collective-permute-start | bytes 589832 | tf_op jit(solution)/shard_map/ppermute | solution.py:330
  19.4 3.3 %place_tiles.1 = (bf16[1024,2048]{1,0:T(8,128)(2,1)S(1)}, bf16[1024,2048]{1,0:T(8,128)(2,1)S(1)}) custom-call(s32[128]{0:T(128)S(1)} %copy-done.2, s32[128]{0:T(128)S(1)} %copy-done.3, s32[1]{0:T(128)S(6)} %copy.7.count, f32[64,8192]{1,0:T(8,128)S(1)} %copy-done.1, f32[48,1024]{1,0:T(8,128)S(1)} %get-tuple-element.28.refs_0_), custom_call_target="tpu_custom_call" | custom-call | flops 10000000000 | bytes 1 | tf_op jit(solution)/shard_map/place_tiles/pallas_call | solution.py:77
  22.7 2.4 %collective-permute-done.3.got = f32[48,1024]{1,0:T(8,128)S(1)} collective-permute-done((f32[48,1024]{1,0:T(8,128)S(1)}, f32[48,1024]{1,0:T(8,128)S(1)}, u32[]{:S(2)}, u32[]{:S(2)}) %collective-permute-start.3) | collective-permute-done | bytes 196640 | tf_op jit(solution)/shard_map/ppermute | solution.py:330
  25.2 0.8 %collective-permute-start.10 = (f32[24,1024]{1,0:T(8,128)S(1)}, f32[24,1024]{1,0:T(8,128)S(1)}, u32[]{:S(2)}, u32[]{:S(2)}) collective-permute-start(f32[24,1024]{1,0:T(8,128)S(1)} %get-tuple-element.34.refs_0_), channel_id=1, source_target_pairs={{0,8},{1,9},{4,12},{5,13},{8,0},{9,1},{12,4},{13,5},{2,10},{3,11},... | collective-permute-start | bytes 294920 | tf_op jit(solution)/shard_map/ppermute | solution.py:327
  25.9 2.2 %collective-permute-start.11 = (f32[24,1024]{1,0:T(8,128)S(1)}, f32[24,1024]{1,0:T(8,128)S(1)}, u32[]{:S(2)}, u32[]{:S(2)}) collective-permute-start(f32[24,1024]{1,0:T(8,128)S(1)} %get-tuple-element.35.refs_1_), channel_id=1, source_target_pairs={{0,9},{1,8},{4,13},{5,12},{8,1},{9,0},{12,5},{13,4},{2,11},{3,10},... | collective-permute-start | bytes 294920 | tf_op jit(solution)/shard_map/ppermute | solution.py:327
  28.1 2.6 %remap_chip.1.refs_0_.chip = f32[48,1024]{1,0:T(8,128)S(1)} custom-call(f32[24,2048]{1,0:T(8,128)S(1)} %get-tuple-element.23.own, f32[24,2048]{1,0:T(8,128)S(1)} %collective-permute-done.refs_0_.sibling, bf16[1024,2048]{1,0:T(8,128)(2,1)S(1)} %get-tuple-element.29.refs_0_.high, bf16[1024,2048]{1,0:T(8,128)(2,1)S(1)} %get-tuple-element.30.low, ...), custom_call_target="tpu_custom_call" | custom-call | flops 10000000000 | bytes 1 | tf_op jit(solution)/shard_map/remap_chip/pallas_call | solution.py:104
  30.8 0.9 %collective-permute-start.6 = (f32[48,1024]{1,0:T(8,128)S(1)}, f32[48,1024]{1,0:T(8,128)S(1)}, u32[]{:S(2)}, u32[]{:S(2)}) collective-permute-start(f32[48,1024]{1,0:T(8,128)S(1)} %remap_chip.1.refs_0_.chip), channel_id=1, source_target_pairs={{0,2},{2,0},{1,3},{3,1},{4,6},{6,4},{5,7},{7,5},{8,10},{10,8},{9,1... | collective-permute-start | bytes 589832 | tf_op jit(solution)/shard_map/ppermute | solution.py:330
  31.7 0.0 collective-permute-done.7.same
  31.7 2.7 %remap_first.1 = (f32[48,1024]{1,0:T(8,128)S(1)}, f32[24,1024]{1,0:T(8,128)S(1)}, f32[48,1024]{1,0:T(8,128)S(1)}) custom-call(f32[24,2048]{1,0:T(8,128)S(1)} %collective-permute-done.4.refs_1_.near_same, f32[24,2048]{1,0:T(8,128)S(1)} %collective-permute-done.5.refs_2_.near_other, f32[24,1024]{1,0:T(8,128)S(1)} %collective-permute-done.7.same, ...), custom_call_target="tpu_custom_call" | custom-call | flops 10000000000 | bytes 1 | tf_op jit(solution)/shard_map/remap_first/pallas_call | solution.py:104
  34.5 1.2 %collective-permute-start.9 = (f32[48,1024]{1,0:T(8,128)S(1)}, f32[48,1024]{1,0:T(8,128)S(1)}, u32[]{:S(2)}, u32[]{:S(2)}) collective-permute-start(f32[48,1024]{1,0:T(8,128)S(1)} %get-tuple-element.38.refs_0_), channel_id=1, source_target_pairs={{0,2},{2,0},{1,3},{3,1},{4,6},{6,4},{5,7},{7,5},{8,10},{10,8},{9,1... | collective-permute-start | bytes 589832 | tf_op jit(solution)/shard_map/ppermute | solution.py:330
  35.7 0.3 collective-permute-done.10.same
  36.0 1.5 %collective-permute-done.11.other = f32[24,1024]{1,0:T(8,128)S(1)} collective-permute-done((f32[24,1024]{1,0:T(8,128)S(1)}, f32[24,1024]{1,0:T(8,128)S(1)}, u32[]{:S(2)}, u32[]{:S(2)}) %collective-permute-start.11) | collective-permute-done | bytes 98336 | tf_op jit(solution)/shard_map/ppermute | solution.py:327
  37.5 2.6 %remap_last.1.last = f32[24,1024]{1,0:T(8,128)S(1)} custom-call(f32[24,1024]{1,0:T(8,128)S(1)} %collective-permute-done.10.same, f32[24,1024]{1,0:T(8,128)S(1)} %collective-permute-done.11.other, bf16[1024,2048]{1,0:T(8,128)(2,1)S(1)} %get-tuple-element.29.refs_0_.high, bf16[1024,2048]{1,0:T(8,128)(2,1)S(1)} %get-tuple-element.30.low, ...), custom_call_target="tpu_custom_call" | custom-call | flops 10000000000 | bytes 1 | tf_op jit(solution)/shard_map/remap_last/pallas_call | solution.py:104
  40.1 0.2 collective-permute-start.12
  40.3 4.7 %collective-permute-done.12.got_last = f32[24,1024]{1,0:T(8,128)S(1)} collective-permute-done((f32[24,1024]{1,0:T(8,128)S(1)}, f32[24,1024]{1,0:T(8,128)S(1)}, u32[]{:S(2)}, u32[]{:S(2)}) %collective-permute-start.12) | collective-permute-done | bytes 98336 | tf_op jit(solution)/shard_map/ppermute | solution.py:330
  45.0 0.8 %finish.1 = f32[96,1024]{1,0:T(8,128)} custom-call(f32[48,1024]{1,0:T(8,128)S(1)} %remap_chip.1.refs_0_.chip, f32[48,1024]{1,0:T(8,128)S(1)} %collective-permute-done.6.got_chip, f32[48,1024]{1,0:T(8,128)S(1)} %get-tuple-element.36.near_own, f32[24,1024]{1,0:T(8,128)S(1)} %get-tuple-element.37.far_own, f32[48,1024]{1,0:T(8,128)S(1)} %collective-permute-done.9.got, ...), custom_call_target="tpu_custom_call" | custom-call | flops 1 | bytes 1 | tf_op jit(solution)/shard_map/finish/pallas_call | solution.py:277
  (13 shorter events, 0.1 us)
Async XLA Ops:
  0.0 0.7 %copy-start = (s32[8]{0:T(128)S(1)}, s32[8]{0:T(128)}, u32[]{:S(2)}) copy-start(s32[8]{0:T(128)} %step_hour.5) | copy-start | bytes 100
  2.6 9.0 %collective-permute-start.2 = (f32[24,1024]{1,0:T(8,128)S(1)}, f32[24,1024]{1,0:T(8,128)S(1)}, u32[]{:S(2)}, u32[]{:S(2)}) collective-permute-start(f32[24,1024]{1,0:T(8,128)S(1)} %get-tuple-element.22.refs_0_), channel_id=1, source_target_pairs={{0,2},{2,0},{1,3},{3,1},{4,6},{6,4},{5,7},{7,5},{8,10},{10,8},{9,1... | collective-permute-start | bytes 294920 | tf_op jit(solution)/shard_map/ppermute | solution.py:330
  8.7 6.8 %collective-permute-start.1 = (f32[24,1024]{1,0:T(8,128)S(1)}, f32[24,1024]{1,0:T(8,128)S(1)}, u32[]{:S(2)}, u32[]{:S(2)}) collective-permute-start(f32[24,1024]{1,0:T(8,128)S(1)} %get-tuple-element.26.refs_0_), channel_id=1, source_target_pairs={{0,2},{2,0},{1,3},{3,1},{4,6},{6,4},{5,7},{7,5},{8,10},{10,8},{9,1... | collective-permute-start | bytes 294920 | tf_op jit(solution)/shard_map/ppermute | solution.py:330
  8.7 6.7 %collective-permute-start = (f32[24,2048]{1,0:T(8,128)S(1)}, f32[24,2048]{1,0:T(8,128)S(1)}, u32[]{:S(2)}, u32[]{:S(2)}) collective-permute-start(f32[24,2048]{1,0:T(8,128)S(1)} %get-tuple-element.24), channel_id=1, source_target_pairs={{0,1},{1,0},{4,5},{5,4},{8,9},{9,8},{12,13},{13,12},{2,3},{3,2},{6... | collective-permute-start | bytes 589832 | tf_op jit(solution)/shard_map/ppermute | solution.py:327
  8.8 13.9 %collective-permute-start.4 = (f32[24,2048]{1,0:T(8,128)S(1)}, f32[24,2048]{1,0:T(8,128)S(1)}, u32[]{:S(2)}, u32[]{:S(2)}) collective-permute-start(f32[24,2048]{1,0:T(8,128)S(1)} %get-tuple-element.32), channel_id=1, source_target_pairs={{0,4},{1,5},{4,0},{5,1},{8,12},{9,13},{12,8},{13,9},{2,6},{3,7},{6... | collective-permute-start | bytes 589832 | tf_op jit(solution)/shard_map/ppermute | solution.py:327
  10.8 11.9 %collective-permute-start.5 = (f32[24,2048]{1,0:T(8,128)S(1)}, f32[24,2048]{1,0:T(8,128)S(1)}, u32[]{:S(2)}, u32[]{:S(2)}) collective-permute-start(f32[24,2048]{1,0:T(8,128)S(1)} %get-tuple-element.33), channel_id=1, source_target_pairs={{0,5},{1,4},{4,1},{5,0},{8,13},{9,12},{12,9},{13,8},{2,7},{3,6},{6... | collective-permute-start | bytes 589832 | tf_op jit(solution)/shard_map/ppermute | solution.py:327
  11.7 20.0 %collective-permute-start.7 = (f32[24,1024]{1,0:T(8,128)S(1)}, f32[24,1024]{1,0:T(8,128)S(1)}, u32[]{:S(2)}, u32[]{:S(2)}) collective-permute-start(f32[24,1024]{1,0:T(8,128)S(1)} %merge.3.refs_1_), channel_id=1, source_target_pairs={{0,12},{1,13},{4,8},{5,9},{8,4},{9,5},{12,0},{13,1},{2,14},{3,15},... | collective-permute-start | bytes 294920 | tf_op jit(solution)/shard_map/ppermute | solution.py:327
  15.5 3.9 %copy-start.1 = (f32[64,8192]{1,0:T(8,128)S(1)}, f32[64,8192]{1,0:T(8,128)}, u32[]{:S(2)}) copy-start(f32[64,8192]{1,0:T(8,128)} %weights.1) | copy-start | bytes 6291460
  15.5 3.9 %copy-start.2 = (s32[128]{0:T(128)S(1)}, s32[128]{0:T(128)}, u32[]{:S(2)}) copy-start(s32[128]{0:T(128)} %rows.1) | copy-start | bytes 1540
  15.5 3.9 %copy-start.3 = (s32[128]{0:T(128)S(1)}, s32[128]{0:T(128)}, u32[]{:S(2)}) copy-start(s32[128]{0:T(128)} %columns.1) | copy-start | bytes 1540
  15.5 16.2 %collective-permute-start.8 = (f32[24,1024]{1,0:T(8,128)S(1)}, f32[24,1024]{1,0:T(8,128)S(1)}, u32[]{:S(2)}, u32[]{:S(2)}) collective-permute-start(f32[24,1024]{1,0:T(8,128)S(1)} %merge.4.refs_0_), channel_id=1, source_target_pairs={{0,13},{1,12},{4,9},{5,8},{8,5},{9,4},{12,1},{13,0},{2,15},{3,14},... | collective-permute-start | bytes 294920 | tf_op jit(solution)/shard_map/ppermute | solution.py:327
  17.8 7.3 %collective-permute-start.3 = (f32[48,1024]{1,0:T(8,128)S(1)}, f32[48,1024]{1,0:T(8,128)S(1)}, u32[]{:S(2)}, u32[]{:S(2)}) collective-permute-start(f32[48,1024]{1,0:T(8,128)S(1)} %get-tuple-element.28.refs_0_), channel_id=1, source_target_pairs={{0,2},{2,0},{1,3},{3,1},{4,6},{6,4},{5,7},{7,5},{8,10},{10,8},{9,1... | collective-permute-start | bytes 589832 | tf_op jit(solution)/shard_map/ppermute | solution.py:330
  25.2 10.8 %collective-permute-start.10 = (f32[24,1024]{1,0:T(8,128)S(1)}, f32[24,1024]{1,0:T(8,128)S(1)}, u32[]{:S(2)}, u32[]{:S(2)}) collective-permute-start(f32[24,1024]{1,0:T(8,128)S(1)} %get-tuple-element.34.refs_0_), channel_id=1, source_target_pairs={{0,8},{1,9},{4,12},{5,13},{8,0},{9,1},{12,4},{13,5},{2,10},{3,11},... | collective-permute-start | bytes 294920 | tf_op jit(solution)/shard_map/ppermute | solution.py:327
  25.9 11.6 %collective-permute-start.11 = (f32[24,1024]{1,0:T(8,128)S(1)}, f32[24,1024]{1,0:T(8,128)S(1)}, u32[]{:S(2)}, u32[]{:S(2)}) collective-permute-start(f32[24,1024]{1,0:T(8,128)S(1)} %get-tuple-element.35.refs_1_), channel_id=1, source_target_pairs={{0,9},{1,8},{4,13},{5,12},{8,1},{9,0},{12,5},{13,4},{2,11},{3,10},... | collective-permute-start | bytes 294920 | tf_op jit(solution)/shard_map/ppermute | solution.py:327
  30.8 14.2 %collective-permute-start.6 = (f32[48,1024]{1,0:T(8,128)S(1)}, f32[48,1024]{1,0:T(8,128)S(1)}, u32[]{:S(2)}, u32[]{:S(2)}) collective-permute-start(f32[48,1024]{1,0:T(8,128)S(1)} %remap_chip.1.refs_0_.chip), channel_id=1, source_target_pairs={{0,2},{2,0},{1,3},{3,1},{4,6},{6,4},{5,7},{7,5},{8,10},{10,8},{9,1... | collective-permute-start | bytes 589832 | tf_op jit(solution)/shard_map/ppermute | solution.py:330
  34.5 10.5 %collective-permute-start.9 = (f32[48,1024]{1,0:T(8,128)S(1)}, f32[48,1024]{1,0:T(8,128)S(1)}, u32[]{:S(2)}, u32[]{:S(2)}) collective-permute-start(f32[48,1024]{1,0:T(8,128)S(1)} %get-tuple-element.38.refs_0_), channel_id=1, source_target_pairs={{0,2},{2,0},{1,3},{3,1},{4,6},{6,4},{5,7},{7,5},{8,10},{10,8},{9,1... | collective-permute-start | bytes 589832 | tf_op jit(solution)/shard_map/ppermute | solution.py:330
  40.1 4.9 %collective-permute-start.12 = (f32[24,1024]{1,0:T(8,128)S(1)}, f32[24,1024]{1,0:T(8,128)S(1)}, u32[]{:S(2)}, u32[]{:S(2)}) collective-permute-start(f32[24,1024]{1,0:T(8,128)S(1)} %remap_last.1.last), channel_id=1, source_target_pairs={{0,2},{2,0},{1,3},{3,1},{4,6},{6,4},{5,7},{7,5},{8,10},{10,8},{9,1... | collective-permute-start | bytes 294920 | tf_op jit(solution)/shard_map/ppermute | solution.py:330

commit v5 on v4

--- a/solution.py
+++ b/solution.py
@@ -117,11 +117,15 @@
         out[:, at] = result
 
 
+def unfold(block):
+    levels = block.shape[0] // 2
+    return jnp.concatenate([block[:levels], block[levels:]], axis=1)
+
+
 def far_rows(same_sub, other_sub):
     even = lax.axis_index("sub") == 0
-    levels = same_sub.shape[0] // 2
     blocks = [jnp.where(even, same_sub, other_sub), jnp.where(even, other_sub, same_sub)]
-    return [jnp.concatenate([block[:levels], block[levels:]], axis=1) for block in blocks]
+    return [unfold(block) for block in blocks]
 
 
 def keeps_near():
@@ -145,30 +149,29 @@
         out[:, at] = by_hour(result, own.shape[0] // HOURS)
 
 
-def remap_first_kernel(near_same, near_other, same, other, high, low, *refs):
+def remap_first_kernel(near_same, near_other, plain, same, other, high, low, *refs):
     near_out, far_out, send = refs[-3:]
     levels = near_same.shape[0] // HOURS
     rows = 2 * HOURS * levels
-    blocks = near_rows(near_same[...], near_other[...]) + far_rows(same[...], other[...])
+    blocks = near_rows(near_same[...], near_other[...]) + [plain[...]] + far_rows(same[...], other[...])
     for at, result in remap_blocks(jnp.concatenate(blocks, axis=0), high, low):
         near_out[:, at] = by_hour(result, levels)
         far_out[:, at] = result[rows:]
     near = keeps_near()
-    half = far_out.shape[0]
 
     @pl.when(near)
     def _():
-        send[:half] = far_out[...]
-        send[half:] = jnp.zeros((send.shape[0] - half, PIXELS_DEV), jnp.float32)
+        send[...] = far_out[...]
 
     @pl.when(jnp.logical_not(near))
     def _():
         send[...] = near_out[...]
 
 
-def remap_last_kernel(same, other, high, low, *refs):
+def remap_last_kernel(block, high, low, *refs):
     out = refs[-1]
-    x = jnp.concatenate(far_rows(same[...], other[...]), axis=0)
+    x = unfold(block[...])
+    x = jnp.concatenate([x, jnp.zeros((out.shape[0] - x.shape[0], x.shape[1]), jnp.float32)], axis=0)
     for at, result in remap_blocks(x, high, low):
         out[:, at] = result
 
@@ -211,12 +214,12 @@
     return copies
 
 
-def sums_kernel(near_peers, far_peers, step_hour, field, *refs):
+def sums_kernel(plain_peers, far_peers, step_hour, field, *refs):
     buffer, arrived = refs[-2:]
-    outs = refs[-2 - len(near_peers) - 2 * len(far_peers) : -2]
-    near, theirs, mine = outs[: len(near_peers)], outs[len(near_peers) :: 2], outs[len(near_peers) + 1 :: 2]
+    outs = refs[-2 - len(plain_peers) - 2 * len(far_peers) : -2]
+    near, theirs, mine = outs[: len(plain_peers)], outs[len(plain_peers) :: 2], outs[len(plain_peers) + 1 :: 2]
     _, levels, steps, cells = buffer.shape
-    peers = [*sum(far_peers, []), *near_peers]
+    peers = [*sum(far_peers, []), *plain_peers]
     copies = field_copies(field, buffer, arrived, peers)
     me = lax.axis_index("tm")
     matrix = hour_matrix(step_hour, levels, steps, (1 - me, me), 2)
@@ -240,15 +243,15 @@
         place += 1
 
 
-def hour_sums(near_peers, far_peers, step_hour, field, *after):
+def hour_sums(plain_peers, far_peers, step_hour, field, *after):
     levels, steps, _ = field.shape
     vmem = pl.BlockSpec(memory_space=pltpu.VMEM)
-    shapes = [(HOURS * levels, CELLS_DEV)] * len(near_peers)
+    shapes = [(HOURS * levels, CELLS_DEV)] * len(plain_peers)
     for members in far_peers:
         shapes += [(len(members) * 2 * levels, CELLS_DEV // 2)] * 2
-    count = len(near_peers) + sum(map(len, far_peers))
+    count = len(plain_peers) + sum(map(len, far_peers))
     outs = pl.pallas_call(
-        functools.partial(sums_kernel, near_peers, far_peers),
+        functools.partial(sums_kernel, plain_peers, far_peers),
         out_shape=[jax.ShapeDtypeStruct(shape, jnp.float32) for shape in shapes],
         in_specs=[pl.BlockSpec(memory_space=pltpu.SMEM)] + [pl.BlockSpec(memory_space=pl.ANY)] * (1 + len(after)),
         out_specs=[vmem] * len(shapes),
@@ -260,8 +263,8 @@
         cost_estimate=LIGHT,
         name="hour_sums",
     )(step_hour, field, *after)
-    far = outs[len(near_peers) :]
-    return outs[: len(near_peers)], list(zip(far[::2], far[1::2]))
+    far = outs[len(plain_peers) :]
+    return outs[: len(plain_peers)], list(zip(far[::2], far[1::2]))
 
 
 def merge_kernel(parts, mine, got, *refs):
@@ -285,14 +288,22 @@
     )(*inputs, *after)
 
 
+def hold_kernel(x, *refs):
+    refs[-1][...] = x[...]
+
+
+def hold(x, *after):
+    return small_call(hold_kernel, [x], after, [x.shape], HEAVY, "hold")[0]
+
+
 def merge(parts, mine, got, *after):
     shapes = [(mine.shape[0] // parts, mine.shape[1])] * parts
     return small_call(functools.partial(merge_kernel, parts), [mine, got], after, shapes, HEAVY, "merge")
 
 
-def finish_kernel(divisor, chip, got_chip, near_own, far_own, got, last, got_last, out):
-    me, lev = lax.axis_index("tm"), lax.axis_index("lev") % 2
-    rows = far_own.shape[0]
+def finish_kernel(divisor, levels, chip, got_chip, near_own, far_own, got, last, got_last, out):
+    me, lev, even = lax.axis_index("tm"), lax.axis_index("lev") % 2, lax.axis_index("sub") == 0
+    rows = 2 * levels
     near = keeps_near()
     for hour in range(HOURS):
         first_at = pl.ds(pl.multiple_of((hour * 2 + 1 - lev) * rows, rows), rows)
@@ -306,12 +317,15 @@
 
         @pl.when(jnp.logical_not(near))
         def _():
-            out[first_at, :] = jnp.where(me == hour, far_own[...], got[:rows]) / divisor
-            out[last_at, :] = jnp.where(me == hour, last[...], got_last[...]) / divisor
-
-
-def finish(arrays, divisor):
-    call = functools.partial(finish_kernel, divisor)
+            out[first_at, :] = jnp.where(me == hour, far_own[rows:], got[rows:]) / divisor
+            plain = far_own[hour * levels : (hour + 1) * levels] + got[hour * levels : (hour + 1) * levels]
+            other = jnp.where(me == hour, last[:levels], got_last[:levels])
+            pair = [jnp.where(even, plain, other), jnp.where(even, other, plain)]
+            out[last_at, :] = jnp.concatenate(pair, axis=0) / divisor
+
+
+def finish(arrays, levels, divisor):
+    call = functools.partial(finish_kernel, divisor, levels)
     shape = (2 * arrays[0].shape[0], PIXELS_DEV)
     return small_call(call, arrays, [], [shape], LIGHT, "finish")[0]
 
@@ -330,43 +344,44 @@
         return lax.ppermute(x, "tm", [(0, 1), (1, 0)])
 
     near_peers = [(1, 0), (1, 1), (0, 1), (0, 0)]
-    chunks = [[(half + 1, 0)], [(half + 1, 1)], [(half, j) for j in range(subs)]]
+    plain, first, second = (half, 0), [(half + 1, j) for j in range(subs)], [(half, 1)]
 
     def send_merged(chunk, mine, got, *after):
         merged = merge(len(chunk), mine, got, *after)
         return merged, [to_peer(x, *peer) for x, peer in zip(merged, chunk)]
 
-    _, [(theirs_0, mine_0)] = hour_sums([], chunks[:1], step_hour, field)
+    (plain_sums,), [(theirs_0, mine_0)] = hour_sums([plain], [first], step_hour, field)
+    plain_got = to_peer(plain_sums, *plain)
     got_0 = swap(theirs_0)
-    near, [(theirs_1, mine_1)] = hour_sums(near_peers, chunks[1:2], step_hour, field, theirs_0)
+    near, [(theirs_1, mine_1)] = hour_sums(near_peers, [second], step_hour, field, theirs_0)
+    near_same, near_other, sibling = [to_peer(x, *peer) for x, peer in zip(near[:3], near_peers)]
+    merged_0, far_0 = send_merged(first, mine_0, got_0, theirs_1)
+    theirs_1 = hold(theirs_1, plain_got, *merged_0)
     got_1 = swap(theirs_1)
-    near_same, near_other, sibling = [to_peer(x, *peer) for x, peer in zip(near[:3], near_peers)]
-    merged_0, far_0 = send_merged(chunks[0], mine_0, got_0, theirs_1)
-    merged_1, far_1 = send_merged(chunks[1], mine_1, got_1, sibling, *merged_0)
-    _, [(theirs_2, mine_2)] = hour_sums([], chunks[2:], step_hour, field, *merged_1)
-    got_2 = swap(theirs_2)
-    high, low = place_tiles(tile_rows, tile_columns, live_count, tile_weight, theirs_2)
-    merged_2, far_2 = send_merged(chunks[2], mine_2, got_2, high, near_same, near_other)
-
-    rows = mine_0.shape[0]
+    high, low = place_tiles(tile_rows, tile_columns, live_count, tile_weight, theirs_1, sibling)
+    merged_1, far_1 = send_merged(second, mine_1, got_1, high)
+
+    levels = field.shape[0]
+    rows = 2 * levels
     (chip,) = remap_call(
-        remap_chip_kernel, [near[3], sibling], merged_2, [2 * rows], high, low, HEAVY, "remap_chip"
+        remap_chip_kernel, [near[3], sibling], merged_1, [2 * rows], high, low, HEAVY, "remap_chip"
     )
     got_chip = swap(chip)
     near_out, far_out, send = remap_call(
         remap_first_kernel,
-        [near_same, near_other, *far_0, *far_1],
+        [near_same, near_other, plain_got, *far_0],
         [chip],
-        [2 * rows, rows, 2 * rows],
+        [2 * rows] * 3,
         high,
         low,
         HEAVY,
         "remap_first",
     )
     got = swap(send)
-    (last,) = remap_call(remap_last_kernel, far_2, [send], [rows], high, low, HEAVY, "remap_last")
+    padded = -(-levels // 16) * 16
+    (last,) = remap_call(remap_last_kernel, far_1, [send], [padded], high, low, HEAVY, "remap_last")
     got_last = swap(last)
-    out = finish([chip, got_chip, near_out, far_out, got, last, got_last], divisor)
+    out = finish([chip, got_chip, near_out, far_out, got, last, got_last], levels, divisor)
     return out.reshape(HOURS, out.shape[0] // HOURS, PIXELS_DEV)
 
 

time: 46 us -> 42.6 us (0.926)
  Pallas kernels: 19.3 us -> 17.7 us
  waiting for transfers between devices: 8.95 us -> 7.6 us
  starting transfers between devices: 16.1 us -> 15.4 us
    ppermute x6 -> x5, waiting for transfers between devices: 7.11 us -> 4.97 us  [swap(): return lax.ppermute(x, 'tm', [(0, 1), (1, 0)])]
    pallas_call x3 -> x2, Pallas kernels: 7.2 us -> 5.53 us  [hour_sums(): pl.pallas_call(functools.partial(sums_kernel, plain_peers, far_peers), ou...]
    ppermute x7, waiting for transfers between devices: 1.84 us -> 2.63 us  [to_peer(): return lax.ppermute(x, ('lev', 'sub'), pairs)]
    ppermute x6 -> x5, starting transfers between devices: 6.99 us -> 6.32 us  [swap(): return lax.ppermute(x, 'tm', [(0, 1), (1, 0)])]
  transfers between devices with their start and end apart: 13 -> 12, of which waited for: 4 -> 4; matrix products, arithmetic and copies ran while one was open for 0% -> 0% of each run, Pallas kernels for 36% -> 34%
where the time goes in v5:
time: 42.6 us; the launch traced here: 42.1 us
  Pallas kernels  17.7 us (42%)
  starting transfers between devices  15.4 us (36%)
  waiting for transfers between devices  7.6 us (18%)
  between operations  0.75 us (2%)
  local copies, waits for them, and re-layouts  0.67 us (2%)
    ppermute x7, starting transfers between devices, to_peer(): return lax.ppermute(x, ('lev', 'sub'), pairs)  9.06 us
    pallas_call x3, Pallas kernels, remap_call(): pl.pallas_call(kernel, out_shape=[jax.ShapeDtypeStruct((rows, PIXELS_DEV)...  7.79 us
    ppermute x5, starting transfers between devices, swap(): return lax.ppermute(x, 'tm', [(0, 1), (1, 0)])  6.32 us
    pallas_call x2, Pallas kernels, hour_sums(): pl.pallas_call(functools.partial(sums_kernel, plain_peers, far_peers), ou...  5.53 us
    ppermute x5, waiting for transfers between devices, swap(): return lax.ppermute(x, 'tm', [(0, 1), (1, 0)])  4.97 us
    pallas_call x1, Pallas kernels, place_tiles(): pl.pallas_call(place_kernel, out_shape=(half, half), in_specs=[smem, smem...  3.56 us
    ppermute x7, waiting for transfers between devices, to_peer(): return lax.ppermute(x, ('lev', 'sub'), pairs)  2.63 us
  transfers between devices with their start and end apart: 12, of which 4 were waited for; matrix products, arithmetic and copies ran while one was open for 0% of the time, Pallas kernels for 34%

profile of v5, /device:TPU:0, one launch (start us, length us, event | category | flops | bytes accessed | tf_op | source)
XLA Modules:
  0.0 42.1 jit_solution(10399051064087080085)
XLA Ops:
  0.0 0.7 %copy-done = s32[8]{0:T(128)S(1)} copy-done((s32[8]{0:T(128)S(1)}, s32[8]{0:T(128)}, u32[]{:S(2)}) %copy-start) | copy-done | bytes 56
  0.7 2.5 %hour_sums.2 = (f32[24,2048]{1,0:T(8,128)S(1)}, f32[48,1024]{1,0:T(8,128)S(1)}, f32[48,1024]{1,0:T(8,128)S(1)}) custom-call(s32[8]{0:T(128)S(1)} %copy-done, f32[12,8,16384]{2,1,0:T(8,128)} %bitcast.2), custom_call_target="tpu_custom_call" | custom-call | flops 1 | bytes 1 | tf_op jit(solution)/shard_map/hour_sums/pallas_call | solution.py:253
  3.2 3.0 %collective-permute-start.2 = (f32[48,1024]{1,0:T(8,128)S(1)}, f32[48,1024]{1,0:T(8,128)S(1)}, u32[]{:S(2)}, u32[]{:S(2)}) collective-permute-start(f32[48,1024]{1,0:T(8,128)S(1)} %get-tuple-element.21.refs_0_), channel_id=1, source_target_pairs={{0,2},{2,0},{1,3},{3,1},{4,6},{6,4},{5,7},{7,5},{8,10},{10,8},{9,1... | collective-permute-start | bytes 589832 | tf_op jit(solution)/shard_map/ppermute | solution.py:344
  6.2 2.6 %collective-permute-start.1 = (f32[24,2048]{1,0:T(8,128)S(1)}, f32[24,2048]{1,0:T(8,128)S(1)}, u32[]{:S(2)}, u32[]{:S(2)}) collective-permute-start(f32[24,2048]{1,0:T(8,128)S(1)} %get-tuple-element.25), channel_id=1, source_target_pairs={{0,8},{1,9},{4,12},{5,13},{8,0},{9,1},{12,4},{13,5},{2,10},{3,11},... | collective-permute-start | bytes 589832 | tf_op jit(solution)/shard_map/ppermute | solution.py:341
  8.8 3.0 %hour_sums.3 = (f32[24,2048]{1,0:T(8,128)S(1)}, f32[24,2048]{1,0:T(8,128)S(1)}, f32[24,2048]{1,0:T(8,128)S(1)}, f32[24,2048]{1,0:T(8,128)S(1)}, f32[24,1024]{1,0:T(8,128)S(1)}, /*index=5*/f32[24,1024]{1,0:T(8,128)S(1)}) custom-call(s32[8]{0:T(128)S(1)} %copy-done, f32[12,8,16384]{2,1,0:T(8,128)} %bitcast.3, f32[48,1024]{1,0:T(8,128)S(1)} %get-tuple-element.21.refs_0_), custom_call_target="tpu_custom_call" | custom-call | flops 1 | bytes 1 | tf_op jit(solution)/shard_map/hour_sums/pallas_call | solution.py:253
  11.8 0.1 collective-permute-start
  11.9 1.6 %collective-permute-start.5 = (f32[24,2048]{1,0:T(8,128)S(1)}, f32[24,2048]{1,0:T(8,128)S(1)}, u32[]{:S(2)}, u32[]{:S(2)}) collective-permute-start(f32[24,2048]{1,0:T(8,128)S(1)} %get-tuple-element.32), channel_id=1, source_target_pairs={{0,4},{1,5},{4,0},{5,1},{8,12},{9,13},{12,8},{13,9},{2,6},{3,7},{6... | collective-permute-start | bytes 589832 | tf_op jit(solution)/shard_map/ppermute | solution.py:341
  13.5 0.2 collective-permute-start.6
  14.4 0.0 collective-permute-done.2.got
  14.4 1.4 %collective-permute-start.7 = (f32[24,1024]{1,0:T(8,128)S(1)}, f32[24,1024]{1,0:T(8,128)S(1)}, u32[]{:S(2)}, u32[]{:S(2)}) collective-permute-start(f32[24,1024]{1,0:T(8,128)S(1)} %get-tuple-element.27.refs_1_), channel_id=1, source_target_pairs={{0,12},{1,13},{4,8},{5,9},{8,4},{9,5},{12,0},{13,1},{2,14},{3,15},... | collective-permute-start | bytes 294920 | tf_op jit(solution)/shard_map/ppermute | solution.py:341
  15.8 1.9 %collective-permute-done.1.refs_0_.plain = f32[24,2048]{1,0:T(8,128)S(1)} collective-permute-done((f32[24,2048]{1,0:T(8,128)S(1)}, f32[24,2048]{1,0:T(8,128)S(1)}, u32[]{:S(2)}, u32[]{:S(2)}) %collective-permute-start.1) | collective-permute-done | bytes 196640 | tf_op jit(solution)/shard_map/ppermute | solution.py:341
  17.8 3.1 %collective-permute-start.8 = (f32[24,1024]{1,0:T(8,128)S(1)}, f32[24,1024]{1,0:T(8,128)S(1)}, u32[]{:S(2)}, u32[]{:S(2)}) collective-permute-start(f32[24,1024]{1,0:T(8,128)S(1)} %get-tuple-element.28.refs_2_), channel_id=1, source_target_pairs={{0,13},{1,12},{4,9},{5,8},{8,5},{9,4},{12,1},{13,0},{2,15},{3,14},... | collective-permute-start | bytes 294920 | tf_op jit(solution)/shard_map/ppermute | solution.py:341
  20.8 0.0 collective-permute-done.refs_1_.sibling
  20.8 0.6 %collective-permute-start.3 = (f32[24,1024]{1,0:T(8,128)S(1)}, f32[24,1024]{1,0:T(8,128)S(1)}, u32[]{:S(2)}, u32[]{:S(2)}) collective-permute-start(f32[24,1024]{1,0:T(8,128)S(1)} %hold.1.refs_0_), channel_id=1, source_target_pairs={{0,2},{2,0},{1,3},{3,1},{4,6},{6,4},{5,7},{7,5},{8,10},{10,8},{9,1... | collective-permute-start | bytes 294920 | tf_op jit(solution)/shard_map/ppermute | solution.py:344
  21.4 3.6 %place_tiles.1 = (bf16[1024,2048]{1,0:T(8,128)(2,1)S(1)}, bf16[1024,2048]{1,0:T(8,128)(2,1)S(1)}) custom-call(s32[128]{0:T(128)S(1)} %copy-done.2, s32[128]{0:T(128)S(1)} %copy-done.3, s32[1]{0:T(128)S(6)} %copy.7.count, f32[64,8192]{1,0:T(8,128)S(1)} %copy-done.1, f32[24,1024]{1,0:T(8,128)S(1)} %hold.1.refs_0_, ...), custom_call_target="tpu_custom_call" | custom-call | flops 10000000000 | bytes 1 | tf_op jit(solution)/shard_map/place_tiles/pallas_call | solution.py:77
  25.0 1.2 %collective-permute-done.3.got = f32[24,1024]{1,0:T(8,128)S(1)} collective-permute-done((f32[24,1024]{1,0:T(8,128)S(1)}, f32[24,1024]{1,0:T(8,128)S(1)}, u32[]{:S(2)}, u32[]{:S(2)}) %collective-permute-start.3) | collective-permute-done | bytes 98336 | tf_op jit(solution)/shard_map/ppermute | solution.py:344
  26.2 0.1 collective-permute-start.10
  26.3 2.6 %remap_chip.1.refs_0_.chip = f32[48,1024]{1,0:T(8,128)S(1)} custom-call(f32[24,2048]{1,0:T(8,128)S(1)} %get-tuple-element.22.own, f32[24,2048]{1,0:T(8,128)S(1)} %collective-permute-done.refs_1_.sibling, bf16[1024,2048]{1,0:T(8,128)(2,1)S(1)} %get-tuple-element.29.refs_0_.high, bf16[1024,2048]{1,0:T(8,128)(2,1)S(1)} %get-tuple-element.30.low, ...), custom_call_target="tpu_custom_call" | custom-call | flops 10000000000 | bytes 1 | tf_op jit(solution)/shard_map/remap_chip/pallas_call | solution.py:104
  28.9 0.0 collective-permute-done.5.near_same
  28.9 0.6 %collective-permute-start.4 = (f32[48,1024]{1,0:T(8,128)S(1)}, f32[48,1024]{1,0:T(8,128)S(1)}, u32[]{:S(2)}, u32[]{:S(2)}) collective-permute-start(f32[48,1024]{1,0:T(8,128)S(1)} %remap_chip.1.refs_0_.chip), channel_id=1, source_target_pairs={{0,2},{2,0},{1,3},{3,1},{4,6},{6,4},{5,7},{7,5},{8,10},{10,8},{9,1... | collective-permute-start | bytes 589832 | tf_op jit(solution)/shard_map/ppermute | solution.py:344
  29.5 0.7 %collective-permute-done.6.near_other = f32[24,2048]{1,0:T(8,128)S(1)} collective-permute-done((f32[24,2048]{1,0:T(8,128)S(1)}, f32[24,2048]{1,0:T(8,128)S(1)}, u32[]{:S(2)}, u32[]{:S(2)}) %collective-permute-start.6) | collective-permute-done | bytes 196640 | tf_op jit(solution)/shard_map/ppermute | solution.py:341
  30.2 0.0 collective-permute-done.7.same
  30.2 0.0 collective-permute-done.8.other
  30.2 2.8 %remap_first.1 = (f32[48,1024]{1,0:T(8,128)S(1)}, f32[48,1024]{1,0:T(8,128)S(1)}, f32[48,1024]{1,0:T(8,128)S(1)}) custom-call(f32[24,2048]{1,0:T(8,128)S(1)} %collective-permute-done.5.near_same, f32[24,2048]{1,0:T(8,128)S(1)} %collective-permute-done.6.near_other, f32[24,2048]{1,0:T(8,128)S(1)} %collective-permute-done.1.refs_0_.plain, ...), custom_call_target="tpu_custom_call" | custom-call | flops 10000000000 | bytes 1 | tf_op jit(solution)/shard_map/remap_first/pallas_call | solution.py:104
  33.0 0.8 %collective-permute-start.9 = (f32[48,1024]{1,0:T(8,128)S(1)}, f32[48,1024]{1,0:T(8,128)S(1)}, u32[]{:S(2)}, u32[]{:S(2)}) collective-permute-start(f32[48,1024]{1,0:T(8,128)S(1)} %get-tuple-element.36.refs_0_), channel_id=1, source_target_pairs={{0,2},{2,0},{1,3},{3,1},{4,6},{6,4},{5,7},{7,5},{8,10},{10,8},{9,1... | collective-permute-start | bytes 589832 | tf_op jit(solution)/shard_map/ppermute | solution.py:344
  33.9 0.0 collective-permute-done.10.block
  33.9 2.4 %remap_last.1.last = f32[16,1024]{1,0:T(8,128)S(1)} custom-call(f32[24,1024]{1,0:T(8,128)S(1)} %collective-permute-done.10.block, bf16[1024,2048]{1,0:T(8,128)(2,1)S(1)} %get-tuple-element.29.refs_0_.high, bf16[1024,2048]{1,0:T(8,128)(2,1)S(1)} %get-tuple-element.30.low, f32[48,1024]{1,0:T(8,128)S(1)} %get-tuple-element.36.refs_0_), custom_call_target="tpu_custom_call" | custom-call | flops 10000000000 | bytes 1 | tf_op jit(solution)/shard_map/remap_last/pallas_call | solution.py:104
  36.3 1.3 %collective-permute-start.11 = (f32[16,1024]{1,0:T(8,128)S(1)}, f32[16,1024]{1,0:T(8,128)S(1)}, u32[]{:S(2)}, u32[]{:S(2)}) collective-permute-start(f32[16,1024]{1,0:T(8,128)S(1)} %remap_last.1.last), channel_id=1, source_target_pairs={{0,2},{2,0},{1,3},{3,1},{4,6},{6,4},{5,7},{7,5},{8,10},{10,8},{9,1... | collective-permute-start | bytes 196616 | tf_op jit(solution)/shard_map/ppermute | solution.py:344
  37.5 3.8 %collective-permute-done.11.got_last = f32[16,1024]{1,0:T(8,128)S(1)} collective-permute-done((f32[16,1024]{1,0:T(8,128)S(1)}, f32[16,1024]{1,0:T(8,128)S(1)}, u32[]{:S(2)}, u32[]{:S(2)}) %collective-permute-start.11) | collective-permute-done | bytes 65568 | tf_op jit(solution)/shard_map/ppermute | solution.py:344
  41.3 0.0 collective-permute-done.9.got
  41.3 0.0 collective-permute-done.4.got_chip
  41.3 0.8 %finish.1 = f32[96,1024]{1,0:T(8,128)} custom-call(f32[48,1024]{1,0:T(8,128)S(1)} %remap_chip.1.refs_0_.chip, f32[48,1024]{1,0:T(8,128)S(1)} %collective-permute-done.4.got_chip, f32[48,1024]{1,0:T(8,128)S(1)} %get-tuple-element.34.near_own, f32[48,1024]{1,0:T(8,128)S(1)} %get-tuple-element.35.far_own, f32[48,1024]{1,0:T(8,128)S(1)} %collective-permute-done.9.got, ...), custom_call_target="tpu_custom_call" | custom-call | flops 1 | bytes 1 | tf_op jit(solution)/shard_map/finish/pallas_call | solution.py:280
  (10 shorter events, 0.1 us)
Async XLA Ops:
  0.0 0.7 %copy-start = (s32[8]{0:T(128)S(1)}, s32[8]{0:T(128)}, u32[]{:S(2)}) copy-start(s32[8]{0:T(128)} %step_hour.3) | copy-start | bytes 100
  3.2 11.2 %collective-permute-start.2 = (f32[48,1024]{1,0:T(8,128)S(1)}, f32[48,1024]{1,0:T(8,128)S(1)}, u32[]{:S(2)}, u32[]{:S(2)}) collective-permute-start(f32[48,1024]{1,0:T(8,128)S(1)} %get-tuple-element.21.refs_0_), channel_id=1, source_target_pairs={{0,2},{2,0},{1,3},{3,1},{4,6},{6,4},{5,7},{7,5},{8,10},{10,8},{9,1... | collective-permute-start | bytes 589832 | tf_op jit(solution)/shard_map/ppermute | solution.py:344
  6.2 11.6 %collective-permute-start.1 = (f32[24,2048]{1,0:T(8,128)S(1)}, f32[24,2048]{1,0:T(8,128)S(1)}, u32[]{:S(2)}, u32[]{:S(2)}) collective-permute-start(f32[24,2048]{1,0:T(8,128)S(1)} %get-tuple-element.25), channel_id=1, source_target_pairs={{0,8},{1,9},{4,12},{5,13},{8,0},{9,1},{12,4},{13,5},{2,10},{3,11},... | collective-permute-start | bytes 589832 | tf_op jit(solution)/shard_map/ppermute | solution.py:341
  11.8 9.0 %collective-permute-start = (f32[24,2048]{1,0:T(8,128)S(1)}, f32[24,2048]{1,0:T(8,128)S(1)}, u32[]{:S(2)}, u32[]{:S(2)}) collective-permute-start(f32[24,2048]{1,0:T(8,128)S(1)} %get-tuple-element.23), channel_id=1, source_target_pairs={{0,1},{1,0},{4,5},{5,4},{8,9},{9,8},{12,13},{13,12},{2,3},{3,2},{6... | collective-permute-start | bytes 589832 | tf_op jit(solution)/shard_map/ppermute | solution.py:341
  11.9 17.0 %collective-permute-start.5 = (f32[24,2048]{1,0:T(8,128)S(1)}, f32[24,2048]{1,0:T(8,128)S(1)}, u32[]{:S(2)}, u32[]{:S(2)}) collective-permute-start(f32[24,2048]{1,0:T(8,128)S(1)} %get-tuple-element.32), channel_id=1, source_target_pairs={{0,4},{1,5},{4,0},{5,1},{8,12},{9,13},{12,8},{13,9},{2,6},{3,7},{6... | collective-permute-start | bytes 589832 | tf_op jit(solution)/shard_map/ppermute | solution.py:341
  13.5 16.7 %collective-permute-start.6 = (f32[24,2048]{1,0:T(8,128)S(1)}, f32[24,2048]{1,0:T(8,128)S(1)}, u32[]{:S(2)}, u32[]{:S(2)}) collective-permute-start(f32[24,2048]{1,0:T(8,128)S(1)} %get-tuple-element.33), channel_id=1, source_target_pairs={{0,5},{1,4},{4,1},{5,0},{8,13},{9,12},{12,9},{13,8},{2,7},{3,6},{6... | collective-permute-start | bytes 589832 | tf_op jit(solution)/shard_map/ppermute | solution.py:341
  14.4 15.8 %collective-permute-start.7 = (f32[24,1024]{1,0:T(8,128)S(1)}, f32[24,1024]{1,0:T(8,128)S(1)}, u32[]{:S(2)}, u32[]{:S(2)}) collective-permute-start(f32[24,1024]{1,0:T(8,128)S(1)} %get-tuple-element.27.refs_1_), channel_id=1, source_target_pairs={{0,12},{1,13},{4,8},{5,9},{8,4},{9,5},{12,0},{13,1},{2,14},{3,15},... | collective-permute-start | bytes 294920 | tf_op jit(solution)/shard_map/ppermute | solution.py:341
  17.7 3.7 %copy-start.1 = (f32[64,8192]{1,0:T(8,128)S(1)}, f32[64,8192]{1,0:T(8,128)}, u32[]{:S(2)}) copy-start(f32[64,8192]{1,0:T(8,128)} %weights.1) | copy-start | bytes 6291460
  17.7 3.7 %copy-start.2 = (s32[128]{0:T(128)S(1)}, s32[128]{0:T(128)}, u32[]{:S(2)}) copy-start(s32[128]{0:T(128)} %rows.1) | copy-start | bytes 1540
  17.7 3.7 %copy-start.3 = (s32[128]{0:T(128)S(1)}, s32[128]{0:T(128)}, u32[]{:S(2)}) copy-start(s32[128]{0:T(128)} %columns.1) | copy-start | bytes 1540
  17.8 12.5 %collective-permute-start.8 = (f32[24,1024]{1,0:T(8,128)S(1)}, f32[24,1024]{1,0:T(8,128)S(1)}, u32[]{:S(2)}, u32[]{:S(2)}) collective-permute-start(f32[24,1024]{1,0:T(8,128)S(1)} %get-tuple-element.28.refs_2_), channel_id=1, source_target_pairs={{0,13},{1,12},{4,9},{5,8},{8,5},{9,4},{12,1},{13,0},{2,15},{3,14},... | collective-permute-start | bytes 294920 | tf_op jit(solution)/shard_map/ppermute | solution.py:341
  20.8 5.4 %collective-permute-start.3 = (f32[24,1024]{1,0:T(8,128)S(1)}, f32[24,1024]{1,0:T(8,128)S(1)}, u32[]{:S(2)}, u32[]{:S(2)}) collective-permute-start(f32[24,1024]{1,0:T(8,128)S(1)} %hold.1.refs_0_), channel_id=1, source_target_pairs={{0,2},{2,0},{1,3},{3,1},{4,6},{6,4},{5,7},{7,5},{8,10},{10,8},{9,1... | collective-permute-start | bytes 294920 | tf_op jit(solution)/shard_map/ppermute | solution.py:344
  26.2 7.7 %collective-permute-start.10 = (f32[24,1024]{1,0:T(8,128)S(1)}, f32[24,1024]{1,0:T(8,128)S(1)}, u32[]{:S(2)}, u32[]{:S(2)}) collective-permute-start(f32[24,1024]{1,0:T(8,128)S(1)} %merge.3.refs_0_), channel_id=1, source_target_pairs={{0,9},{1,8},{4,13},{5,12},{8,1},{9,0},{12,5},{13,4},{2,11},{3,10},... | collective-permute-start | bytes 294920 | tf_op jit(solution)/shard_map/ppermute | solution.py:341
  28.9 12.4 %collective-permute-start.4 = (f32[48,1024]{1,0:T(8,128)S(1)}, f32[48,1024]{1,0:T(8,128)S(1)}, u32[]{:S(2)}, u32[]{:S(2)}) collective-permute-start(f32[48,1024]{1,0:T(8,128)S(1)} %remap_chip.1.refs_0_.chip), channel_id=1, source_target_pairs={{0,2},{2,0},{1,3},{3,1},{4,6},{6,4},{5,7},{7,5},{8,10},{10,8},{9,1... | collective-permute-start | bytes 589832 | tf_op jit(solution)/shard_map/ppermute | solution.py:344
  33.0 8.3 %collective-permute-start.9 = (f32[48,1024]{1,0:T(8,128)S(1)}, f32[48,1024]{1,0:T(8,128)S(1)}, u32[]{:S(2)}, u32[]{:S(2)}) collective-permute-start(f32[48,1024]{1,0:T(8,128)S(1)} %get-tuple-element.36.refs_0_), channel_id=1, source_target_pairs={{0,2},{2,0},{1,3},{3,1},{4,6},{6,4},{5,7},{7,5},{8,10},{10,8},{9,1... | collective-permute-start | bytes 589832 | tf_op jit(solution)/shard_map/ppermute | solution.py:344
  36.3 5.0 %collective-permute-start.11 = (f32[16,1024]{1,0:T(8,128)S(1)}, f32[16,1024]{1,0:T(8,128)S(1)}, u32[]{:S(2)}, u32[]{:S(2)}) collective-permute-start(f32[16,1024]{1,0:T(8,128)S(1)} %remap_last.1.last), channel_id=1, source_target_pairs={{0,2},{2,0},{1,3},{3,1},{4,6},{6,4},{5,7},{7,5},{8,10},{10,8},{9,1... | collective-permute-start | bytes 196616 | tf_op jit(solution)/shard_map/ppermute | solution.py:344

commit v6 on v5

--- a/solution.py
+++ b/solution.py
@@ -18,6 +18,7 @@
 MIB = 1 << 20
 
 LIGHT = pl.CostEstimate(flops=1, bytes_accessed=1, transcendentals=0)
+MEDIUM = pl.CostEstimate(flops=2_500_000_000, bytes_accessed=1, transcendentals=0)
 HEAVY = pl.CostEstimate(flops=10_000_000_000, bytes_accessed=1, transcendentals=0)
 
 NT = (((1,), (1,)), ((), ()))
@@ -99,13 +100,14 @@
         yield at, first[:m] + first[m:] + dot(x_high, low[at, :], NT)
 
 
-def remap_call(kernel, inputs, after, out_rows, high, low, cost, name):
+def remap_call(kernel, inputs, after, out_rows, high, low, cost, name, scratch_rows=()):
     vmem = pl.BlockSpec(memory_space=pltpu.VMEM)
     return pl.pallas_call(
         kernel,
         out_shape=[jax.ShapeDtypeStruct((rows, PIXELS_DEV), jnp.float32) for rows in out_rows],
         in_specs=[vmem] * (len(inputs) + 2) + [pl.BlockSpec(memory_space=pl.ANY)] * len(after),
         out_specs=[vmem] * len(out_rows),
+        scratch_shapes=[pltpu.VMEM((rows, PIXELS_DEV), jnp.float32) for rows in scratch_rows],
         compiler_params=pltpu.CompilerParams(vmem_limit_bytes=24 * MIB),
         cost_estimate=cost,
         name=name,
@@ -142,30 +144,38 @@
     return jnp.concatenate([pieces[sub * HOURS + hour] for hour in range(HOURS) for sub in range(2)], axis=0)
 
 
-def remap_chip_kernel(own, sibling, high, low, *refs):
-    out = refs[-1]
-    x = jnp.concatenate(near_rows(own[...], sibling[...]), axis=0)
-    for at, result in remap_blocks(x, high, low):
-        out[:, at] = by_hour(result, own.shape[0] // HOURS)
-
-
-def remap_first_kernel(near_same, near_other, plain, same, other, high, low, *refs):
-    near_out, far_out, send = refs[-3:]
-    levels = near_same.shape[0] // HOURS
-    rows = 2 * HOURS * levels
-    blocks = near_rows(near_same[...], near_other[...]) + [plain[...]] + far_rows(same[...], other[...])
-    for at, result in remap_blocks(jnp.concatenate(blocks, axis=0), high, low):
-        near_out[:, at] = by_hour(result, levels)
-        far_out[:, at] = result[rows:]
+def sort_out(near_result, far_result, keep, send):
     near = keeps_near()
 
     @pl.when(near)
     def _():
-        send[...] = far_out[...]
+        keep[...], send[...] = near_result[...], far_result[...]
 
     @pl.when(jnp.logical_not(near))
     def _():
-        send[...] = near_out[...]
+        keep[...], send[...] = far_result[...], near_result[...]
+
+
+def remap_both_kernel(own, pack, plain, high, low, *refs):
+    keep, send, near_result, far_result = refs[-4:]
+    rows = own.shape[0]
+    other = jnp.concatenate([pack[:rows], pack[rows : 2 * rows]], axis=1)
+    blocks = near_rows(own[...], other) + [plain[...]]
+    for at, result in remap_blocks(jnp.concatenate(blocks, axis=0), high, low):
+        near_result[:, at] = by_hour(result, rows // HOURS)
+        far_result[:rows, at] = result[2 * rows :]
+    far_result[rows:] = jnp.zeros((rows, PIXELS_DEV), jnp.float32)
+    sort_out(near_result, far_result, keep, send)
+
+
+def remap_one_kernel(near, far, high, low, *refs):
+    keep, send, near_result, far_result = refs[-4:]
+    rows = far.shape[0]
+    blocks = far_rows(near[:rows], near[rows:]) + [far[...]]
+    for at, result in remap_blocks(jnp.concatenate(blocks, axis=0), high, low):
+        near_result[:, at] = result[:rows]
+        far_result[:, at] = result[rows:]
+    sort_out(near_result, far_result, keep, send)
 
 
 def remap_last_kernel(block, high, low, *refs):
@@ -214,46 +224,53 @@
     return copies
 
 
-def sums_kernel(plain_peers, far_peers, step_hour, field, *refs):
-    buffer, arrived = refs[-2:]
-    outs = refs[-2 - len(plain_peers) - 2 * len(far_peers) : -2]
-    near, theirs, mine = outs[: len(plain_peers)], outs[len(plain_peers) :: 2], outs[len(plain_peers) + 1 :: 2]
+def sums_kernel(plain, first, second, step_hour, field, *refs):
+    plain_out, own, pack, theirs_0, mine_0, theirs_1, mine_1, theirs_2, mine_2, buffer, arrived = refs
     _, levels, steps, cells = buffer.shape
-    peers = [*sum(far_peers, []), *plain_peers]
+    rows, cut = HOURS * levels, cells // 2
+    peers = [plain, *first, (1, 0), (1, 1), (0, 1), (0, 0), second]
     copies = field_copies(field, buffer, arrived, peers)
     me = lax.axis_index("tm")
-    matrix = hour_matrix(step_hour, levels, steps, (1 - me, me), 2)
-    rows, cut = 2 * levels, cells // 2
-    place = 0
-    for chunk, members in enumerate(far_peers):
-        for j in range(len(members)):
-            copies[place].wait()
-            high, low = split(buffer[place].reshape(levels * steps, cells))
-            halves = [high[:, :cut], low[:, :cut], high[:, cut:], low[:, cut:]]
-            result = dot(matrix, jnp.concatenate(halves, axis=0), NN)
-            theirs[chunk][j * rows : (j + 1) * rows] = result[:rows]
-            mine[chunk][j * rows : (j + 1) * rows] = result[rows:]
-            place += 1
-    if near:
-        matrix = hour_matrix(step_hour, levels, steps, range(HOURS), 1)
-    for out in near:
+    by_place = hour_matrix(step_hour, levels, steps, (1 - me, me), 2)
+    by_hour = hour_matrix(step_hour, levels, steps, range(HOURS), 1)
+
+    def halves(place):
         copies[place].wait()
-        x = buffer[place].reshape(levels * steps, cells)
-        out[...] = dot(matrix, jnp.concatenate(split(x), axis=0), NN)
-        place += 1
-
-
-def hour_sums(plain_peers, far_peers, step_hour, field, *after):
+        return split(buffer[place].reshape(levels * steps, cells))
+
+    def with_both_hours(place):
+        return dot(by_hour, jnp.concatenate(halves(place), axis=0), NN)
+
+    def theirs_and_mine(place):
+        high, low = halves(place)
+        stacked = [high[:, :cut], low[:, :cut], high[:, cut:], low[:, cut:]]
+        result = dot(by_place, jnp.concatenate(stacked, axis=0), NN)
+        return result[:rows], result[rows:]
+
+    plain_out[...] = with_both_hours(0)
+    for j in range(len(first)):
+        at = slice(j * rows, (j + 1) * rows)
+        theirs_0[at], mine_0[at] = theirs_and_mine(1 + j)
+    place = 1 + len(first)
+    theirs_1[...], mine_1[...] = theirs_and_mine(place)
+    pack[2 * rows : 3 * rows], pack[3 * rows :] = theirs_and_mine(place + 1)
+    result = with_both_hours(place + 2)
+    pack[:rows], pack[rows : 2 * rows] = result[:, :cut], result[:, cut:]
+    own[...] = with_both_hours(place + 3)
+    theirs_2[...], mine_2[...] = theirs_and_mine(place + 4)
+
+
+def hour_sums(plain, first, second, step_hour, field):
     levels, steps, _ = field.shape
+    rows, cut = HOURS * levels, CELLS_DEV // 2
     vmem = pl.BlockSpec(memory_space=pltpu.VMEM)
-    shapes = [(HOURS * levels, CELLS_DEV)] * len(plain_peers)
-    for members in far_peers:
-        shapes += [(len(members) * 2 * levels, CELLS_DEV // 2)] * 2
-    count = len(plain_peers) + sum(map(len, far_peers))
-    outs = pl.pallas_call(
-        functools.partial(sums_kernel, plain_peers, far_peers),
+    shapes = [(rows, CELLS_DEV)] * 2 + [(4 * rows, cut)]
+    shapes += [(len(first) * rows, cut)] * 2 + [(rows, cut)] * 4
+    count = len(first) + 6
+    return pl.pallas_call(
+        functools.partial(sums_kernel, plain, first, second),
         out_shape=[jax.ShapeDtypeStruct(shape, jnp.float32) for shape in shapes],
-        in_specs=[pl.BlockSpec(memory_space=pltpu.SMEM)] + [pl.BlockSpec(memory_space=pl.ANY)] * (1 + len(after)),
+        in_specs=[pl.BlockSpec(memory_space=pltpu.SMEM), pl.BlockSpec(memory_space=pl.ANY)],
         out_specs=[vmem] * len(shapes),
         scratch_shapes=[
             pltpu.VMEM((count, levels, steps, CELLS_DEV), jnp.float32),
@@ -262,17 +279,29 @@
         compiler_params=pltpu.CompilerParams(vmem_limit_bytes=52 * MIB),
         cost_estimate=LIGHT,
         name="hour_sums",
-    )(step_hour, field, *after)
-    far = outs[len(plain_peers) :]
-    return outs[: len(plain_peers)], list(zip(far[::2], far[1::2]))
-
-
-def merge_kernel(parts, mine, got, *refs):
-    outs = refs[-parts:]
-    rows = mine.shape[0] // parts
+    )(step_hour, field)
+
+
+def merge_first_kernel(mine, got, theirs_near, mine_near, pack, theirs_last, mine_last, *refs):
+    *outs, theirs, kept = refs[-4:]
+    rows = theirs_near.shape[0]
     for place, out in enumerate(outs):
         at = slice(place * rows, (place + 1) * rows)
         out[...] = mine[at] + got[at]
+    theirs[:rows], kept[:rows] = theirs_near[...], mine_near[...]
+    theirs[rows : 2 * rows], kept[rows : 2 * rows] = pack[2 * rows : 3 * rows], pack[3 * rows :]
+    theirs[2 * rows :], kept[2 * rows :] = theirs_last[...], mine_last[...]
+
+
+def merge_last_kernel(mine, got, *refs):
+    near, last = refs[-2:]
+    rows = near.shape[0]
+    near[...] = mine[:rows] + got[:rows]
+    last[...] = mine[rows:] + got[rows:]
+
+
+def far_rows_kernel(same_sub, other_sub, out):
+    out[...] = jnp.concatenate(far_rows(same_sub[...], other_sub[...]), axis=0)
 
 
 def small_call(kernel, inputs, after, shapes, cost, name):
@@ -288,40 +317,27 @@
     )(*inputs, *after)
 
 
-def hold_kernel(x, *refs):
-    refs[-1][...] = x[...]
-
-
-def hold(x, *after):
-    return small_call(hold_kernel, [x], after, [x.shape], HEAVY, "hold")[0]
-
-
-def merge(parts, mine, got, *after):
-    shapes = [(mine.shape[0] // parts, mine.shape[1])] * parts
-    return small_call(functools.partial(merge_kernel, parts), [mine, got], after, shapes, HEAVY, "merge")
-
-
-def finish_kernel(divisor, levels, chip, got_chip, near_own, far_own, got, last, got_last, out):
+def finish_kernel(divisor, levels, both, got_both, one, got_one, last, got_last, out):
     me, lev, even = lax.axis_index("tm"), lax.axis_index("lev") % 2, lax.axis_index("sub") == 0
     rows = 2 * levels
     near = keeps_near()
     for hour in range(HOURS):
-        first_at = pl.ds(pl.multiple_of((hour * 2 + 1 - lev) * rows, rows), rows)
-        last_at = pl.ds(pl.multiple_of((hour * 2 + lev) * rows, rows), rows)
-        here = slice(hour * rows, (hour + 1) * rows)
+        one_at = pl.ds(pl.multiple_of((hour * 2 + 1 - lev) * rows, rows), rows)
+        both_at = pl.ds(pl.multiple_of((hour * 2 + lev) * rows, rows), rows)
+        out[one_at, :] = jnp.where(me == hour, one[...], got_one[...]) / divisor
 
         @pl.when(near)
         def _():
-            out[first_at, :] = (near_own[here] + got[here]) / divisor
-            out[last_at, :] = (chip[here] + got_chip[here]) / divisor
+            here = slice(hour * rows, (hour + 1) * rows)
+            out[both_at, :] = (both[here] + got_both[here]) / divisor
 
         @pl.when(jnp.logical_not(near))
         def _():
-            out[first_at, :] = jnp.where(me == hour, far_own[rows:], got[rows:]) / divisor
-            plain = far_own[hour * levels : (hour + 1) * levels] + got[hour * levels : (hour + 1) * levels]
+            here = slice(hour * levels, (hour + 1) * levels)
+            plain = both[here] + got_both[here]
             other = jnp.where(me == hour, last[:levels], got_last[:levels])
             pair = [jnp.where(even, plain, other), jnp.where(even, other, plain)]
-            out[last_at, :] = jnp.concatenate(pair, axis=0) / divisor
+            out[both_at, :] = jnp.concatenate(pair, axis=0) / divisor
 
 
 def finish(arrays, levels, divisor):
@@ -343,45 +359,52 @@
     def swap(x):
         return lax.ppermute(x, "tm", [(0, 1), (1, 0)])
 
-    near_peers = [(1, 0), (1, 1), (0, 1), (0, 0)]
-    plain, first, second = (half, 0), [(half + 1, j) for j in range(subs)], [(half, 1)]
-
-    def send_merged(chunk, mine, got, *after):
-        merged = merge(len(chunk), mine, got, *after)
-        return merged, [to_peer(x, *peer) for x, peer in zip(merged, chunk)]
-
-    (plain_sums,), [(theirs_0, mine_0)] = hour_sums([plain], [first], step_hour, field)
+    plain, first, second = (half, 0), [(half + 1, j) for j in range(subs)], (half, 1)
+    sums = hour_sums(plain, first, second, step_hour, field)
+    plain_sums, own, pack, theirs_0, mine_0, theirs_1, mine_1, theirs_2, mine_2 = sums
+    rows = 2 * field.shape[0]
+    folded = theirs_1.shape
+    pack = to_peer(pack, 0, 1)
+    got_0 = swap(theirs_0)
     plain_got = to_peer(plain_sums, *plain)
-    got_0 = swap(theirs_0)
-    near, [(theirs_1, mine_1)] = hour_sums(near_peers, [second], step_hour, field, theirs_0)
-    near_same, near_other, sibling = [to_peer(x, *peer) for x, peer in zip(near[:3], near_peers)]
-    merged_0, far_0 = send_merged(first, mine_0, got_0, theirs_1)
-    theirs_1 = hold(theirs_1, plain_got, *merged_0)
+    high, low = place_tiles(tile_rows, tile_columns, live_count, tile_weight, theirs_0)
+
+    *merged, theirs_1, mine_1 = small_call(
+        merge_first_kernel,
+        [mine_0, got_0, theirs_1, mine_1, pack, theirs_2, mine_2],
+        [high],
+        [folded] * 2 + [(3 * rows, folded[1])] * 2,
+        HEAVY,
+        "merge_first",
+    )
+    first_got = [to_peer(x, *peer) for x, peer in reversed(list(zip(merged, first)))][::-1]
     got_1 = swap(theirs_1)
-    high, low = place_tiles(tile_rows, tile_columns, live_count, tile_weight, theirs_1, sibling)
-    merged_1, far_1 = send_merged(second, mine_1, got_1, high)
-
-    levels = field.shape[0]
-    rows = 2 * levels
-    (chip,) = remap_call(
-        remap_chip_kernel, [near[3], sibling], merged_1, [2 * rows], high, low, HEAVY, "remap_chip"
-    )
-    got_chip = swap(chip)
-    near_out, far_out, send = remap_call(
-        remap_first_kernel,
-        [near_same, near_other, plain_got, *far_0],
-        [chip],
-        [2 * rows] * 3,
+    both, send = remap_call(
+        remap_both_kernel,
+        [own, pack, plain_got],
+        merged,
+        [2 * rows] * 2,
         high,
         low,
-        HEAVY,
-        "remap_first",
-    )
-    got = swap(send)
-    padded = -(-levels // 16) * 16
-    (last,) = remap_call(remap_last_kernel, far_1, [send], [padded], high, low, HEAVY, "remap_last")
+        MEDIUM,
+        "remap_both",
+        [2 * rows] * 2,
+    )
+    got_both = swap(send)
+    near, last = small_call(
+        merge_last_kernel, [mine_1, got_1], [both], [(2 * rows, folded[1]), folded], HEAVY, "merge_last"
+    )
+    near_got = to_peer(near, 1, 0)
+    second_got = to_peer(last, *second)
+    far = small_call(far_rows_kernel, first_got, [], [(rows, CELLS_DEV)], HEAVY, "far_rows")[0]
+    one, send = remap_call(
+        remap_one_kernel, [near_got, far], [], [rows] * 2, high, low, LIGHT, "remap_one", [rows] * 2
+    )
+    got_one = swap(send)
+    padded = -(-rows // 32) * 16
+    (last,) = remap_call(remap_last_kernel, [second_got], [one], [padded], high, low, HEAVY, "remap_last")
     got_last = swap(last)
-    out = finish([chip, got_chip, near_out, far_out, got, last, got_last], levels, divisor)
+    out = finish([both, got_both, one, got_one, last, got_last], rows // 2, divisor)
     return out.reshape(HOURS, out.shape[0] // HOURS, PIXELS_DEV)
 
 

time: 42.6 us -> 45.3 us (1.063); the launches traced: 42.1 us -> 45.5 us
  waiting for transfers between devices: 7.6 us -> 13.1 us
  Pallas kernels: 17.7 us -> 15.6 us
    ppermute x7 -> x6, waiting for transfers between devices: 2.63 us -> 7.98 us  [to_peer(): return lax.ppermute(x, ('lev', 'sub'), pairs)]
    pallas_call x2 -> x1, Pallas kernels: 5.53 us -> 3.9 us  [hour_sums(): pl.pallas_call(functools.partial(sums_kernel, plain, first, second), out_...]
    pallas_call x1, Pallas kernels: 3.56 us -> 3.04 us  [place_tiles(): pl.pallas_call(place_kernel, out_shape=(half, half), in_specs=[smem, smem...]
    ppermute x7 -> x6, starting transfers between devices: 9.06 us -> 8.62 us  [to_peer(): return lax.ppermute(x, ('lev', 'sub'), pairs)]
  transfers between devices with their start and end apart: 12 -> 11, of which waited for: 4 -> 4; matrix products, arithmetic and copies ran while one was open for 0% -> 0% of each run, Pallas kernels for 34% -> 24%
where the time goes in v6:
time: 45.3 us; the launch traced here: 45.5 us
  Pallas kernels  15.6 us (34%)
  starting transfers between devices  15.4 us (34%)
  waiting for transfers between devices  13.1 us (29%)
  between operations  0.74 us (2%)
  local copies, waits for them, and re-layouts  0.69 us (2%)
    ppermute x6, starting transfers between devices, to_peer(): return lax.ppermute(x, ('lev', 'sub'), pairs)  8.62 us
    ppermute x6, waiting for transfers between devices, to_peer(): return lax.ppermute(x, ('lev', 'sub'), pairs)  7.98 us
    pallas_call x3, Pallas kernels, remap_call(): pl.pallas_call(kernel, out_shape=[jax.ShapeDtypeStruct((rows, PIXELS_DEV)...  7.75 us
    ppermute x5, starting transfers between devices, swap(): return lax.ppermute(x, 'tm', [(0, 1), (1, 0)])  6.75 us
    ppermute x5, waiting for transfers between devices, swap(): return lax.ppermute(x, 'tm', [(0, 1), (1, 0)])  5.08 us
    pallas_call x1, Pallas kernels, hour_sums(): pl.pallas_call(functools.partial(sums_kernel, plain, first, second), out_...  3.9 us
    pallas_call x1, Pallas kernels, place_tiles(): pl.pallas_call(place_kernel, out_shape=(half, half), in_specs=[smem, smem...  3.04 us
    pallas_call x4, Pallas kernels, small_call(): pl.pallas_call(kernel, out_shape=[jax.ShapeDtypeStruct(shape, jnp.float32...  0.94 us
  transfers between devices with their start and end apart: 11, of which 4 were waited for; matrix products, arithmetic and copies ran while one was open for 0% of the time, Pallas kernels for 24%

profile of v6, /device:TPU:0, one launch (start us, length us, event | category | flops | bytes accessed | tf_op | source)
XLA Modules:
  0.0 45.5 jit_solution(5416706763729308030)
XLA Ops:
  0.0 0.7 %copy-done = s32[8]{0:T(128)S(1)} copy-done((s32[8]{0:T(128)S(1)}, s32[8]{0:T(128)}, u32[]{:S(2)}) %copy-start) | copy-done | bytes 56
  0.7 3.9 %hour_sums.1 = (f32[24,2048]{1,0:T(8,128)S(1)}, f32[24,2048]{1,0:T(8,128)S(1)}, f32[96,1024]{1,0:T(8,128)S(1)}, f32[48,1024]{1,0:T(8,128)S(1)}, f32[48,1024]{1,0...) custom-call(s32[8]{0:T(128)S(1)} %copy-done, ...), custom_call_target="tpu_custom_call" | custom-call | flops 1 | bytes 1 | tf_op jit(solution)/shard_map/hour_sums/pallas_call | solution.py:270
  4.6 4.1 %collective-permute-start.1 = (f32[24,2048]{1,0:T(8,128)S(1)}, f32[24,2048]{1,0:T(8,128)S(1)}, u32[]{:S(2)}, u32[]{:S(2)}) collective-permute-start(f32[24,2048]{1,0:T(8,128)S(1)} %get-tuple-element.28), channel_id=1, source_target_pairs={{0,8},{1,9},{4,12},{5,13},{8,0},{9,1},{12,4},{13,5},{2,10},{3,11},... | collective-permute-start | bytes 589832 | tf_op jit(solution)/shard_map/ppermute | solution.py:357
  8.7 1.5 %collective-permute-start.2 = (f32[48,1024]{1,0:T(8,128)S(1)}, f32[48,1024]{1,0:T(8,128)S(1)}, u32[]{:S(2)}, u32[]{:S(2)}) collective-permute-start(f32[48,1024]{1,0:T(8,128)S(1)} %get-tuple-element.29.refs_0_), channel_id=1, source_target_pairs={{0,2},{2,0},{1,3},{3,1},{4,6},{6,4},{5,7},{7,5},{8,10},{10,8},{9,1... | collective-permute-start | bytes 589832 | tf_op jit(solution)/shard_map/ppermute | solution.py:360
  10.2 0.0 collective-permute-start
  10.8 0.0 copy-done.3
  10.9 0.0 copy-done.2
  10.9 3.0 %place_tiles.1 = (bf16[1024,2048]{1,0:T(8,128)(2,1)S(1)}, bf16[1024,2048]{1,0:T(8,128)(2,1)S(1)}) custom-call(s32[128]{0:T(128)S(1)} %copy-done.2, s32[128]{0:T(128)S(1)} %copy-done.3, s32[1]{0:T(128)S(6)} %copy.7.count, f32[64,8192]{1,0:T(8,128)S(1)} %copy-done.1, f32[48,1024]{1,0:T(8,128)S(1)} %get-tuple-element.29.refs_0_), custom_call_target="tpu_custom_call" | custom-call | flops 10000000000 | bytes 1 | tf_op jit(solution)/shard_map/place_tiles/pallas_call | solution.py:78
  13.9 1.1 %collective-permute-done.2.got = f32[48,1024]{1,0:T(8,128)S(1)} collective-permute-done((f32[48,1024]{1,0:T(8,128)S(1)}, f32[48,1024]{1,0:T(8,128)S(1)}, u32[]{:S(2)}, u32[]{:S(2)}) %collective-permute-start.2) | collective-permute-done | bytes 196640 | tf_op jit(solution)/shard_map/ppermute | solution.py:360
  15.1 0.0 collective-permute-done.pack
  15.1 0.1 merge_first.1
  15.1 1.6 %collective-permute-start.4 = (f32[72,1024]{1,0:T(8,128)S(1)}, f32[72,1024]{1,0:T(8,128)S(1)}, u32[]{:S(2)}, u32[]{:S(2)}) collective-permute-start(f32[72,1024]{1,0:T(8,128)S(1)} %get-tuple-element.42), channel_id=1, source_target_pairs={{0,2},{2,0},{1,3},{3,1},{4,6},{6,4},{5,7},{7,5},{8,10},{10,8},{9,1... | collective-permute-start | bytes 884744 | tf_op jit(solution)/shard_map/ppermute | solution.py:360
  16.7 1.4 %collective-permute-start.6 = (f32[24,1024]{1,0:T(8,128)S(1)}, f32[24,1024]{1,0:T(8,128)S(1)}, u32[]{:S(2)}, u32[]{:S(2)}) collective-permute-start(f32[24,1024]{1,0:T(8,128)S(1)} %get-tuple-element.37.refs_0_), channel_id=1, source_target_pairs={{0,12},{1,13},{4,8},{5,9},{8,4},{9,5},{12,0},{13,1},{2,14},{3,15},... | collective-permute-start | bytes 294920 | tf_op jit(solution)/shard_map/ppermute | solution.py:357
  18.1 1.2 %collective-permute-start.7 = (f32[24,1024]{1,0:T(8,128)S(1)}, f32[24,1024]{1,0:T(8,128)S(1)}, u32[]{:S(2)}, u32[]{:S(2)}) collective-permute-start(f32[24,1024]{1,0:T(8,128)S(1)} %get-tuple-element.38.refs_1_), channel_id=1, source_target_pairs={{0,13},{1,12},{4,9},{5,8},{8,5},{9,4},{12,1},{13,0},{2,15},{3,14},... | collective-permute-start | bytes 294920 | tf_op jit(solution)/shard_map/ppermute | solution.py:357
  19.3 0.0 collective-permute-done.1.plain
  19.3 2.7 %remap_both.1 = (f32[48,1024]{1,0:T(8,128)S(1)}, f32[48,1024]{1,0:T(8,128)S(1)}) custom-call(f32[24,2048]{1,0:T(8,128)S(1)} %get-tuple-element.26.own, f32[96,1024]{1,0:T(8,128)S(1)} %collective-permute-done.pack, f32[24,2048]{1,0:T(8,128)S(1)} %collective-permute-done.1.plain, bf16[1024,2048]{1,0:T(8,128)(2,1)S(1)} %get-tuple-element.30.refs_0_.high, ...), custom_call_target="tpu_custom_call" | custom-call | flops 2500000000 | bytes 1 | tf_op jit(solution)/shard_map/remap_both/pallas_call | solution.py:105
  22.0 1.6 %collective-permute-start.3 = (f32[48,1024]{1,0:T(8,128)S(1)}, f32[48,1024]{1,0:T(8,128)S(1)}, u32[]{:S(2)}, u32[]{:S(2)}) collective-permute-start(f32[48,1024]{1,0:T(8,128)S(1)} %get-tuple-element.40), channel_id=1, source_target_pairs={{0,2},{2,0},{1,3},{3,1},{4,6},{6,4},{5,7},{7,5},{8,10},{10,8},{9,1... | collective-permute-start | bytes 589832 | tf_op jit(solution)/shard_map/ppermute | solution.py:360
  23.6 1.2 %collective-permute-done.4.got = f32[72,1024]{1,0:T(8,128)S(1)} collective-permute-done((f32[72,1024]{1,0:T(8,128)S(1)}, f32[72,1024]{1,0:T(8,128)S(1)}, u32[]{:S(2)}, u32[]{:S(2)}) %collective-permute-start.4) | collective-permute-done | bytes 294944 | tf_op jit(solution)/shard_map/ppermute | solution.py:360
  24.8 0.1 collective-permute-start.9
  24.9 1.8 %collective-permute-start.5 = (f32[48,1024]{1,0:T(8,128)S(1)}, f32[48,1024]{1,0:T(8,128)S(1)}, u32[]{:S(2)}, u32[]{:S(2)}) collective-permute-start(f32[48,1024]{1,0:T(8,128)S(1)} %get-tuple-element.43), channel_id=1, source_target_pairs={{0,4},{1,5},{4,0},{5,1},{8,12},{9,13},{12,8},{13,9},{2,6},{3,7},{6... | collective-permute-start | bytes 589832 | tf_op jit(solution)/shard_map/ppermute | solution.py:357
  26.7 0.0 collective-permute-done.6.same_sub
  26.7 0.0 collective-permute-done.7.other_sub
  26.8 8.0 %collective-permute-done.5.near = f32[48,1024]{1,0:T(8,128)S(1)} collective-permute-done((f32[48,1024]{1,0:T(8,128)S(1)}, f32[48,1024]{1,0:T(8,128)S(1)}, u32[]{:S(2)}, u32[]{:S(2)}) %collective-permute-start.5) | collective-permute-done | bytes 196640 | tf_op jit(solution)/shard_map/ppermute | solution.py:357
  34.8 2.7 %remap_one.1 = (f32[24,1024]{1,0:T(8,128)S(1)}, f32[24,1024]{1,0:T(8,128)S(1)}) custom-call(f32[48,1024]{1,0:T(8,128)S(1)} %collective-permute-done.5.near, f32[24,2048]{1,0:T(8,128)S(1)} %far_rows.1.far, bf16[1024,2048]{1,0:T(8,128)(2,1)S(1)} %get-tuple-element.30.refs_0_.high, bf16[1024,2048]{1,0:T(8,128)(2,1)S(1)} %get-tuple-element.31.low), custom_call_target="tpu_custom_call" | custom-call | flops 1 | bytes 1 | tf_op jit(solution)/shard_map/remap_one/pallas_call | solution.py:105
  37.4 0.6 %collective-permute-start.8 = (f32[24,1024]{1,0:T(8,128)S(1)}, f32[24,1024]{1,0:T(8,128)S(1)}, u32[]{:S(2)}, u32[]{:S(2)}) collective-permute-start(f32[24,1024]{1,0:T(8,128)S(1)} %get-tuple-element.45), channel_id=1, source_target_pairs={{0,2},{2,0},{1,3},{3,1},{4,6},{6,4},{5,7},{7,5},{8,10},{10,8},{9,1... | collective-permute-start | bytes 294920 | tf_op jit(solution)/shard_map/ppermute | solution.py:360
  38.0 0.0 collective-permute-done.9.block
  38.0 2.4 %remap_last.1.last = f32[16,1024]{1,0:T(8,128)S(1)} custom-call(f32[24,1024]{1,0:T(8,128)S(1)} %collective-permute-done.9.block, bf16[1024,2048]{1,0:T(8,128)(2,1)S(1)} %get-tuple-element.30.refs_0_.high, bf16[1024,2048]{1,0:T(8,128)(2,1)S(1)} %get-tuple-element.31.low, f32[24,1024]{1,0:T(8,128)S(1)} %get-tuple-element.44.refs_0_.one), custom_call_target="tpu_custom_call" | custom-call | flops 10000000000 | bytes 1 | tf_op jit(solution)/shard_map/remap_last/pallas_call | solution.py:105
  40.4 1.5 %collective-permute-start.10 = (f32[16,1024]{1,0:T(8,128)S(1)}, f32[16,1024]{1,0:T(8,128)S(1)}, u32[]{:S(2)}, u32[]{:S(2)}) collective-permute-start(f32[16,1024]{1,0:T(8,128)S(1)} %remap_last.1.last), channel_id=1, source_target_pairs={{0,2},{2,0},{1,3},{3,1},{4,6},{6,4},{5,7},{7,5},{8,10},{10,8},{9,1... | collective-permute-start | bytes 196616 | tf_op jit(solution)/shard_map/ppermute | solution.py:360
  41.9 0.0 collective-permute-done.3.got_both
  41.9 2.8 %collective-permute-done.10.got_last = f32[16,1024]{1,0:T(8,128)S(1)} collective-permute-done((f32[16,1024]{1,0:T(8,128)S(1)}, f32[16,1024]{1,0:T(8,128)S(1)}, u32[]{:S(2)}, u32[]{:S(2)}) %collective-permute-start.10) | collective-permute-done | bytes 65568 | tf_op jit(solution)/shard_map/ppermute | solution.py:360
  44.7 0.0 collective-permute-done.8.got_one
  44.7 0.8 %finish.1 = f32[96,1024]{1,0:T(8,128)} custom-call(f32[48,1024]{1,0:T(8,128)S(1)} %get-tuple-element.39.refs_0_.both, f32[48,1024]{1,0:T(8,128)S(1)} %collective-permute-done.3.got_both, f32[24,1024]{1,0:T(8,128)S(1)} %get-tuple-element.44.refs_0_.one, f32[24,1024]{1,0:T(8,128)S(1)} %collective-permute-done.8.got_one, f32[16,1024]{1,0:T(8,128)S(1)} %remap_last.1.last, ...), custom_call_target="tpu_custom_call" | custom-call | flops 1 | bytes 1 | tf_op jit(solution)/shard_map/finish/pallas_call | solution.py:309
  (7 shorter events, 0.1 us)
Async XLA Ops:
  0.0 10.8 %copy-start.3 = (s32[128]{0:T(128)S(1)}, s32[128]{0:T(128)}, u32[]{:S(2)}) copy-start(s32[128]{0:T(128)} %columns.1) | copy-start | bytes 1540
  0.0 10.9 %copy-start.2 = (s32[128]{0:T(128)S(1)}, s32[128]{0:T(128)}, u32[]{:S(2)}) copy-start(s32[128]{0:T(128)} %rows.1) | copy-start | bytes 1540
  0.0 0.7 %copy-start = (s32[8]{0:T(128)S(1)}, s32[8]{0:T(128)}, u32[]{:S(2)}) copy-start(s32[8]{0:T(128)} %step_hour.1) | copy-start | bytes 100
  0.7 10.2 %copy-start.1 = (f32[64,8192]{1,0:T(8,128)S(1)}, f32[64,8192]{1,0:T(8,128)}, u32[]{:S(2)}) copy-start(f32[64,8192]{1,0:T(8,128)} %weights.1) | copy-start | bytes 6291460
  4.6 14.7 %collective-permute-start.1 = (f32[24,2048]{1,0:T(8,128)S(1)}, f32[24,2048]{1,0:T(8,128)S(1)}, u32[]{:S(2)}, u32[]{:S(2)}) collective-permute-start(f32[24,2048]{1,0:T(8,128)S(1)} %get-tuple-element.28), channel_id=1, source_target_pairs={{0,8},{1,9},{4,12},{5,13},{8,0},{9,1},{12,4},{13,5},{2,10},{3,11},... | collective-permute-start | bytes 589832 | tf_op jit(solution)/shard_map/ppermute | solution.py:357
  8.7 6.4 %collective-permute-start.2 = (f32[48,1024]{1,0:T(8,128)S(1)}, f32[48,1024]{1,0:T(8,128)S(1)}, u32[]{:S(2)}, u32[]{:S(2)}) collective-permute-start(f32[48,1024]{1,0:T(8,128)S(1)} %get-tuple-element.29.refs_0_), channel_id=1, source_target_pairs={{0,2},{2,0},{1,3},{3,1},{4,6},{6,4},{5,7},{7,5},{8,10},{10,8},{9,1... | collective-permute-start | bytes 589832 | tf_op jit(solution)/shard_map/ppermute | solution.py:360
  10.2 4.9 %collective-permute-start = (f32[96,1024]{1,0:T(8,128)S(1)}, f32[96,1024]{1,0:T(8,128)S(1)}, u32[]{:S(2)}, u32[]{:S(2)}) collective-permute-start(f32[96,1024]{1,0:T(8,128)S(1)} %get-tuple-element.27), channel_id=1, source_target_pairs={{0,1},{1,0},{4,5},{5,4},{8,9},{9,8},{12,13},{13,12},{2,3},{3,2},{6... | collective-permute-start | bytes 1179656 | tf_op jit(solution)/shard_map/ppermute | solution.py:357
  15.1 9.7 %collective-permute-start.4 = (f32[72,1024]{1,0:T(8,128)S(1)}, f32[72,1024]{1,0:T(8,128)S(1)}, u32[]{:S(2)}, u32[]{:S(2)}) collective-permute-start(f32[72,1024]{1,0:T(8,128)S(1)} %get-tuple-element.42), channel_id=1, source_target_pairs={{0,2},{2,0},{1,3},{3,1},{4,6},{6,4},{5,7},{7,5},{8,10},{10,8},{9,1... | collective-permute-start | bytes 884744 | tf_op jit(solution)/shard_map/ppermute | solution.py:360
  16.7 10.1 %collective-permute-start.6 = (f32[24,1024]{1,0:T(8,128)S(1)}, f32[24,1024]{1,0:T(8,128)S(1)}, u32[]{:S(2)}, u32[]{:S(2)}) collective-permute-start(f32[24,1024]{1,0:T(8,128)S(1)} %get-tuple-element.37.refs_0_), channel_id=1, source_target_pairs={{0,12},{1,13},{4,8},{5,9},{8,4},{9,5},{12,0},{13,1},{2,14},{3,15},... | collective-permute-start | bytes 294920 | tf_op jit(solution)/shard_map/ppermute | solution.py:357
  18.1 8.7 %collective-permute-start.7 = (f32[24,1024]{1,0:T(8,128)S(1)}, f32[24,1024]{1,0:T(8,128)S(1)}, u32[]{:S(2)}, u32[]{:S(2)}) collective-permute-start(f32[24,1024]{1,0:T(8,128)S(1)} %get-tuple-element.38.refs_1_), channel_id=1, source_target_pairs={{0,13},{1,12},{4,9},{5,8},{8,5},{9,4},{12,1},{13,0},{2,15},{3,14},... | collective-permute-start | bytes 294920 | tf_op jit(solution)/shard_map/ppermute | solution.py:357
  22.0 19.9 %collective-permute-start.3 = (f32[48,1024]{1,0:T(8,128)S(1)}, f32[48,1024]{1,0:T(8,128)S(1)}, u32[]{:S(2)}, u32[]{:S(2)}) collective-permute-start(f32[48,1024]{1,0:T(8,128)S(1)} %get-tuple-element.40), channel_id=1, source_target_pairs={{0,2},{2,0},{1,3},{3,1},{4,6},{6,4},{5,7},{7,5},{8,10},{10,8},{9,1... | collective-permute-start | bytes 589832 | tf_op jit(solution)/shard_map/ppermute | solution.py:360
  24.8 13.2 %collective-permute-start.9 = (f32[24,1024]{1,0:T(8,128)S(1)}, f32[24,1024]{1,0:T(8,128)S(1)}, u32[]{:S(2)}, u32[]{:S(2)}) collective-permute-start(f32[24,1024]{1,0:T(8,128)S(1)} %get-tuple-element.46), channel_id=1, source_target_pairs={{0,9},{1,8},{4,13},{5,12},{8,1},{9,0},{12,5},{13,4},{2,11},{3,10},... | collective-permute-start | bytes 294920 | tf_op jit(solution)/shard_map/ppermute | solution.py:357
  24.9 9.9 %collective-permute-start.5 = (f32[48,1024]{1,0:T(8,128)S(1)}, f32[48,1024]{1,0:T(8,128)S(1)}, u32[]{:S(2)}, u32[]{:S(2)}) collective-permute-start(f32[48,1024]{1,0:T(8,128)S(1)} %get-tuple-element.43), channel_id=1, source_target_pairs={{0,4},{1,5},{4,0},{5,1},{8,12},{9,13},{12,8},{13,9},{2,6},{3,7},{6... | collective-permute-start | bytes 589832 | tf_op jit(solution)/shard_map/ppermute | solution.py:357
  37.4 7.3 %collective-permute-start.8 = (f32[24,1024]{1,0:T(8,128)S(1)}, f32[24,1024]{1,0:T(8,128)S(1)}, u32[]{:S(2)}, u32[]{:S(2)}) collective-permute-start(f32[24,1024]{1,0:T(8,128)S(1)} %get-tuple-element.45), channel_id=1, source_target_pairs={{0,2},{2,0},{1,3},{3,1},{4,6},{6,4},{5,7},{7,5},{8,10},{10,8},{9,1... | collective-permute-start | bytes 294920 | tf_op jit(solution)/shard_map/ppermute | solution.py:360
  40.4 4.3 %collective-permute-start.10 = (f32[16,1024]{1,0:T(8,128)S(1)}, f32[16,1024]{1,0:T(8,128)S(1)}, u32[]{:S(2)}, u32[]{:S(2)}) collective-permute-start(f32[16,1024]{1,0:T(8,128)S(1)} %remap_last.1.last), channel_id=1, source_target_pairs={{0,2},{2,0},{1,3},{3,1},{4,6},{6,4},{5,7},{7,5},{8,10},{10,8},{9,1... | collective-permute-start | bytes 196616 | tf_op jit(solution)/shard_map/ppermute | solution.py:360
